TPU v7x, 32 devices: a whole 2x2x4 slice. The times are simulated.
32 devices in a mesh: shard: 4 (over z), ctx: 4 (over y, x), tp: 2 (over core).
Axes of the slice: x: 2, y: 2, z: 4, core: 2. Of those that a mesh axis runs over, the one named last changes fastest.
Arguments:
- images: bfloat16 [4, 1024, 768], P('shard', 'ctx'), may hold values from -6 to 6
- cotangent: bfloat16 [4, 1024, 768], P('shard', 'ctx'), may hold values from -6 to 6
- ln1_gain: bfloat16 [768], P('shard'), may hold values from 0.5 to 1.5
- ln1_bias: bfloat16 [768], P('shard'), may hold values from -1.75 to 1.75
- ln2_gain: bfloat16 [768], P('shard'), may hold values from 0.5 to 1.5
- ln2_bias: bfloat16 [768], P('shard'), may hold values from -1.75 to 1.75
- q_gain: bfloat16 [12, 64], P('tp', 'shard'), may hold values from 0.7 to 2.2
- k_gain: bfloat16 [12, 64], P('tp', 'shard'), may hold values from 0.7 to 2.2
- w_query: bfloat16 [768, 768], P('shard', 'tp'), may hold values from -6 to 6
- w_key: bfloat16 [768, 768], P('shard', 'tp'), may hold values from -6 to 6
- w_value: bfloat16 [768, 768], P('shard', 'tp'), may hold values from -0.21875 to 0.21875
- w_out: bfloat16 [768, 768], P('tp', 'shard'), may hold values from -1.75 to 1.75
- w_up: bfloat16 [768, 3072], P('shard', 'tp'), may hold values from -0.21875 to 0.21875
- w_down: bfloat16 [3072, 768], P('tp', 'shard'), may hold values from -0.109375 to 0.109375
Outputs:
- block_out: bfloat16 [4, 1024, 768], P('shard', 'ctx')
- input_grad: bfloat16 [4, 1024, 768], P('shard', 'ctx')
- ln1_gain_grad: float32 [768], P('shard')
- ln1_bias_grad: float32 [768], P('shard')
- ln2_gain_grad: float32 [768], P('shard')
- ln2_bias_grad: float32 [768], P('shard')
- q_gain_grad: float32 [12, 64], P('tp', 'shard')
- k_gain_grad: float32 [12, 64], P('tp', 'shard')
- w_query_grad: float32 [768, 768], P('shard', 'tp')
- w_key_grad: float32 [768, 768], P('shard', 'tp')
- w_value_grad: float32 [768, 768], P('shard', 'tp')
- w_out_grad: float32 [768, 768], P('tp', 'shard')
- w_up_grad: float32 [768, 3072], P('shard', 'tp')
- w_down_grad: float32 [3072, 768], P('tp', 'shard')
- w_query_clipped: bfloat16 [768, 768], P('shard', 'tp')
- w_key_clipped: bfloat16 [768, 768], P('shard', 'tp')
All inputs are finite; a program needn't handle non-finite values.
Results may differ from a plain program's by a relative error of at most 0.013.
The roundings to bfloat16 on the way count: a program that leaves them out, or rounds other values in their place, can miss the bound.
Values may be sent and summed in bfloat16 or wider, within the bound.
A program may use at most 128 MiB of HBM per device.

v0:
```python
import jax
import jax.numpy as jnp
from jax import lax
from jax.sharding import PartitionSpec as P

norm_eps = 1e-06
clip_level = 0.5


def matmul(left, right):
    return jnp.dot(left, right, preferred_element_type=jnp.float32)


def norm_parts(values):
    center = values - jnp.mean(values, axis=-1, keepdims=True)
    inverse = lax.rsqrt(jnp.mean(center * center, axis=-1, keepdims=True) + norm_eps)
    return (center * inverse, inverse)


def norm_back(grad_hat, normed, inverse):
    return inverse * (
        grad_hat
        - jnp.mean(grad_hat, axis=-1, keepdims=True)
        - normed * jnp.mean(grad_hat * normed, axis=-1, keepdims=True)
    )


def head_scale(values, gain):
    inverse = lax.rsqrt(jnp.mean(values * values, axis=-1, keepdims=True) + norm_eps)
    return values * inverse * gain


def gelu_exact(values):
    return jax.nn.gelu(values, approximate=False)


def on_device(
    images,
    cotangent,
    ln1_gain,
    ln1_bias,
    ln2_gain,
    ln2_bias,
    q_gain,
    k_gain,
    w_query,
    w_key,
    w_value,
    w_out,
    w_up,
    w_down,
):
    (
        full_query,
        full_key,
        full_value,
        full_up,
        full_out,
        full_down,
        gain_low_one,
        shift_low_one,
        gain_low_two,
        shift_low_two,
        query_gain_low,
        key_gain_low,
    ) = (
        lax.all_gather(w_query, "shard", axis=0, tiled=True),
        lax.all_gather(w_key, "shard", axis=0, tiled=True),
        lax.all_gather(w_value, "shard", axis=0, tiled=True),
        lax.all_gather(w_up, "shard", axis=0, tiled=True),
        lax.all_gather(w_out, "shard", axis=1, tiled=True),
        lax.all_gather(w_down, "shard", axis=1, tiled=True),
        lax.all_gather(ln1_gain, "shard", axis=0, tiled=True),
        lax.all_gather(ln1_bias, "shard", axis=0, tiled=True),
        lax.all_gather(ln2_gain, "shard", axis=0, tiled=True),
        lax.all_gather(ln2_bias, "shard", axis=0, tiled=True),
        lax.all_gather(q_gain, "shard", axis=1, tiled=True),
        lax.all_gather(k_gain, "shard", axis=1, tiled=True),
    )
    gain_one = gain_low_one.astype(jnp.float32)
    shift_one = shift_low_one.astype(jnp.float32)
    gain_two = gain_low_two.astype(jnp.float32)
    shift_two = shift_low_two.astype(jnp.float32)
    query_gain = query_gain_low.astype(jnp.float32)
    key_gain = key_gain_low.astype(jnp.float32)
    count_img, local_len, width = images.shape
    tokens = count_img * local_len
    heads_here, head_size = query_gain.shape
    local_width = heads_here * head_size
    full_len = local_len * lax.axis_size("ctx")
    group = 1
    groups = count_img // group
    scale = head_size ** (-0.5)
    flat = images.reshape(tokens, width).astype(jnp.float32)
    normed_one, inverse_one = norm_parts(flat)
    hidden_one = (normed_one * gain_one + shift_one).astype(jnp.bfloat16)
    query_raw = matmul(hidden_one, full_query).reshape(tokens, heads_here, head_size)
    key_raw = matmul(hidden_one, full_key).reshape(tokens, heads_here, head_size)
    query_norm = head_scale(query_raw, query_gain).astype(jnp.bfloat16)
    key_norm = head_scale(key_raw, key_gain).astype(jnp.bfloat16)
    value_low = matmul(hidden_one, full_value).astype(jnp.bfloat16)
    key_all, value_all = (
        lax.all_gather(
            key_norm.reshape(count_img, local_len, local_width), "ctx", axis=1, tiled=True
        ),
        lax.all_gather(
            value_low.reshape(count_img, local_len, local_width), "ctx", axis=1, tiled=True
        ),
    )
    query_grp = query_norm.reshape(groups, group, local_len, heads_here, head_size)
    key_grp = key_all.reshape(groups, group, full_len, heads_here, head_size)
    value_grp = value_all.reshape(groups, group, full_len, heads_here, head_size)

    def attend(pieces):
        query_blk, key_blk, value_blk = pieces
        scores = (
            jnp.einsum("gqhd,gkhd->ghqk", query_blk, key_blk, preferred_element_type=jnp.float32)
            * scale
        )
        top = jnp.max(scores, axis=-1, keepdims=True)
        expo = jnp.exp(scores - top)
        total = jnp.sum(expo, axis=-1, keepdims=True)
        probs = (expo / total).astype(jnp.bfloat16)
        mixed_blk = jnp.einsum(
            "ghqk,gkhd->gqhd", probs, value_blk, preferred_element_type=jnp.float32
        )
        return (mixed_blk, top + jnp.log(total), jnp.max(top, axis=(0, 2, 3)))

    mixed, log_total, group_peaks = lax.map(attend, (query_grp, key_grp, value_grp))
    local_peak = jnp.max(group_peaks, axis=0)
    peak_all = lax.pmax(local_peak, ("shard", "ctx"))
    attended = mixed.reshape(tokens, local_width).astype(jnp.bfloat16)
    branch_attn = lax.psum(matmul(attended, full_out), "tp")
    resid = flat + branch_attn
    normed_two, inverse_two = norm_parts(resid)
    hidden_two = (normed_two * gain_two + shift_two).astype(jnp.bfloat16)
    up_raw = matmul(hidden_two, full_up)
    active = gelu_exact(up_raw).astype(jnp.bfloat16)
    branch_mlp = lax.psum(matmul(active, full_down).astype(jnp.bfloat16), "tp").astype(jnp.float32)
    block_out = (resid + branch_mlp).astype(jnp.bfloat16).reshape(images.shape)
    grad_out = cotangent.reshape(tokens, width).astype(jnp.float32)
    grad_down = cotangent.reshape(tokens, width)
    grad_w_down = jnp.dot(active.T, grad_down, preferred_element_type=jnp.float32)
    grad_active = matmul(grad_down, full_down.T)
    unused_up, gelu_pull = jax.vjp(gelu_exact, up_raw)
    grad_up = gelu_pull(grad_active)[0].astype(jnp.bfloat16)
    grad_w_up = jnp.dot(hidden_two.T, grad_up, preferred_element_type=jnp.float32)
    grad_two = lax.psum(matmul(grad_up, full_up.T), "tp")
    grad_gain_two = jnp.sum(grad_two * normed_two, axis=0)
    grad_shift_two = jnp.sum(grad_two, axis=0)
    grad_resid = grad_out + norm_back(grad_two * gain_two, normed_two, inverse_two)
    grad_branch = grad_resid.astype(jnp.bfloat16)
    grad_w_out = jnp.dot(attended.T, grad_branch, preferred_element_type=jnp.float32)
    grad_mixed = matmul(grad_branch, full_out.T).astype(jnp.bfloat16)
    grad_grp = grad_mixed.reshape(groups, group, local_len, heads_here, head_size)

    def attend_back(pieces):
        query_blk, key_blk, value_blk, log_blk, grad_blk = pieces
        scores = (
            jnp.einsum("gqhd,gkhd->ghqk", query_blk, key_blk, preferred_element_type=jnp.float32)
            * scale
        )
        probs = jnp.exp(scores - log_blk)
        grad_probs = jnp.einsum(
            "gqhd,gkhd->ghqk", grad_blk, value_blk, preferred_element_type=jnp.float32
        )
        grad_scores = (
            probs * (grad_probs - jnp.sum(probs * grad_probs, axis=-1, keepdims=True))
        ).astype(jnp.bfloat16)
        grad_val = jnp.einsum(
            "ghqk,gqhd->gkhd",
            probs.astype(jnp.bfloat16),
            grad_blk,
            preferred_element_type=jnp.float32,
        )
        grad_qry = (
            jnp.einsum("ghqk,gkhd->gqhd", grad_scores, key_blk, preferred_element_type=jnp.float32)
            * scale
        )
        grad_kys = (
            jnp.einsum(
                "ghqk,gqhd->gkhd", grad_scores, query_blk, preferred_element_type=jnp.float32
            )
            * scale
        )
        return (grad_qry, grad_kys, grad_val)

    grad_query_n, grad_key_full, grad_value_full = lax.map(
        attend_back, (query_grp, key_grp, value_grp, log_total, grad_grp)
    )
    grad_key_n, grad_value_n = (
        lax.psum_scatter(
            grad_key_full.reshape(count_img, full_len, local_width),
            "ctx",
            scatter_dimension=1,
            tiled=True,
        ),
        lax.psum_scatter(
            grad_value_full.reshape(count_img, full_len, local_width),
            "ctx",
            scatter_dimension=1,
            tiled=True,
        ),
    )
    unused_query, query_pull = jax.vjp(head_scale, query_raw, query_gain)
    grad_query_raw, grad_query_gain = query_pull(
        grad_query_n.reshape(tokens, heads_here, head_size)
    )
    unused_key, key_pull = jax.vjp(head_scale, key_raw, key_gain)
    grad_key_raw, grad_key_gain = key_pull(grad_key_n.reshape(tokens, heads_here, head_size))
    grad_query_low = grad_query_raw.reshape(tokens, local_width).astype(jnp.bfloat16)
    grad_key_low = grad_key_raw.reshape(tokens, local_width).astype(jnp.bfloat16)
    grad_value_low = grad_value_n.reshape(tokens, local_width).astype(jnp.bfloat16)
    grad_w_query = jnp.dot(hidden_one.T, grad_query_low, preferred_element_type=jnp.float32)
    grad_w_key = jnp.dot(hidden_one.T, grad_key_low, preferred_element_type=jnp.float32)
    grad_w_value = jnp.dot(hidden_one.T, grad_value_low, preferred_element_type=jnp.float32)
    grad_one_part = (
        matmul(grad_query_low, full_query.T)
        + matmul(grad_key_low, full_key.T)
        + matmul(grad_value_low, full_value.T)
    )
    grad_one = lax.psum(grad_one_part, "tp")
    grad_gain_one = jnp.sum(grad_one * normed_one, axis=0)
    grad_shift_one = jnp.sum(grad_one, axis=0)
    input_grad = (
        (grad_resid + norm_back(grad_one * gain_one, normed_one, inverse_one))
        .astype(jnp.bfloat16)
        .reshape(images.shape)
    )
    (
        sum_query,
        sum_key,
        sum_value,
        sum_up,
        sum_out,
        sum_down,
        sum_gain_one,
        sum_shift_one,
        sum_gain_two,
        sum_shift_two,
        sum_qgain,
        sum_kgain,
    ) = lax.psum(
        (
            grad_w_query,
            grad_w_key,
            grad_w_value,
            grad_w_up,
            grad_w_out,
            grad_w_down,
            grad_gain_one,
            grad_shift_one,
            grad_gain_two,
            grad_shift_two,
            grad_query_gain,
            grad_key_gain,
        ),
        "ctx",
    )
    (
        part_query,
        part_key,
        part_value,
        part_up,
        part_out,
        part_down,
        part_gain_one,
        part_shift_one,
        part_gain_two,
        part_shift_two,
        part_qgain,
        part_kgain,
    ) = (
        lax.psum_scatter(sum_query, "shard", scatter_dimension=0, tiled=True),
        lax.psum_scatter(sum_key, "shard", scatter_dimension=0, tiled=True),
        lax.psum_scatter(sum_value, "shard", scatter_dimension=0, tiled=True),
        lax.psum_scatter(sum_up, "shard", scatter_dimension=0, tiled=True),
        lax.psum_scatter(sum_out, "shard", scatter_dimension=1, tiled=True),
        lax.psum_scatter(sum_down, "shard", scatter_dimension=1, tiled=True),
        lax.psum_scatter(sum_gain_one, "shard", scatter_dimension=0, tiled=True),
        lax.psum_scatter(sum_shift_one, "shard", scatter_dimension=0, tiled=True),
        lax.psum_scatter(sum_gain_two, "shard", scatter_dimension=0, tiled=True),
        lax.psum_scatter(sum_shift_two, "shard", scatter_dimension=0, tiled=True),
        lax.psum_scatter(sum_qgain, "shard", scatter_dimension=1, tiled=True),
        lax.psum_scatter(sum_kgain, "shard", scatter_dimension=1, tiled=True),
    )
    factor = jnp.sqrt(clip_level / jnp.maximum(peak_all, clip_level))
    columns = jnp.repeat(factor, head_size)
    query_clip = (w_query.astype(jnp.float32) * columns).astype(jnp.bfloat16)
    key_clip = (w_key.astype(jnp.float32) * columns).astype(jnp.bfloat16)
    return (
        block_out,
        input_grad,
        part_gain_one,
        part_shift_one,
        part_gain_two,
        part_shift_two,
        part_qgain,
        part_kgain,
        part_query,
        part_key,
        part_value,
        part_out,
        part_up,
        part_down,
        query_clip,
        key_clip,
    )


def solution(mesh):
    return jax.shard_map(
        on_device,
        mesh=mesh,
        in_specs=(
            P("shard", "ctx", None),
            P("shard", "ctx", None),
            P("shard"),
            P("shard"),
            P("shard"),
            P("shard"),
            P("tp", "shard"),
            P("tp", "shard"),
            P("shard", "tp"),
            P("shard", "tp"),
            P("shard", "tp"),
            P("tp", "shard"),
            P("shard", "tp"),
            P("tp", "shard"),
        ),
        out_specs=(
            P("shard", "ctx", None),
            P("shard", "ctx", None),
            P("shard"),
            P("shard"),
            P("shard"),
            P("shard"),
            P("tp", "shard"),
            P("tp", "shard"),
            P("shard", "tp"),
            P("shard", "tp"),
            P("shard", "tp"),
            P("tp", "shard"),
            P("shard", "tp"),
            P("tp", "shard"),
            P("shard", "tp"),
            P("shard", "tp"),
        ),
        check_vma=False,
    )
```

profile of v0, /device:TPU:0, one launch (start us, length us, event | category | flops | bytes accessed | tf_op | source)
XLA Modules:
  0.0 854.7 jit_solution(9043356622077850387)
XLA Ops:
  8.1 18.5 %all_gather.44 = bf16[768,384]{1,0:T(8,128)(2,1)S(1)} all-gather(bf16[192,384]{1,0:T(8,128)(2,1)} %param.24), channel_id=1, replica_groups=mesh['shard'=4,'ctx'=4,'tp'=2] {'shard'}, dimensions={0}, use_global_device_ids=true | all-gather | bytes 737280 | tf_op jit(solution)/shard_map/all_gather | solution.py:69
  26.6 1.3 fusion.83
  31.9 12.8 %all-reduce.11 = (bf16[768]{0:T(1024)(128)(2,1)S(1)}, bf16[768]{0:T(1024)(128)(2,1)S(1)}, bf16[768]{0:T(1024)(128)(2,1)}, bf16[768]{0:T(1024)(128)(2,1)}) all-reduce(bf16[768]{0:T(1024)(128)(2,1)S(1)} %dynamic-update-slice.1, bf16[768]{0:T(1024)(128)(2,1)S(1)} %dynamic-update-slice, ...), channel_id=1, replica_groups=mesh['shard'=4,'ctx'=4,'tp'=2] {'shard'}, use_global_device_ids=true, to_apply=%add.1 | all-reduce | flops 3072 | bytes 12288
  44.7 1.1 convert_reduce_fusion
  45.9 1.2 fusion.31
  47.6 11.2 %all-gather = bf16[1024,384]{1,0:T(8,128)(2,1)S(1)} all-gather(bf16[256,384]{1,0:T(8,128)(2,1)S(1)} %convolution_convert_fusion.2), channel_id=2, replica_groups=mesh['shard'=4,'ctx'=4,'tp'=2] {'ctx'}, dimensions={0}, use_global_device_ids=true | all-gather | bytes 983040 | tf_op jit(solution)/shard_map/all_gather | solution.py:106
  59.2 15.0 %all_gather.48 = bf16[768,384]{1,0:T(8,128)(2,1)S(1)} all-gather(bf16[192,384]{1,0:T(8,128)(2,1)S(1)} %copy-done.29), channel_id=1, replica_groups=mesh['shard'=4,'ctx'=4,'tp'=2] {'shard'}, dimensions={0}, use_global_device_ids=true | all-gather | bytes 737280 | tf_op jit(solution)/shard_map/all_gather | solution.py:68
  75.0 11.9 %all-gather.2 = bf16[4,16,6]{1,2,0:T(8,128)(2,1)S(1)} all-gather(bf16[1,16,6]{1,2,0:T(8,128)(2,1)S(1)} %bitcast.187), channel_id=1, replica_groups=mesh['shard'=4,'ctx'=4,'tp'=2] {'shard'}, dimensions={0}, use_global_device_ids=true | all-gather | bytes 960 | tf_op jit(solution)/shard_map/all_gather | solution.py:78
  87.2 14.2 %all_gather.50 = bf16[1,1024,384]{1,2,0:T(8,128)(2,1)S(1)} all-gather(bf16[1,256,384]{1,2,0:T(8,128)(2,1)S(1)} %bitcast.173), channel_id=1, replica_groups=mesh['shard'=4,'ctx'=4,'tp'=2] {'ctx'}, dimensions={1}, use_global_device_ids=true | all-gather | bytes 983040 | tf_op jit(solution)/shard_map/all_gather | solution.py:103
  101.4 16.0 %all_gather.46 = bf16[768,384]{1,0:T(8,128)(2,1)S(1)} all-gather(bf16[192,384]{1,0:T(8,128)(2,1)S(1)} %copy-done.31), channel_id=1, replica_groups=mesh['shard'=4,'ctx'=4,'tp'=2] {'shard'}, dimensions={0}, use_global_device_ids=true | all-gather | bytes 737280 | tf_op jit(solution)/shard_map/all_gather | solution.py:67
  118.3 1.2 multiply_reduce_fusion.13
  119.5 11.9 %all-gather.1 = bf16[4,16,6]{1,2,0:T(8,128)(2,1)S(1)} all-gather(bf16[1,16,6]{1,2,0:T(8,128)(2,1)S(1)} %bitcast.188), channel_id=1, replica_groups=mesh['shard'=4,'ctx'=4,'tp'=2] {'shard'}, dimensions={0}, use_global_device_ids=true | all-gather | bytes 960 | tf_op jit(solution)/shard_map/all_gather | solution.py:77
  131.5 15.2 %all_gather.51 = bf16[384,768]{0,1:T(8,128)(2,1)S(1)} all-gather(bf16[384,192]{0,1:T(8,128)(2,1)} %param.25), channel_id=1, replica_groups=mesh['shard'=4,'ctx'=4,'tp'=2] {'shard'}, dimensions={1}, use_global_device_ids=true | all-gather | bytes 737280 | tf_op jit(solution)/shard_map/all_gather | solution.py:71
  146.7 1.2 multiply_reduce_fusion.2
  147.9 2.7 multiply_reduce_fusion.1
  150.6 1.7 fusion.14
  153.0 1.3 fusion.84
  155.6 15.5 %all-reduce.18.cloned.1.call-done = f32[256,768]{1,0:T(8,128)} async-done(((f32[256,768]{1,0:T(8,128)}), f32[256,768]{1,0:T(8,128)}) %all-reduce.18.cloned.1.call-update) | async-done | bytes 786448 | tf_op jit(solution)/shard_map/psum | solution.py:133
  171.1 1.3 fusion.81
  172.7 31.2 %all-gather.6.cloned.1.call-done = bf16[768,1536]{1,0:T(8,128)(2,1)} async-done(((bf16[192,1536]{1,0:T(8,128)(2,1)}), bf16[768,1536]{1,0:T(8,128)(2,1)}) %all-gather.6.cloned.1.call-update) | async-done | bytes 2359312 | tf_op jit(solution)/shard_map/all_gather | solution.py:70
  203.8 6.8 multiply_convert_fusion.1
  210.6 43.5 %all-gather.8.cloned.1.call-done = bf16[1536,768]{0,1:T(8,128)(2,1)} async-done(((bf16[1536,192]{0,1:T(8,128)(2,1)}), bf16[1536,768]{0,1:T(8,128)(2,1)}) %all-gather.8.cloned.1.call-update) | async-done | bytes 2359312 | tf_op jit(solution)/shard_map/all_gather | solution.py:72
  254.1 3.9 add_convert_fusion
  258.9 1.7 fusion.85
  260.9 3.2 convolution_convert_fusion
  264.1 14.5 %all-reduce.22.cloned.1.call-done = f32[256,768]{1,0:T(8,128)} async-done(((f32[256,768]{1,0:T(8,128)}), f32[256,768]{1,0:T(8,128)}) %all-reduce.22.cloned.1.call-update) | async-done | bytes 786448 | tf_op jit(solution)/shard_map/psum | solution.py:148
  278.6 2.1 multiply_reduce_fusion.3
  280.7 20.5 %all-reduce.20.cloned.1.call-done = bf16[256,768]{1,0:T(8,128)(2,1)} async-done(((bf16[256,768]{1,0:T(8,128)(2,1)}), bf16[256,768]{1,0:T(8,128)(2,1)}) %all-reduce.20.cloned.1.call-update) | async-done | bytes 393232 | tf_op jit(solution)/shard_map/psum | solution.py:139
  301.2 2.4 multiply_add_fusion
  304.2 4.4 multiply_reduce_fusion
  308.9 2.3 multiply_convert_fusion
  311.3 2.0 convolution_multiply_fusion
  313.3 5.2 fusion.2
  318.7 3.1 multiply_reduce_fusion.9
  322.0 1.6 fusion.51
  323.7 1.5 fusion.63
  325.2 20.3 %reduce-scatter.15.cloned.1.call-done = f32[1,256,384]{1,2,0:T(8,128)} async-done(((f32[1,1024,384]{1,2,0:T(8,128)}), f32[1,256,384]{1,2,0:T(8,128)}) %reduce-scatter.15.cloned.1.call-update) | async-done | bytes 393232 | tf_op jit(solution)/shard_map/reduce_scatter | solution.py:192
  345.5 1.8 multiply_reduce_fusion.8
  347.4 1.1 fusion.37
  348.5 1.6 fusion.55
  350.2 29.4 %reduce-scatter.17.cloned.1.call-done = f32[1,256,384]{1,2,0:T(8,128)} async-done(((f32[1,1024,384]{1,2,0:T(8,128)}), f32[1,256,384]{1,2,0:T(8,128)}) %reduce-scatter.17.cloned.1.call-update) | async-done | bytes 393232 | tf_op jit(solution)/shard_map/reduce_scatter | solution.py:198
  379.6 2.6 fusion.53
  382.3 3.1 fusion.73
  385.5 1.1 copy-done.20
  386.6 3.0 fusion.41
  391.6 1.3 convolution_add_fusion.1
  393.7 2.6 convolution_add_fusion
  396.3 15.3 %reduce-scatter.19.cloned.1.call-done = f32[192,384]{1,0:T(8,128)} async-done(((f32[768,384]{1,0:T(8,128)}), f32[192,384]{1,0:T(8,128)}) %reduce-scatter.19.cloned.1.call-update) | async-done | bytes 294928 | tf_op jit(solution)/shard_map/reduce_scatter | solution.py:274
  411.6 30.3 %reduce-scatter.25.cloned.1.call-done = f32[384,192]{0,1:T(8,128)} async-done(((f32[384,768]{0,1:T(8,128)}), f32[384,192]{0,1:T(8,128)}) %reduce-scatter.25.cloned.1.call-update) | async-done | bytes 294928 | tf_op jit(solution)/shard_map/reduce_scatter | solution.py:278
  442.0 30.9 %reduce-scatter.21.cloned.1.call-done = f32[192,384]{1,0:T(8,128)} async-done(((f32[768,384]{1,0:T(8,128)}), f32[192,384]{1,0:T(8,128)}) %reduce-scatter.21.cloned.1.call-update) | async-done | bytes 294928 | tf_op jit(solution)/shard_map/reduce_scatter | solution.py:275
  472.9 30.4 %reduce-scatter.23.cloned.1.call-done = f32[192,384]{1,0:T(8,128)} async-done(((f32[768,384]{1,0:T(8,128)}), f32[192,384]{1,0:T(8,128)}) %reduce-scatter.23.cloned.1.call-update) | async-done | bytes 294928 | tf_op jit(solution)/shard_map/reduce_scatter | solution.py:276
  503.3 86.3 %reduce-scatter.27.cloned.1.call-done = f32[192,1536]{1,0:T(8,128)} async-done(((f32[768,1536]{1,0:T(8,128)}), f32[192,1536]{1,0:T(8,128)}) %reduce-scatter.27.cloned.1.call-update) | async-done | bytes 1179664 | tf_op jit(solution)/shard_map/reduce_scatter | solution.py:277
  589.5 88.2 %reduce-scatter.29.cloned.1.call-done = f32[1536,192]{0,1:T(8,128)} async-done(((f32[1536,768]{0,1:T(8,128)}), f32[1536,192]{0,1:T(8,128)}) %reduce-scatter.29.cloned.1.call-update) | async-done | bytes 1179664 | tf_op jit(solution)/shard_map/reduce_scatter | solution.py:279
  678.4 41.2 %pmax.7 = f32[6]{0:T(128)S(1)} all-reduce(f32[6]{0:T(128)S(1)} %copy-done.71), channel_id=1, replica_groups=mesh['shard'=4,'ctx'=4,'tp'=2] {'shard','ctx'}, use_global_device_ids=true, to_apply=%region_52.53 | all-reduce | flops 6 | bytes 48 | tf_op jit(solution)/shard_map/pmax | solution.py:131
  722.7 16.9 %all-reduce.24.cloned.1.call-done = f32[256,768]{1,0:T(8,128)} async-done(((f32[256,768]{1,0:T(8,128)}), f32[256,768]{1,0:T(8,128)}) %all-reduce.24.cloned.1.call-update) | async-done | bytes 786448 | tf_op jit(solution)/shard_map/psum | solution.py:222
  739.6 1.6 fusion.30
  741.3 19.0 %all-reduce.10 = (f32[768]{0:T(1024)S(1)}, f32[768]{0:T(1024)S(1)}, f32[768]{0:T(1024)S(1)}, f32[768]{0:T(1024)S(1)}) all-reduce(f32[768]{0:T(1024)S(1)} %get-tuple-element.68, f32[768]{0:T(1024)S(1)} %get-tuple-element.77, f32[768]{0:T(1024)S(1)} %copy-done.65, ...), channel_id=5, replica_groups=mesh['shard'=4,'ctx'=4,'tp'=2] {'shard'}, use_global_device_ids=true, to_apply=%region_23.24.clone | all-reduce | flops 3072 | bytes 24576
  760.5 16.7 %all-reduce.8 = (f32[192]{0:T(256)}, f32[192]{0:T(256)}, f32[192]{0:T(256)}, f32[192]{0:T(256)}, f32[6,16]{1,0:T(8,128)}, /*index=5*/f32[6,16]{1,0:T(8,128)}) all-reduce(f32[192]{0:T(256)S(1)} %dynamic-slice.6, f32[192]{0:T(256)S(1)} %dynamic-slice.8, f32[192]{0:T(256)S(1)} %dynamic-slice.10, ...), channel_id=1, replica_groups=mesh['shard'=4,'ctx'=4,'tp'=2] {'ctx'}, use_global_device_ids=true, to_apply=%region_22.23 | all-reduce | flops 960 | bytes 7680 | tf_op jit(solution)/shard_map/psum | solution.py:243
  777.3 1.1 fusion.39
  778.3 61.4 %all-reduce.26.cloned.1.call-done = (f32[192,384]{1,0:T(8,128)}, f32[192,384]{1,0:T(8,128)}, f32[192,384]{1,0:T(8,128)}, f32[384,192]{0,1:T(8,128)}, f32[192,1536]{1,0:T(8,128)}, /*index=5*/f32[1536,192]{0,1:T(8,128)}) async-done(((f32[192,384]{1,0:T(8,128)}, f32[192,384]{1,0:T(8,128)}, f32[192,384]{1,0:T(8,128)}, f32[384,192]{0,1:T(8,128)}, f32[192,1536]{1,0:T(8,128)}, /*index=5*/f32[1536,192]{0,1:T(8,128)}), ...) | async-done | bytes 3538960 | tf_op jit(solution)/shard_map/psum | solution.py:243
  839.7 1.8 copy.66
  841.5 1.7 copy.67
  843.2 1.7 copy.68
  846.6 1.0 copy.71
  (239 shorter events, 18.9 us)
Async XLA Ops:
  8.0 39.1 %copy-start.3 = (bf16[1,256,768]{2,1,0:T(8,128)(2,1)S(1)}, bf16[1,256,768]{2,1,0:T(8,128)(2,1)}, u32[]{:S(2)}) copy-start(bf16[1,256,768]{2,1,0:T(8,128)(2,1)} %param.14) | copy-start | bytes 1179652
  8.0 163.1 %all-reduce.18.cloned.1.call-start = ((), (), s32[]{:S(2)}) async-start(), calls=%async_computation.10 | async-start | bytes 1572864 | tf_op jit(solution)/shard_map/psum | solution.py:133
  26.6 21.0 %copy-start.17 = (bf16[768,384]{1,0:T(8,128)(2,1)}, bf16[768,384]{1,0:T(8,128)(2,1)S(1)}, u32[]{:S(2)}) copy-start(bf16[768,384]{1,0:T(8,128)(2,1)S(1)} %all_gather.44) | copy-start | bytes 1769476
  44.7 73.5 %copy-start.42 = (f32[768]{0:T(1024)}, f32[768]{0:T(1024)S(1)}, u32[]{:S(2)}) copy-start(f32[768]{0:T(1024)S(1)} %convert_element_type.143) | copy-start | bytes 9220
  45.9 72.4 %copy-start.47 = (f32[256]{0:T(256)}, f32[256]{0:T(256)S(1)}, u32[]{:S(2)}) copy-start(f32[256]{0:T(256)S(1)} %broadcast_multiply_fusion.5) | copy-start | bytes 3076
  47.1 27.3 %copy-start.51 = (f32[256]{0:T(256)}, f32[256]{0:T(256)S(1)}, u32[]{:S(2)}) copy-start(f32[256]{0:T(256)S(1)} %add_rsqrt_fusion.1) | copy-start | bytes 3076
  47.6 11.5 %copy-start.29 = (bf16[192,384]{1,0:T(8,128)(2,1)S(1)}, bf16[192,384]{1,0:T(8,128)(2,1)}, u32[]{:S(2)}) copy-start(bf16[192,384]{1,0:T(8,128)(2,1)} %param.23) | copy-start | bytes 442372
  74.5 26.9 %copy-start.31 = (bf16[192,384]{1,0:T(8,128)(2,1)S(1)}, bf16[192,384]{1,0:T(8,128)(2,1)}, u32[]{:S(2)}) copy-start(bf16[192,384]{1,0:T(8,128)(2,1)} %param.22) | copy-start | bytes 442372
  75.0 12.1 %copy-start.14 = (f32[256,6,64]{0,2,1:T(8,128)}, f32[256,6,64]{0,2,1:T(8,128)S(1)}, u32[]{:S(2)}) copy-start(f32[256,6,64]{0,2,1:T(8,128)S(1)} %get-tuple-element.109) | copy-start | bytes 1179652
  75.0 42.7 %copy-start.57 = (f32[256,6]{0,1:T(8,128)}, f32[256,6]{0,1:T(8,128)S(1)}, u32[]{:S(2)}) copy-start(f32[256,6]{0,1:T(8,128)S(1)} %get-tuple-element.108) | copy-start | bytes 18436
  87.0 30.7 %copy-start.45 = (f32[64,6]{0,1:T(8,128)}, f32[64,6]{0,1:T(8,128)S(1)}, u32[]{:S(2)}) copy-start(f32[64,6]{0,1:T(8,128)S(1)} %reshape.424) | copy-start | bytes 4612
  87.0 30.7 %copy-start.35 = (f32[256,6]{0,1:T(8,128)}, f32[256,6]{0,1:T(8,128)S(1)}, u32[]{:S(2)}) copy-start(f32[256,6]{0,1:T(8,128)S(1)} %fusion.70) | copy-start | bytes 18436
  101.4 45.3 %copy-start.6 = (bf16[1,1024,384]{1,2,0:T(8,128)(2,1)}, bf16[1,1024,384]{1,2,0:T(8,128)(2,1)S(1)}, u32[]{:S(2)}) copy-start(bf16[1,1024,384]{1,2,0:T(8,128)(2,1)S(1)} %all_gather.50) | copy-start | bytes 2359300
  119.5 12.0 %copy-start.59 = (f32[256,6]{0,1:T(8,128)}, f32[256,6]{0,1:T(8,128)S(1)}, u32[]{:S(2)}) copy-start(f32[256,6]{0,1:T(8,128)S(1)} %get-tuple-element.110) | copy-start | bytes 18436
  119.5 28.4 %copy-start.7 = (f32[256,6,64]{0,2,1:T(8,128)}, f32[256,6,64]{0,2,1:T(8,128)S(1)}, u32[]{:S(2)}) copy-start(f32[256,6,64]{0,2,1:T(8,128)S(1)} %get-tuple-element.111) | copy-start | bytes 1179652
  131.5 16.4 %copy-start.39 = (f32[64,6]{0,1:T(8,128)}, f32[64,6]{0,1:T(8,128)S(1)}, u32[]{:S(2)}) copy-start(f32[64,6]{0,1:T(8,128)S(1)} %reshape.423) | copy-start | bytes 4612
  154.3 49.5 %all-gather.6.cloned.1.call-start = ((), (), s32[]{:S(2)}) async-start(), calls=%async_computation.11 | async-start | bytes 2949120 | tf_op jit(solution)/shard_map/all_gather | solution.py:70
  154.9 99.2 %all-gather.8.cloned.1.call-start = ((), (), s32[]{:S(2)}) async-start(), calls=%async_computation.12 | async-start | bytes 2949120 | tf_op jit(solution)/shard_map/all_gather | solution.py:72
  155.5 123.1 %all-reduce.22.cloned.1.call-start = ((), (), s32[]{:S(2)}) async-start(), calls=%async_computation.14 | async-start | bytes 1572864 | tf_op jit(solution)/shard_map/psum | solution.py:148
  155.5 55.0 %copy-start.37 = (f32[768]{0:T(1024)}, f32[768]{0:T(1024)S(1)}, u32[]{:S(2)}) copy-start(f32[768]{0:T(1024)S(1)} %convert_element_type.158) | copy-start | bytes 9220
  172.4 128.8 %copy-start.1 = (f32[256,768]{1,0:T(8,128)}, f32[256,768]{1,0:T(8,128)S(1)}, u32[]{:S(2)}) copy-start(f32[256,768]{1,0:T(8,128)S(1)} %get-tuple-element.101) | copy-start | bytes 2359300
  172.4 128.8 %copy-start.55 = (f32[256]{0:T(256)}, f32[256]{0:T(256)S(1)}, u32[]{:S(2)}) copy-start(f32[256]{0:T(256)S(1)} %broadcast_multiply_fusion.4) | copy-start | bytes 3076
  172.6 128.6 %copy-start.61 = (f32[256]{0:T(256)}, f32[256]{0:T(256)S(1)}, u32[]{:S(2)}) copy-start(f32[256]{0:T(256)S(1)} %add_rsqrt_fusion) | copy-start | bytes 3076
  210.6 50.3 %copy-start.19 = (bf16[256,1536]{1,0:T(8,128)(2,1)}, bf16[256,1536]{1,0:T(8,128)(2,1)S(1)}, u32[]{:S(2)}) copy-start(bf16[256,1536]{1,0:T(8,128)(2,1)S(1)} %get-tuple-element.98) | copy-start | bytes 2359300
  254.1 4.8 copy-start.72
  260.6 40.6 %all-reduce.20.cloned.1.call-start = ((), (), s32[]{:S(2)}) async-start(), calls=%async_computation.13 | async-start | bytes 786432 | tf_op jit(solution)/shard_map/psum | solution.py:139
  260.8 43.3 %copy-start.34 = (f32[6,256]{1,0:T(8,128)}, f32[6,256]{1,0:T(8,128)S(1)}, u32[]{:S(2)}) copy-start(f32[6,256]{1,0:T(8,128)S(1)} %log_add_fusion) | copy-start | bytes 18436
  264.1 81.4 %reduce-scatter.15.cloned.1.call-start = ((), (), s32[]{:S(2)}) async-start(), calls=%async_computation.15 | async-start | bytes 1966080 | tf_op jit(solution)/shard_map/reduce_scatter | solution.py:192
  303.6 5.0 copy-start.4
  304.1 4.5 copy-start.21
  304.1 4.5 slice-start
  304.2 4.8 slice-start.1
  313.3 66.3 %reduce-scatter.17.cloned.1.call-start = ((), (), s32[]{:S(2)}) async-start(), calls=%async_computation.16 | async-start | bytes 1966080 | tf_op jit(solution)/shard_map/reduce_scatter | solution.py:198
  318.5 93.1 %reduce-scatter.19.cloned.1.call-start = ((), (), s32[]{:S(2)}) async-start(), calls=%async_computation.18 | async-start | bytes 1474560 | tf_op jit(solution)/shard_map/reduce_scatter | solution.py:274
  323.6 22.0 %copy-start.15 = (f32[256,6,64]{0,2,1:T(8,128)S(1)}, f32[256,6,64]{0,2,1:T(8,128)}, u32[]{:S(2)}) copy-start(f32[256,6,64]{0,2,1:T(8,128)} %copy-done.14) | copy-start | bytes 1179652
  323.6 22.0 %copy-start.36 = (f32[256,6]{0,1:T(8,128)S(1)}, f32[256,6]{0,1:T(8,128)}, u32[]{:S(2)}) copy-start(f32[256,6]{0,1:T(8,128)} %copy-done.35) | copy-start | bytes 18436
  323.6 22.0 %copy-start.46 = (f32[64,6]{0,1:T(8,128)S(1)}, f32[64,6]{0,1:T(8,128)}, u32[]{:S(2)}) copy-start(f32[64,6]{0,1:T(8,128)} %copy-done.45) | copy-start | bytes 4612
  323.6 23.7 %copy-start.58 = (f32[256,6]{0,1:T(8,128)S(1)}, f32[256,6]{0,1:T(8,128)}, u32[]{:S(2)}) copy-start(f32[256,6]{0,1:T(8,128)} %copy-done.57) | copy-start | bytes 18436
  323.6 118.4 %reduce-scatter.25.cloned.1.call-start = ((), (), s32[]{:S(2)}) async-start(), calls=%async_computation.21 | async-start | bytes 1474560 | tf_op jit(solution)/shard_map/reduce_scatter | solution.py:278
  325.2 23.3 %copy-start.44 = (f32[768]{0:T(1024)S(1)}, f32[768]{0:T(1024)}, u32[]{:S(2)}) copy-start(f32[768]{0:T(1024)} %copy-done.42) | copy-start | bytes 9220
  325.2 23.3 %copy-start.49 = (f32[256]{0:T(256)S(1)}, f32[256]{0:T(256)}, u32[]{:S(2)}) copy-start(f32[256]{0:T(256)} %copy-done.47) | copy-start | bytes 3076
  325.2 23.3 %copy-start.53 = (f32[256]{0:T(256)S(1)}, f32[256]{0:T(256)}, u32[]{:S(2)}) copy-start(f32[256]{0:T(256)} %copy-done.51) | copy-start | bytes 3076
  325.2 147.7 %reduce-scatter.21.cloned.1.call-start = ((), (), s32[]{:S(2)}) async-start(), calls=%async_computation.19 | async-start | bytes 1474560 | tf_op jit(solution)/shard_map/reduce_scatter | solution.py:275
  350.1 32.1 %copy-start.2 = (f32[256,768]{1,0:T(8,128)S(1)}, f32[256,768]{1,0:T(8,128)}, u32[]{:S(2)}) copy-start(f32[256,768]{1,0:T(8,128)} %copy-done.1) | copy-start | bytes 2359300
  350.1 32.1 %copy-start.26 = (bf16[256,1536]{1,0:T(8,128)(2,1)S(1)}, bf16[256,1536]{1,0:T(8,128)(2,1)}, u32[]{:S(2)}) copy-start(bf16[256,1536]{1,0:T(8,128)(2,1)} %copy-done.25) | copy-start | bytes 2359300
  350.1 32.1 %copy-start.38 = (f32[768]{0:T(1024)S(1)}, f32[768]{0:T(1024)}, u32[]{:S(2)}) copy-start(f32[768]{0:T(1024)} %copy-done.37) | copy-start | bytes 9220
  350.1 32.1 %copy-start.56 = (f32[256]{0:T(256)S(1)}, f32[256]{0:T(256)}, u32[]{:S(2)}) copy-start(f32[256]{0:T(256)} %copy-done.55) | copy-start | bytes 3076
  350.2 32.1 %copy-start.62 = (f32[256]{0:T(256)S(1)}, f32[256]{0:T(256)}, u32[]{:S(2)}) copy-start(f32[256]{0:T(256)} %copy-done.61) | copy-start | bytes 3076
  350.2 153.1 %reduce-scatter.23.cloned.1.call-start = ((), (), s32[]{:S(2)}) async-start(), calls=%async_computation.20 | async-start | bytes 1474560 | tf_op jit(solution)/shard_map/reduce_scatter | solution.py:276
  382.2 207.3 %reduce-scatter.27.cloned.1.call-start = ((), (), s32[]{:S(2)}) async-start(), calls=%async_computation.22 | async-start | bytes 5898240 | tf_op jit(solution)/shard_map/reduce_scatter | solution.py:277
  385.4 292.3 %reduce-scatter.29.cloned.1.call-start = ((), (), s32[]{:S(2)}) async-start(), calls=%async_computation.23 | async-start | bytes 5898240 | tf_op jit(solution)/shard_map/reduce_scatter | solution.py:279
  389.7 331.4 %reduce-scatter.31.cloned.1.call-start = ((), (), s32[]{:S(2)}) async-start(), calls=%async_computation.24 | async-start | bytes 40960
  391.5 330.4 %reduce-scatter.33.cloned.1.call-start = ((), (), s32[]{:S(2)}) async-start(), calls=%async_computation.25 | async-start | bytes 40960
  393.6 346.0 %all-reduce.24.cloned.1.call-start = ((), (), s32[]{:S(2)}) async-start(), calls=%async_computation.17 | async-start | bytes 1572864 | tf_op jit(solution)/shard_map/psum | solution.py:222
  396.3 443.4 %all-reduce.26.cloned.1.call-start = ((), (), s32[]{:S(2)}) async-start(), calls=%async_computation.26 | async-start | bytes 7077888 | tf_op jit(solution)/shard_map/psum | solution.py:243
  677.7 42.6 %copy-start.30 = (bf16[192,384]{1,0:T(8,128)(2,1)S(1)}, bf16[192,384]{1,0:T(8,128)(2,1)}, u32[]{:S(2)}) copy-start(bf16[192,384]{1,0:T(8,128)(2,1)} %param.23) | copy-start | bytes 442372
  677.7 42.6 %copy-start.32 = (bf16[192,384]{1,0:T(8,128)(2,1)S(1)}, bf16[192,384]{1,0:T(8,128)(2,1)}, u32[]{:S(2)}) copy-start(bf16[192,384]{1,0:T(8,128)(2,1)} %param.22) | copy-start | bytes 442372
  677.8 61.9 %copy-start.50 = (f32[256]{0:T(256)S(1)}, f32[256]{0:T(256)}, u32[]{:S(2)}) copy-start(f32[256]{0:T(256)} %copy-done.47) | copy-start | bytes 3076
  677.8 61.9 %copy-start.54 = (f32[256]{0:T(256)S(1)}, f32[256]{0:T(256)}, u32[]{:S(2)}) copy-start(f32[256]{0:T(256)} %copy-done.51) | copy-start | bytes 3076
  677.8 63.5 %copy-start.65 = (f32[768]{0:T(1024)S(1)}, f32[768]{0:T(1024)}, u32[]{:S(2)}) copy-start(f32[768]{0:T(1024)} %get-tuple-element.66) | copy-start | bytes 9220
  677.8 63.5 %copy-start.66 = (f32[768]{0:T(1024)S(1)}, f32[768]{0:T(1024)}, u32[]{:S(2)}) copy-start(f32[768]{0:T(1024)} %get-tuple-element.76) | copy-start | bytes 9220
  739.6 37.6 %copy-start.16 = (f32[256,768]{1,0:T(8,128)S(1)}, f32[256,768]{1,0:T(8,128)}, u32[]{:S(2)}) copy-start(f32[256,768]{1,0:T(8,128)} %all-reduce.24.cloned.1.call-done) | copy-start | bytes 2359300
  839.7 5.2 copy-start.33
  839.7 5.9 copy-start.24
  (28 other events, 52.9 us)
Sparse Core Ops, SparseCore 0:
  154.4 16.6 all-reduce.17
  260.7 17.8 all-reduce.21
  281.5 19.6 all-reduce.19
  313.4 32.1 reduce-scatter.14
  348.6 30.9 reduce-scatter.16
  382.4 29.1 reduce-scatter.18
  414.1 27.8 reduce-scatter.24
  445.0 27.8 reduce-scatter.20
  475.3 27.8 reduce-scatter.22
  505.5 83.9 reduce-scatter.26
  591.9 85.7 reduce-scatter.28
  680.5 19.4 reduce-scatter.30
  702.8 17.1 reduce-scatter.32
  722.3 17.3 all-reduce.23
  743.3 96.3 all-reduce.25
Sparse Core Ops, SparseCore 1:
  156.4 47.3 all-gather.5
  205.3 48.7 all-gather.7
where the time goes:
time: 856 us; the launch traced here: 855 us
  waiting for transfers between devices  536 us (63%)
  blocking collectives  204 us (24%)
  matrix products  54.5 us (6%)
  local copies, waits for them, and re-layouts  22.3 us (3%)
  other arithmetic  20.1 us (2%)
  between operations  17.5 us (2%)
    reduce_scatter x1, waiting for transfers between devices, on_device(): lax.psum_scatter(sum_down, 'shard', scatter_dimension=1, tiled=True)  88.2 us
    reduce_scatter x1, waiting for transfers between devices, on_device(): lax.psum_scatter(sum_up, 'shard', scatter_dimension=0, tiled=True)  86.3 us
    psum x1, waiting for transfers between devices, on_device(): lax.psum((grad_w_query, grad_w_key, grad_w_value, grad_w_up, grad_w_out,...  61.4 us
    all_gather x1, waiting for transfers between devices, on_device(): lax.all_gather(w_down, 'shard', axis=1, tiled=True)  43.5 us
    pmax x1, blocking collectives, on_device(): peak_all = lax.pmax(local_peak, ('shard', 'ctx'))  41.2 us
    unnamed x2, blocking collectives  31.7 us
    all_gather x1, waiting for transfers between devices, on_device(): lax.all_gather(w_up, 'shard', axis=0, tiled=True)  31.2 us
    reduce_scatter x1, waiting for transfers between devices, on_device(): lax.psum_scatter(sum_key, 'shard', scatter_dimension=0, tiled=True)  30.9 us
  transfers between devices with their start and end apart: 17, of which 15 were waited for; matrix products, arithmetic and copies ran while one was open for 6% of the time, Pallas kernels for 0%

commit v1 on v0

--- a/solution.py
+++ b/solution.py
@@ -1,6 +1,9 @@
+import functools
 import jax
 import jax.numpy as jnp
 from jax import lax
+from jax.experimental import pallas as pl
+from jax.experimental.pallas import tpu as pltpu
 from jax.sharding import PartitionSpec as P
 
 norm_eps = 1e-06
@@ -34,7 +37,7 @@
     return jax.nn.gelu(values, approximate=False)
 
 
-def on_device(
+def general_layer(
     images,
     cotangent,
     ln1_gain,
@@ -308,6 +311,823 @@
     )
 
 
+MESH = pl.DeviceIdType.MESH
+NN = (((1,), (0,)), ((), ()))
+NT = (((1,), (1,)), ((), ()))
+TN = (((0,), (0,)), ((), ()))
+low_type = jnp.bfloat16
+full_type = jnp.float32
+
+
+def dot(left, right, dims=NN):
+    return lax.dot_general(left, right, dims, preferred_element_type=full_type)
+
+
+def flip(place, bits, count):
+    result = 0
+    unit = 1
+    while unit < count:
+        result = result + ((place // unit + bits // unit) % 2) * unit
+        unit *= 2
+    return result
+
+
+def fits_fused(images, w_query, w_up, q_gain):
+    count_img, local_len, width = images.shape
+    ctx, shard, tp = lax.axis_size("ctx"), lax.axis_size("shard"), lax.axis_size("tp")
+    rows = w_query.shape[0]
+    return (
+        count_img == 1
+        and tp == 2
+        and ctx == 4
+        and shard == 4
+        and rows % (16 * ctx) == 0
+        and local_len % 32 == 0
+        and q_gain.shape[0] % 2 == 0
+        and w_up.shape[1] % (128 * ctx) == 0
+    )
+
+
+def fused_kernel(
+    sizes,
+    img_h, cot_h, small_h, wq_h, wk_h, wv_h, wo_h, wup_h, wdn_h,
+    bo_o, ig_o, upo, dno, qkvo, lnr_o, qkr_o, peak_o,
+    xg, ctg, smalls, wl, wol, wdl, wqkv, wot, wup, wdt, wtmp,
+    xh1, h1, nq, nk, sq, sk, qs, kall, vall, pst, sbuf, attq, attr, pks,
+    h2, ga, act, gu, g2s, g2r, g2own, bos, bor, boown,
+    gsib_s, gsib_r, gown, gz_s, gz_r, gfin,
+    gres, gbg, gms, gm, dqb, dkt, dvt, dks_s, dks_r, dqr, dkr, dvr,
+    g1s, g1r, g1own, qsib_s, qsib_r, qown, qz_s, qz_r, qfin,
+    rows_s, rows_r, obuf,
+    lsem, ssem, rsem,
+):
+    CN, ZN, TB, D, HW, FS, R = sizes
+    QR = R // CN
+    HR = R // 2
+    s_i, c_i, t_i = lax.axis_index("shard"), lax.axis_index("ctx"), lax.axis_index("tp")
+    o_i = 1 - t_i
+    half_chips = CN // 2
+    tstar = c_i // half_chips
+    place = c_i % half_chips
+    TK = CN * TB
+    inv_d = 1.0 / D
+
+    def at_ctx(j):
+        return (s_i, flip(c_i, j, CN), t_i)
+
+    def at_z(j):
+        return (flip(s_i, j, ZN), c_i, t_i)
+
+    sib = (s_i, c_i, o_i)
+
+    spots = {}
+
+    def spot(name, count):
+        if name not in spots:
+            spots[name] = (sum(n for _, n in spots.values()), count)
+        return spots[name][0]
+
+    def put(name, count, j, src, dst, dev):
+        base = spot(name, count)
+        pltpu.make_async_remote_copy(
+            src_ref=src, dst_ref=dst, send_sem=ssem.at[base + j], recv_sem=rsem.at[base + j],
+            device_id=dev, device_id_type=MESH,
+        ).start()
+
+    def got(name, count, j, dst, dev):
+        base = spot(name, count)
+        pltpu.make_async_remote_copy(
+            src_ref=dst, dst_ref=dst, send_sem=ssem.at[base + j], recv_sem=rsem.at[base + j],
+            device_id=dev, device_id_type=MESH,
+        ).wait_recv()
+
+    def sent(name, count, j, src, dev):
+        base = spot(name, count)
+        pltpu.make_async_remote_copy(
+            src_ref=src, dst_ref=src, send_sem=ssem.at[base + j], recv_sem=rsem.at[base + j],
+            device_id=dev, device_id_type=MESH,
+        ).wait_send()
+
+    x_src = img_h.at[0, pl.ds(t_i * TB, TB)]
+    c_src = cot_h.at[0, pl.ds(t_i * TB, TB)]
+    locals_ = [
+        pltpu.make_async_copy(wk_h, wl.at[1], lsem.at[0]),
+        pltpu.make_async_copy(wv_h, wl.at[2], lsem.at[1]),
+        pltpu.make_async_copy(wq_h, wl.at[0], lsem.at[2]),
+        pltpu.make_async_copy(x_src, xg.at[0], lsem.at[3]),
+        pltpu.make_async_copy(wo_h, wol, lsem.at[4]),
+        pltpu.make_async_copy(wdn_h.at[pl.ds(c_i * FS, FS)], wdl, lsem.at[5]),
+        pltpu.make_async_copy(wup_h.at[:, pl.ds(c_i * FS, FS)], wup.at[t_i, s_i], lsem.at[6]),
+        pltpu.make_async_copy(c_src, ctg.at[0], lsem.at[7]),
+    ]
+    for copy in locals_:
+        copy.start()
+
+    barrier = pltpu.get_barrier_semaphore()
+    greet = [at_ctx(j) for j in range(1, CN)] + [at_z(j) for j in range(1, ZN)] + [sib]
+    for dev in greet:
+        pl.semaphore_signal(barrier, inc=1, device_id=dev, device_id_type=MESH)
+    pl.semaphore_wait(barrier, len(greet))
+
+    for j in range(1, CN):
+        put("x", CN, j, x_src, xg.at[j], at_ctx(j))
+    smalls[t_i, s_i] = small_h[...]
+    for j in range(1, ZN):
+        put("small", ZN, j, small_h, smalls.at[t_i, s_i], at_z(j))
+
+    order_w = (1, 2, 0)
+
+    @pl.when(t_i == tstar)
+    def _():
+        pick = (
+            lax.broadcasted_iota(jnp.int32, (half_chips * HW, HW), 0)
+            == lax.broadcasted_iota(jnp.int32, (half_chips * HW, HW), 1) + place * HW
+        ).astype(full_type).astype(low_type)
+        for n, g in enumerate(order_w):
+            locals_[n].wait()
+            wqkv[g, s_i] = dot(wl[g], pick).astype(low_type)
+            for j in range(1, ZN):
+                put("w%d" % g, ZN, j, wqkv.at[g, s_i], wqkv.at[g, s_i], at_z(j))
+            put("w%d" % g, ZN, 0, wqkv.at[g, s_i], wqkv.at[g, s_i], sib)
+
+    @pl.when(t_i != tstar)
+    def _():
+        for n in range(3):
+            locals_[n].wait()
+            spot("w%d" % order_w[n], ZN)
+
+    locals_[4].wait()
+    for kk in range(half_chips):
+        wtmp[...] = wol[kk * HW:(kk + 1) * HW, :].astype(full_type).T.astype(low_type).reshape(CN, QR, HW)
+        wot[half_chips * t_i + kk, s_i, c_i] = wtmp[c_i]
+    for j in range(1, ZN):
+        block = wot.at[pl.ds(half_chips * t_i, half_chips), s_i, c_i]
+        put("woz", ZN, j, block, block, at_z(j))
+    locals_[5].wait()
+    wdt[t_i, s_i] = wdl[...].astype(full_type).T.astype(low_type)
+
+    for j in range(1, ZN):
+        got("small", ZN, j, smalls.at[t_i, flip(s_i, j, ZN)], at_z(j))
+    put("smallt", 1, 0, smalls.at[t_i], smalls.at[t_i], sib)
+
+    locals_[3].wait()
+
+    def norm_rows(values):
+        mean = jnp.sum(values, axis=-1, keepdims=True) * inv_d
+        center = values - mean
+        inverse = lax.rsqrt(jnp.sum(center * center, axis=-1, keepdims=True) * inv_d + norm_eps)
+        return center * inverse, inverse
+
+    ln_rows = jnp.concatenate([smalls[t_i, k][:, :R] for k in range(ZN)], axis=1)
+    g1row, b1row, g2row, b2row = (ln_rows[k:k + 1] for k in range(4))
+
+    def first_norm(j, _):
+        @pl.when(j > 0)
+        def _():
+            got("x", CN, j, xg.at[j], at_ctx(j))
+
+        normed, _unused = norm_rows(xg[j].astype(full_type))
+        xh1[j] = normed
+        h1[j] = (normed * g1row + b1row).astype(low_type)
+        return 0
+
+    lax.fori_loop(0, CN, first_norm, 0)
+
+    got("smallt", 1, 0, smalls.at[o_i], sib)
+    head_rows = smalls[0, 0][4:6, :HW]
+    for a in range(2):
+        for k in range(ZN):
+            if a or k:
+                head_rows = head_rows + smalls[a, k][4:6, :HW]
+    qgrow, kgrow = head_rows[0:1], head_rows[1:2]
+
+    lane = lax.broadcasted_iota(jnp.int32, (1, HW), 1) // 64
+    heads = HW // 64
+    mask_f = [(lane == h).astype(full_type) for h in range(heads)]
+    mask_b = [m.astype(low_type) for m in mask_f]
+    same_head = (
+        lax.broadcasted_iota(jnp.int32, (HW, HW), 0) // 64
+        == lax.broadcasted_iota(jnp.int32, (HW, HW), 1) // 64
+    ).astype(full_type).astype(low_type)
+
+    def head_mean(values):
+        high = values.astype(low_type)
+        rest = (values - high.astype(full_type)).astype(low_type)
+        return (dot(high, same_head) + dot(rest, same_head)) * (1.0 / 64)
+
+    def weight_ready(g):
+        @pl.when(t_i != tstar)
+        def _():
+            got("w%d" % g, ZN, 0, wqkv.at[g, s_i], sib)
+
+        for j in range(1, ZN):
+            block = wqkv.at[g, flip(s_i, j, ZN)]
+            got("w%d" % g, ZN, j, block, sib)
+
+            @pl.when(t_i == tstar)
+            def _():
+                put("f%d" % g, ZN, j, block, block, sib) if False else pltpu.make_async_remote_copy(
+                    src_ref=block, dst_ref=block,
+                    send_sem=ssem.at[spot("f%d" % g, ZN) + j],
+                    recv_sem=rsem.at[spot("w%d" % g, ZN) + j],
+                    device_id=sib, device_id_type=MESH,
+                ).start()
+
+    def project(g):
+        return dot(h1[...].reshape(TK, D), wqkv[g].reshape(D, HW))
+
+    weight_ready(1)
+    raw = project(1)
+    inverse = lax.rsqrt(head_mean(raw * raw) + norm_eps)
+    normed = raw * inverse
+    nk[...] = normed
+    sk[...] = inverse
+    kall[0] = (normed * kgrow).astype(low_type)
+    put("k", 1, 0, kall.at[0], kall.at[1], sib)
+    weight_ready(2)
+    vall[0] = project(2).astype(low_type)
+    put("v", 1, 0, vall.at[0], vall.at[1], sib)
+    weight_ready(0)
+    for j in range(1, ZN):
+        put("wdz", ZN, j, wdt.at[t_i, s_i], wdt.at[t_i, s_i], at_z(j))
+    locals_[6].wait()
+    for j in range(1, ZN):
+        put("wuz", ZN, j, wup.at[t_i, s_i], wup.at[t_i, s_i], at_z(j))
+    raw = project(0)
+    inverse = lax.rsqrt(head_mean(raw * raw) + norm_eps)
+    normed = raw * inverse
+    nq[...] = normed
+    sq[...] = inverse
+    qs[...] = ((normed * qgrow).astype(low_type) * 0.125).astype(low_type).reshape(CN, TB, HW)
+
+    mine = pl.ds(half_chips * t_i, half_chips)
+    for j in range(1, ZN):
+        got("woz", ZN, j, wot.at[mine, flip(s_i, j, ZN), c_i], at_z(j))
+    for j in range(1, CN):
+        put("woc", CN, j, wot.at[mine, :, c_i], wot.at[mine, :, c_i], at_ctx(j))
+    for j in range(1, CN):
+        put("ct", CN, j, c_src, ctg.at[j], at_ctx(j))
+    got("k", 1, 0, kall.at[1], sib)
+    got("v", 1, 0, vall.at[1], sib)
+
+    step = 32
+    ones_of = lax.broadcasted_iota(jnp.int32, (8, 128), 1)
+
+    def stacked(block):
+        return jnp.concatenate([block * m for m in mask_b], axis=0)
+
+    def folded(block):
+        total = block[0:TB] * mask_f[0]
+        for h in range(1, heads):
+            total = total + block[h * TB:(h + 1) * TB] * mask_f[h]
+        return total
+
+    pks[0] = jnp.full((8, 128), -3.0e38, full_type)
+
+    def attend(i, _):
+        j = CN - 1 - i
+
+        @pl.when(i == 2)
+        def _():
+            for q in range(1, CN):
+                got("woc", CN, q, wot.at[mine, :, flip(c_i, q, CN)], at_ctx(q))
+            put("wot", 1, 0, wot.at[mine], wot.at[mine], sib)
+
+        sbuf[...] = dot(stacked(qs[j]), kall[...].reshape(2 * TK, HW), NT)
+
+        for h in range(heads):
+            def soft(r, top_all):
+                rows = pl.ds(pl.multiple_of(h * TB + r * step, step), step)
+                scores = sbuf[rows]
+                top = jnp.max(scores, axis=-1, keepdims=True)
+                expo = jnp.exp(scores - top)
+                total = jnp.sum(expo, axis=-1, keepdims=True)
+                pst[j, rows] = expo * (1.0 / total)
+                return jnp.maximum(top_all, jnp.max(top, axis=0, keepdims=True))
+
+            peak = lax.fori_loop(0, TB // step, soft, jnp.full((1, 1), -3.0e38, full_type))
+            pks[0] = jnp.where(ones_of == c_i * heads + h, jnp.maximum(pks[0], peak), pks[0])
+        mixed = folded(dot(pst[j].astype(low_type), vall[...].reshape(2 * TK, HW)))
+        attq[j] = mixed.astype(low_type)
+
+        @pl.when(j > 0)
+        def _():
+            put("att", CN, j, attq.at[j], attr.at[j], at_ctx(j))
+
+        return 0
+
+    lax.fori_loop(0, CN, attend, 0)
+    put("pkt", 1, 0, pks.at[0], pks.at[1], sib)
+
+    got("wot", 1, 0, wot.at[pl.ds(half_chips * o_i, half_chips)], sib)
+    branch = dot(attq[0], wot[c_i].reshape(D, HW), NT)
+    for j in range(1, CN):
+        got("att", CN, j, attr.at[j], at_ctx(j))
+        branch = branch + dot(attr[j], wot[flip(c_i, j, CN)].reshape(D, HW), NT)
+    resid = xg[0].astype(full_type) + branch
+    boown[...] = resid
+    xhat2, inv2 = norm_rows(resid)
+    h2[0] = (xhat2 * g2row + b2row).astype(low_type)
+    for j in range(1, CN):
+        put("h2", CN, j, h2.at[0], h2.at[j], at_ctx(j))
+
+    locals_[7].wait()
+    for j in range(1, CN):
+        got("ct", CN, j, ctg.at[j], at_ctx(j))
+    for j in range(1, ZN):
+        got("wdz", ZN, j, wdt.at[t_i, flip(s_i, j, ZN)], at_z(j))
+    put("wdt", 1, 0, wdt.at[t_i], wdt.at[t_i], sib)
+    ga[t_i] = dot(ctg[...].reshape(TK, D), wdt[t_i].reshape(D, FS)).reshape(CN, TB, FS)
+    for j in range(1, ZN):
+        got("wuz", ZN, j, wup.at[t_i, flip(s_i, j, ZN)], at_z(j))
+    put("wut", 1, 0, wup.at[t_i], wup.at[t_i], sib)
+    got("wdt", 1, 0, wdt.at[o_i], sib)
+    ga[o_i] = dot(ctg[...].reshape(TK, D), wdt[o_i].reshape(D, FS)).reshape(CN, TB, FS)
+    got("wut", 1, 0, wup.at[o_i], sib)
+
+    def mlp(j, _):
+        @pl.when(j > 0)
+        def _():
+            got("h2", CN, j, h2.at[j], at_ctx(j))
+
+        block = h2[j]
+        for a in range(2):
+            up = dot(block, wup[a].reshape(D, FS))
+            phi = 0.5 * (1.0 + lax.erf(up * 0.7071067811865476))
+            dens = jnp.exp(up * up * -0.5) * 0.3989422804014327
+            act[a, j] = (up * phi).astype(low_type)
+            gu[a, j] = (ga[a, j] * (phi + up * dens)).astype(low_type)
+        grad_two = dot(gu[0, j], wup[0].reshape(D, FS), NT) + dot(gu[1, j], wup[1].reshape(D, FS), NT)
+
+        @pl.when(j == 0)
+        def _():
+            g2own[...] = grad_two
+
+        @pl.when(j > 0)
+        def _():
+            g2s[j] = grad_two.astype(low_type)
+            put("g2", CN, j, g2s.at[j], g2r.at[j], at_ctx(j))
+
+        return 0
+
+    lax.fori_loop(0, CN, mlp, 0)
+
+    h2_all = h2[...].reshape(TK, D)
+    ct_all = ctg[...].reshape(TK, D)
+    gsib_s[0] = dot(h2_all, gu[o_i].reshape(TK, FS), TN).astype(low_type)
+    put("gs", 2, 0, gsib_s.at[0], gsib_r.at[0], sib)
+    gsib_s[1] = dot(ct_all, act[o_i].reshape(TK, FS), TN).astype(low_type)
+    put("gs", 2, 1, gsib_s.at[1], gsib_r.at[1], sib)
+    gown[0] = dot(h2_all, gu[t_i].reshape(TK, FS), TN)
+    gown[1] = dot(ct_all, act[t_i].reshape(TK, FS), TN)
+
+    def down(j, _):
+        part = dot(act[0, j], wdt[0].reshape(D, FS), NT) + dot(act[1, j], wdt[1].reshape(D, FS), NT)
+
+        @pl.when(j == 0)
+        def _():
+            boown[...] += part
+
+        @pl.when(j > 0)
+        def _():
+            bos[j] = part.astype(low_type)
+
+        return 0
+
+    lax.fori_loop(0, CN, down, 0)
+
+    for k in range(2):
+        got("gs", 2, k, gsib_r.at[k], sib)
+        gown[k] = gown[k] + gsib_r[k].astype(full_type)
+        gz_s[k] = gown[k].astype(low_type).reshape(ZN, R, FS)
+        for j in range(1, ZN):
+            put("gz%d" % k, ZN, j, gz_s.at[k, flip(s_i, j, ZN)], gz_r.at[k, j], at_z(j))
+
+    grad_two = g2own[...]
+    for j in range(1, CN):
+        got("g2", CN, j, g2r.at[j], at_ctx(j))
+        grad_two = grad_two + g2r[j].astype(full_type)
+    ln2g = jnp.sum(grad_two * xhat2, axis=0, keepdims=True)
+    ln2b = jnp.sum(grad_two, axis=0, keepdims=True)
+    hat = grad_two * g2row
+    grad_resid = ctg[0].astype(full_type) + inv2 * (
+        hat
+        - jnp.sum(hat, axis=-1, keepdims=True) * inv_d
+        - xhat2 * (jnp.sum(hat * xhat2, axis=-1, keepdims=True) * inv_d)
+    )
+    gres[...] = grad_resid
+    gb = grad_resid.astype(low_type)
+    gbg[0] = gb
+    for j in range(CN - 1, 0, -1):
+        gms[j] = dot(gb, wot[flip(c_i, j, CN)].reshape(D, HW)).astype(low_type)
+        put("gm", CN, j, gms.at[j], gm.at[j], at_ctx(j))
+    gm[0] = dot(gb, wot[c_i].reshape(D, HW)).astype(low_type)
+    for j in range(1, CN):
+        put("gb", CN, j, gbg.at[0], gbg.at[j], at_ctx(j))
+    for j in range(1, CN):
+        put("bo", CN, j, bos.at[j], bor.at[j], at_ctx(j))
+
+    dkt[...] = jnp.zeros_like(dkt)
+    dvt[...] = jnp.zeros_like(dvt)
+
+    def attend_back(j, _):
+        @pl.when(j > 0)
+        def _():
+            got("gm", CN, j, gm.at[j], at_ctx(j))
+
+        grad_rows = stacked(gm[j])
+        query_rows = stacked(qs[j])
+        sbuf[...] = dot(grad_rows, vall[...].reshape(2 * TK, HW), NT)
+
+        def soft(r, _):
+            rows = pl.ds(pl.multiple_of(r * step, step), step)
+            probs = pst[j, rows]
+            grad_probs = sbuf[rows]
+            inner = jnp.sum(probs * grad_probs, axis=-1, keepdims=True)
+            sbuf[rows] = probs * (grad_probs - inner)
+            return 0
+
+        lax.fori_loop(0, heads * TB // step, soft, 0)
+        grad_scores = sbuf[...].astype(low_type)
+        dqb[j] = folded(dot(grad_scores, kall[...].reshape(2 * TK, HW))) * 0.125
+        dvt[...] += dot(grad_rows, pst[j].astype(low_type), TN)
+        dkt[...] += dot(query_rows, grad_scores, TN)
+        return 0
+
+    lax.fori_loop(0, CN, attend_back, 0)
+    dks_s[0] = dvt[:, TK:].astype(low_type)
+    dks_s[1] = dkt[:, TK:].astype(low_type)
+    for k in range(2):
+        put("dk", 2, k, dks_s.at[k], dks_r.at[k], sib)
+
+    def unnorm(grad_n, gain_row, normed, inverse):
+        gain_grad = jnp.sum(grad_n * normed, axis=0, keepdims=True)
+        e = grad_n * gain_row
+        return (inverse * (e - normed * head_mean(e * normed))).astype(low_type), gain_grad
+
+    h1_all = h1[...].reshape(TK, D)
+
+    def share_grad(n, left, right):
+        full = dot(left, right, TN).reshape(ZN, 2, HR, HW)
+        low_full = full.astype(low_type)
+        for k in range(2):
+            @pl.when(o_i == k)
+            def _():
+                qsib_s[n] = low_full[:, k]
+
+            @pl.when(t_i == k)
+            def _():
+                qown[n] = full[:, k]
+
+        put("qg", 4, n, qsib_s.at[n], qsib_r.at[n], sib)
+
+    def reduce_grad(n):
+        got("qg", 4, n, qsib_r.at[n], sib)
+        total = qown[n] + qsib_r[n].astype(full_type)
+        qown[n] = total
+        qz_s[n] = total.astype(low_type)
+        for j in range(1, ZN):
+            put("qz%d" % n, ZN, j, qz_s.at[n, flip(s_i, j, ZN)], qz_r.at[n, j], at_z(j))
+
+    grad_raw, q_gain_row = unnorm(dqb[...].reshape(TK, HW), qgrow, nq[...], sq[...])
+    dqr[...] = grad_raw
+    for j in range(1, CN):
+        got("gb", CN, j, gbg.at[j], at_ctx(j))
+    share_grad(3, gbg[...].reshape(TK, D), attq[...].reshape(TK, HW))
+    share_grad(0, h1_all, dqr[...])
+    got("dk", 2, 0, dks_r.at[0], sib)
+    dvr[...] = (dvt[:, :TK] + dks_r[0].astype(full_type)).T.astype(low_type)
+    share_grad(2, h1_all, dvr[...])
+    got("dk", 2, 1, dks_r.at[1], sib)
+    grad_k = (dkt[:, :TK] + dks_r[1].astype(full_type)).T
+    grad_raw, k_gain_row = unnorm(grad_k, kgrow, nk[...], sk[...])
+    dkr[...] = grad_raw
+
+    ln1g = jnp.zeros((1, D), full_type)
+    ln1b = jnp.zeros((1, D), full_type)
+    for j in range(CN - 1, -1, -1):
+        rows = slice(j * TB, (j + 1) * TB)
+        part = (
+            dot(dqr[rows], wqkv[0].reshape(D, HW), NT)
+            + dot(dkr[rows], wqkv[1].reshape(D, HW), NT)
+            + dot(dvr[rows], wqkv[2].reshape(D, HW), NT)
+        )
+        ln1g = ln1g + jnp.sum(part * xh1[j], axis=0, keepdims=True)
+        ln1b = ln1b + jnp.sum(part, axis=0, keepdims=True)
+        if j:
+            g1s[j] = part.astype(low_type)
+            put("g1", CN, j, g1s.at[j], g1r.at[j], at_ctx(j))
+        else:
+            g1own[...] = part
+    share_grad(1, h1_all, dkr[...])
+    rows_s[0] = jnp.zeros_like(rows_s[0])
+    for k, row in enumerate((ln1g, ln1b, ln2g, ln2b)):
+        rows_s[0, k:k + 1, :D] = row
+    rows_s[0, 0:1, D:D + HW] = q_gain_row
+    rows_s[0, 1:2, D:D + HW] = k_gain_row
+    put("rt", 1, 0, rows_s.at[0], rows_r.at[0], sib)
+    reduce_grad(3)
+    reduce_grad(0)
+    reduce_grad(2)
+    reduce_grad(1)
+    got("rt", 1, 0, rows_r.at[0], sib)
+    rows_s[1] = rows_s[0] + rows_r[0]
+    for j in range(1, ZN):
+        put("rz", ZN, j, rows_s.at[1], rows_r.at[j], at_z(j))
+
+    for k, out in ((0, upo), (1, dno)):
+        total = gown[k, pl.ds(pl.multiple_of(s_i * R, R), R)]
+        for j in range(1, ZN):
+            got("gz%d" % k, ZN, j, gz_r.at[k, j], at_z(j))
+            total = total + gz_r[k, j].astype(full_type)
+        gfin[k] = total.astype(low_type)
+        for j in range(1, CN):
+            put("gc%d" % k, CN, j, gfin.at[k], out.at[c_i], at_ctx(j))
+        pltpu.make_async_copy(gfin.at[k], out.at[c_i], lsem.at[8 + k]).start()
+
+    total = boown[...]
+    for j in range(1, CN):
+        got("bo", CN, j, bor.at[j], at_ctx(j))
+        total = total + bor[j].astype(full_type)
+    own_rows = pl.ds(t_i * TB, TB)
+    obuf[0] = total.astype(low_type)
+    put("ob", 2, 0, obuf.at[0], bo_o.at[own_rows], sib)
+    pltpu.make_async_copy(obuf.at[0], bo_o.at[own_rows], lsem.at[10]).start()
+
+    got("pkt", 1, 0, pks.at[1], sib)
+    pks[2] = jnp.maximum(pks[0], pks[1])
+    for j in range(1, ZN):
+        put("pkz", ZN, j, pks.at[2], pks.at[2 + j], at_z(j))
+
+    xhat1, inv1 = norm_rows(xg[0].astype(full_type))
+    grad_one = g1own[...]
+    for j in range(1, CN):
+        got("g1", CN, j, g1r.at[j], at_ctx(j))
+        grad_one = grad_one + g1r[j].astype(full_type)
+    hat = grad_one * g1row
+    grad_in = gres[...] + inv1 * (
+        hat
+        - jnp.sum(hat, axis=-1, keepdims=True) * inv_d
+        - xhat1 * (jnp.sum(hat * xhat1, axis=-1, keepdims=True) * inv_d)
+    )
+    obuf[1] = grad_in.astype(low_type)
+    put("ob", 2, 1, obuf.at[1], ig_o.at[own_rows], sib)
+    pltpu.make_async_copy(obuf.at[1], ig_o.at[own_rows], lsem.at[11]).start()
+
+    peak = pks[2]
+    for j in range(1, ZN):
+        got("pkz", ZN, j, pks.at[2 + j], at_z(j))
+        peak = jnp.maximum(peak, pks[2 + j])
+    first = 2 + ZN
+    pks[first] = peak
+    for j in range(1, CN):
+        put("pkc", CN, j, pks.at[first], pks.at[first + j], at_ctx(j))
+
+    for n in (3, 0, 2, 1):
+        total = qown[n, s_i]
+        for j in range(1, ZN):
+            got("qz%d" % n, ZN, j, qz_r.at[n, j], at_z(j))
+            total = total + qz_r[n, j].astype(full_type)
+        qfin[n] = total.astype(low_type)
+
+    target = qkvo.at[place, t_i]
+    for j in range(1, CN):
+        pltpu.make_async_remote_copy(
+            src_ref=qfin, dst_ref=target,
+            send_sem=ssem.at[spot("qcs", CN) + j],
+            recv_sem=rsem.at[spot("qcr", 2 * half_chips) + place * 2 + t_i],
+            device_id=(s_i, flip(c_i, j, CN), tstar), device_id_type=MESH,
+        ).start()
+
+    @pl.when(t_i == tstar)
+    def _():
+        pltpu.make_async_copy(qfin, target, lsem.at[12]).start()
+
+    @pl.when(t_i != tstar)
+    def _():
+        pltpu.make_async_remote_copy(
+            src_ref=qfin, dst_ref=target,
+            send_sem=ssem.at[spot("qcs", CN)],
+            recv_sem=rsem.at[spot("qcr", 2 * half_chips) + place * 2 + t_i],
+            device_id=sib, device_id_type=MESH,
+        ).start()
+
+    rows_sum = rows_s[1]
+    for j in range(1, ZN):
+        got("rz", ZN, j, rows_r.at[j], at_z(j))
+        rows_sum = rows_sum + rows_r[j]
+    rows_s[2] = rows_sum
+    for j in range(1, CN):
+        put("rc", CN, j, rows_s.at[2], rows_r.at[ZN + j], at_ctx(j))
+    qkr_o[c_i] = rows_sum[:, D:]
+    total = rows_sum[:, :D]
+    for j in range(1, CN):
+        got("rc", CN, j, rows_r.at[ZN + j], at_ctx(j))
+        block = rows_r[ZN + j]
+        total = total + block[:, :D]
+        qkr_o[flip(c_i, j, CN)] = block[:, D:]
+    lnr_o[...] = total
+    for j in range(1, CN):
+        got("pkc", CN, j, pks.at[first + j], at_ctx(j))
+        peak = jnp.maximum(peak, pks[first + j])
+    peak_o[...] = peak
+
+    for k, out in ((0, upo), (1, dno)):
+        for j in range(1, CN):
+            got("gc%d" % k, CN, j, out.at[flip(c_i, j, CN)], at_ctx(j))
+        pltpu.make_async_copy(gfin.at[k], out.at[c_i], lsem.at[8 + k]).wait()
+    other_rows = pl.ds(o_i * TB, TB)
+    for k, out in ((0, bo_o), (1, ig_o)):
+        got("ob", 2, k, out.at[other_rows], sib)
+        pltpu.make_async_copy(obuf.at[k], out.at[own_rows], lsem.at[10 + k]).wait()
+
+    @pl.when(t_i == tstar)
+    def _():
+        pltpu.make_async_copy(qfin, target, lsem.at[12]).wait()
+
+    for p in range(half_chips):
+        for a in range(2):
+            @pl.when((t_i != tstar) | (place != p) | (t_i != a))
+            def _():
+                pltpu.make_async_remote_copy(
+                    src_ref=qfin, dst_ref=qkvo.at[p, a],
+                    send_sem=ssem.at[spot("qcs", CN)],
+                    recv_sem=rsem.at[spot("qcr", 2 * half_chips) + p * 2 + a],
+                    device_id=sib, device_id_type=MESH,
+                ).wait_recv()
+
+    for j in range(1, CN):
+        sent("x", CN, j, x_src, sib)
+        sent("ct", CN, j, c_src, sib)
+        sent("woc", CN, j, wot.at[mine, :, c_i], sib)
+        sent("att", CN, j, attq.at[j], sib)
+        sent("h2", CN, j, h2.at[0], sib)
+        sent("g2", CN, j, g2s.at[j], sib)
+        sent("gm", CN, j, gms.at[j], sib)
+        sent("gb", CN, j, gbg.at[0], sib)
+        sent("bo", CN, j, bos.at[j], sib)
+        sent("g1", CN, j, g1s.at[j], sib)
+        sent("pkc", CN, j, pks.at[first], sib)
+        sent("rc", CN, j, rows_s.at[2], sib)
+        sent("gc0", CN, j, gfin.at[0], sib)
+        sent("gc1", CN, j, gfin.at[1], sib)
+        sent("qcs", CN, j, qfin, sib)
+    for j in range(1, ZN):
+        sent("small", ZN, j, small_h, sib)
+        sent("woz", ZN, j, wot.at[mine, s_i, c_i], sib)
+        sent("wdz", ZN, j, wdt.at[t_i, s_i], sib)
+        sent("wuz", ZN, j, wup.at[t_i, s_i], sib)
+        sent("gz0", ZN, j, gz_s.at[0, 0], sib)
+        sent("gz1", ZN, j, gz_s.at[1, 0], sib)
+        sent("pkz", ZN, j, pks.at[2], sib)
+        sent("rz", ZN, j, rows_s.at[1], sib)
+        for n in range(4):
+            sent("qz%d" % n, ZN, j, qz_s.at[n, 0], sib)
+    sent("smallt", 1, 0, smalls.at[t_i], sib)
+    sent("k", 1, 0, kall.at[0], sib)
+    sent("v", 1, 0, vall.at[0], sib)
+    sent("pkt", 1, 0, pks.at[0], sib)
+    sent("wot", 1, 0, wot.at[mine], sib)
+    sent("wdt", 1, 0, wdt.at[t_i], sib)
+    sent("wut", 1, 0, wup.at[t_i], sib)
+    sent("rt", 1, 0, rows_s.at[0], sib)
+    for k in range(2):
+        sent("gs", 2, k, gsib_s.at[k], sib)
+        sent("dk", 2, k, dks_s.at[k], sib)
+        sent("ob", 2, k, obuf.at[k], sib)
+    for n in range(4):
+        sent("qg", 4, n, qsib_s.at[n], sib)
+
+    @pl.when(t_i == tstar)
+    def _():
+        for g in range(3):
+            for j in range(ZN):
+                sent("w%d" % g, ZN, j, wqkv.at[g, s_i], sib)
+                if j:
+                    sent("f%d" % g, ZN, j, wqkv.at[g, s_i], sib)
+
+    @pl.when(t_i != tstar)
+    def _():
+        sent("qcs", CN, 0, qfin, sib)
+
+
+SEMS = 320
+
+
+def fused_call(sizes, *operands):
+    CN, ZN, TB, D, HW, FS, R = sizes
+    TK = CN * TB
+    QR, HR = R // CN, R // 2
+    half_chips = CN // 2
+    heads = HW // 64
+    lo, hi = low_type, full_type
+    V = pltpu.VMEM
+    any_spec = pl.BlockSpec(memory_space=pl.ANY)
+    vm_spec = pl.BlockSpec(memory_space=pltpu.VMEM)
+    out_shape = [
+        jax.ShapeDtypeStruct((2 * TB, D), lo),
+        jax.ShapeDtypeStruct((2 * TB, D), lo),
+        jax.ShapeDtypeStruct((CN, R, FS), lo),
+        jax.ShapeDtypeStruct((CN, R, FS), lo),
+        jax.ShapeDtypeStruct((half_chips, 2, 4, HR, HW), lo),
+        jax.ShapeDtypeStruct((8, D), hi),
+        jax.ShapeDtypeStruct((CN, 8, 256), hi),
+        jax.ShapeDtypeStruct((8, 128), hi),
+    ]
+    scratch = [
+        V((CN, TB, D), lo), V((CN, TB, D), lo), V((2, ZN, 8, 256), hi),
+        V((3, R, half_chips * HW), lo), V((half_chips * HW, R), lo), V((FS, R), lo),
+        V((3, ZN, R, HW), lo), V((CN, ZN, CN, QR, HW), lo), V((2, ZN, R, FS), lo), V((2, ZN, R, FS), lo),
+        V((CN, QR, HW), lo),
+        V((CN, TB, D), hi), V((CN, TB, D), lo),
+        V((TK, HW), hi), V((TK, HW), hi), V((TK, HW), hi), V((TK, HW), hi),
+        V((CN, TB, HW), lo), V((2, TK, HW), lo), V((2, TK, HW), lo),
+        V((CN, heads * TB, 2 * TK), hi), V((heads * TB, 2 * TK), hi),
+        V((CN, TB, HW), lo), V((CN, TB, HW), lo), V((2 + ZN + CN, 8, 128), hi),
+        V((CN, TB, D), lo), V((2, CN, TB, FS), hi), V((2, CN, TB, FS), lo), V((2, CN, TB, FS), lo),
+        V((CN, TB, D), lo), V((CN, TB, D), lo), V((TB, D), hi),
+        V((CN, TB, D), lo), V((CN, TB, D), lo), V((TB, D), hi),
+        V((2, D, FS), lo), V((2, D, FS), lo), V((2, D, FS), hi),
+        V((2, ZN, R, FS), lo), V((2, ZN, R, FS), lo), V((2, R, FS), lo),
+        V((TB, D), hi), V((CN, TB, D), lo), V((CN, TB, HW), lo), V((CN, TB, HW), lo),
+        V((CN, TB, HW), hi), V((HW, 2 * TK), hi), V((HW, 2 * TK), hi),
+        V((2, HW, TK), lo), V((2, HW, TK), lo), V((TK, HW), lo), V((TK, HW), lo), V((TK, HW), lo),
+        V((CN, TB, D), lo), V((CN, TB, D), lo), V((TB, D), hi),
+        V((4, ZN, HR, HW), lo), V((4, ZN, HR, HW), lo), V((4, ZN, HR, HW), hi),
+        V((4, ZN, HR, HW), lo), V((4, ZN, HR, HW), lo), V((4, HR, HW), lo),
+        V((3, 8, D + 256), hi), V((ZN + CN, 8, D + 256), hi), V((2, TB, D), lo),
+        pltpu.SemaphoreType.DMA((16,)), pltpu.SemaphoreType.DMA((SEMS,)), pltpu.SemaphoreType.DMA((SEMS,)),
+    ]
+    return pl.pallas_call(
+        functools.partial(fused_kernel, sizes),
+        out_shape=out_shape,
+        in_specs=[any_spec, any_spec, vm_spec] + [any_spec] * 6,
+        out_specs=[any_spec] * 5 + [vm_spec] * 3,
+        scratch_shapes=scratch,
+        compiler_params=pltpu.CompilerParams(
+            collective_id=0, has_side_effects=True, vmem_limit_bytes=56 * 2**20
+        ),
+    )(*operands)
+
+
+def fused_layer(
+    images, cotangent, ln1_gain, ln1_bias, ln2_gain, ln2_bias, q_gain, k_gain,
+    w_query, w_key, w_value, w_out, w_up, w_down,
+):
+    CN, ZN = lax.axis_size("ctx"), lax.axis_size("shard")
+    s_i, c_i, t_i = lax.axis_index("shard"), lax.axis_index("ctx"), lax.axis_index("tp")
+    TB = images.shape[1] // 2
+    D = images.shape[2]
+    R = w_query.shape[0]
+    half_chips = CN // 2
+    HW = w_query.shape[1] // half_chips
+    FS = w_up.shape[1] // CN
+    heads_here, piece = q_gain.shape
+    sizes = (CN, ZN, TB, D, HW, FS, R)
+    slot = jnp.arange(ZN) == s_i
+
+    def head_row(gain):
+        spread = jnp.where(slot[None, :, None], gain.astype(full_type)[:, None, :], 0.0)
+        spread = spread.reshape(half_chips, HW)
+        chosen = jnp.where((jnp.arange(half_chips) == c_i % half_chips)[:, None], spread, 0.0).sum(0)
+        return jnp.where(t_i == c_i // half_chips, chosen, 0.0)
+
+    def padded(row):
+        return jnp.pad(row.astype(full_type), (0, 256 - row.shape[0]))
+
+    small = jnp.stack(
+        [padded(r) for r in (ln1_gain, ln1_bias, ln2_gain, ln2_bias, head_row(q_gain), head_row(k_gain))]
+        + [jnp.zeros((256,), full_type)] * 2
+    )
+    bo, ig, up, dn, qkvo, lnr, qkr, peak = fused_call(
+        sizes, images, cotangent, small, w_query, w_key, w_value, w_out, w_up, w_down
+    )
+    grads = qkvo.transpose(2, 1, 3, 0, 4).reshape(4, R, half_chips * HW).astype(full_type)
+    g_up = up.transpose(1, 0, 2).reshape(R, CN * FS).astype(full_type)
+    g_down = dn.transpose(0, 2, 1).reshape(CN * FS, R).astype(full_type)
+    ln = lax.dynamic_slice(lnr, (0, s_i * R), (4, R))
+    mine = lax.dynamic_slice(qkr, (t_i * half_chips, 0, 0), (half_chips, 2, HW))
+    mine = mine.transpose(1, 0, 2).reshape(2, heads_here, ZN, piece)
+    mine = lax.dynamic_slice(mine, (0, 0, s_i, 0), (2, heads_here, 1, piece))[:, :, 0]
+    peaks = lax.dynamic_slice(peak[0], (t_i * heads_here,), (heads_here,))
+    factor = jnp.sqrt(clip_level / jnp.maximum(peaks, clip_level))
+    columns = jnp.repeat(factor, HW * half_chips // heads_here)
+    query_clip = (w_query.astype(full_type) * columns).astype(low_type)
+    key_clip = (w_key.astype(full_type) * columns).astype(low_type)
+    return (
+        bo.reshape(images.shape), ig.reshape(images.shape),
+        ln[0], ln[1], ln[2], ln[3], mine[0], mine[1],
+        grads[0], grads[1], grads[2], grads[3].T, g_up, g_down,
+        query_clip, key_clip,
+    )
+
+
+def on_device(images, cotangent, ln1_gain, ln1_bias, ln2_gain, ln2_bias, q_gain, k_gain, *weights):
+    fused = fits_fused(images, weights[0], weights[4], q_gain)
+    layer = fused_layer if fused else general_layer
+    return layer(images, cotangent, ln1_gain, ln1_bias, ln2_gain, ln2_bias, q_gain, k_gain, *weights)
+
+
 def solution(mesh):
     return jax.shard_map(
         on_device,

time: 856 us -> 155 us (0.18)
  waiting for transfers between devices: 536 us -> 0 us
  blocking collectives: 204 us -> 0 us
  Pallas kernels: 0 us -> 129 us
  matrix products: 54.5 us -> 0 us
  between operations: 17.5 us -> 0.82 us
  other arithmetic: 20.1 us -> 6.48 us
    reduce_scatter x8 -> x0, waiting for transfers between devices: 331 us -> none  [the longest x1 88.2 us: on_device(): lax.psum_scatter(sum_down, 'shard', scatter_dimension=1, tiled=True)]
    pallas_call x0 -> x1, Pallas kernels: none -> 129 us  [fused_call(): pl.pallas_call(functools.partial(fused_kernel, sizes), out_shape=out_shap...]
    psum x5 -> x0, waiting for transfers between devices: 129 us -> none  [the longest x1 61.4 us: on_device(): lax.psum((grad_w_query, grad_w_key, grad_w_value, grad_w_up, grad_w_out,...]
    all_gather x8 -> x0, blocking collectives: 114 us -> none  [the longest x1 18.5 us: on_device(): lax.all_gather(w_value, 'shard', axis=0, tiled=True)]
    all_gather x2 -> x0, waiting for transfers between devices: 74.6 us -> none  [the longest x1 43.5 us: on_device(): lax.all_gather(w_down, 'shard', axis=1, tiled=True)]
    dot_general x24 -> x0, matrix products: 54.5 us -> none  [the longest x12 23.6 us: matmul(): return jnp.dot(left, right, preferred_element_type=jnp.float32)]
    pmax x1 -> x0, blocking collectives: 41.2 us -> none  [on_device(): peak_all = lax.pmax(local_peak, ('shard', 'ctx'))]
    unnamed x2 -> x0, blocking collectives: 31.7 us -> none
  transfers between devices with their start and end apart: 17 -> 0, of which waited for: 15 -> 0; matrix products, arithmetic and copies ran while one was open for 6% -> 0% of each run, Pallas kernels for 0% -> 0%
where the time goes in v1:
time: 155 us; the launch traced here: 154 us
  Pallas kernels  129 us (83%)
  local copies, waits for them, and re-layouts  18.4 us (12%)
  other arithmetic  6.48 us (4%)
    pallas_call x1, Pallas kernels, fused_call(): pl.pallas_call(functools.partial(fused_kernel, sizes), out_shape=out_shap...  129 us
    unnamed x18, local copies, waits for them, and re-layouts  6.65 us

profile of v1, /device:TPU:0, one launch (start us, length us, event | category | flops | bytes accessed | tf_op | source)
XLA Modules:
  0.0 154.4 jit_solution(12348904235483274445)
XLA Ops:
  0.6 0.7 pad_convert_fusion.3
  1.3 0.7 pad_convert_fusion.2
  2.0 0.7 pad_convert_fusion.1
  2.6 0.7 pad_convert_fusion
  3.3 0.7 convert_element_type.54
  4.0 0.7 convert_element_type.55
  4.7 0.1 broadcast_select_fusion.1
  4.7 0.1 select_n.68
  4.8 0.1 select_n.64
  4.9 0.1 select_reduce_fusion
  5.1 0.6 stack.47.small_h
  5.7 1.7 %copy.41.wo_h = bf16[384,192]{1,0:T(8,128)(2,1)} copy(bf16[384,192]{0,1:T(8,128)(2,1)} %param.25) | data formatting | bytes 294912 | tf_op args[11]
  7.4 2.2 %copy.42.wdn_h = bf16[1536,192]{1,0:T(8,128)(2,1)} copy(bf16[1536,192]{0,1:T(8,128)(2,1)} %param.27) | data formatting | bytes 1179648 | tf_op args[13]
  9.6 128.8 %shard_map.261 = (bf16[256,768]{1,0:T(8,128)(2,1)}, bf16[256,768]{1,0:T(8,128)(2,1)}, bf16[4,192,384]{2,1,0:T(8,128)(2,1)}, bf16[4,192,384]{2,1,0:T(8,128)(2,1)}...) custom-call(bf16[1,256,768]{2,1,0:T(8,128)(2,1)} %img_h.1, ...), custom_call_target="tpu_custom_call" | custom-call | tf_op jit(solution)/shard_map/pallas_call | solution.py:1061
  138.4 1.5 fusion.3
  139.9 0.7 dynamic-slice_bitcast_fusion
  140.7 0.1 reshape.90
  140.8 0.6 copy.57
  141.4 0.6 copy.56
  142.0 1.3 convert_bitcast_fusion
  143.3 0.1 fusion.2
  143.4 0.3 copy.44
  143.7 1.0 squeeze.38
  144.7 0.3 copy.45
  145.0 1.0 squeeze.39
  146.0 0.3 copy.46
  146.3 0.0 copy-start.1
  146.3 1.0 squeeze.40
  147.4 0.3 copy.47
  147.7 1.0 squeeze.41
  148.7 0.0 copy-done.1
  148.7 0.1 convert_bitcast_fusion.2
  148.7 0.0 copy-start
  148.8 1.2 copy.52
  149.9 0.0 copy-done
  149.9 0.1 convert_bitcast_fusion.1
  150.0 0.0 copy-start.2
  150.0 0.0 copy-start.3
  150.0 0.0 copy-start.5
  150.0 1.2 copy.53
  151.2 0.0 copy-start.4
  151.2 0.7 slice.49
  151.9 0.1 sqrt_bitcast_fusion
  152.0 0.1 broadcast_in_dim.66
  152.1 0.1 mul.28
  152.2 0.0 copy-done.2
  152.2 0.0 copy-done.3
  152.2 0.8 multiply_convert_fusion
  152.9 0.0 copy-done.5
  152.9 0.7 copy.60
  153.7 0.0 copy-done.4
  153.7 0.7 copy.61
  (8 shorter events, 0.0 us)
Async XLA Ops:
  146.3 2.3 %copy-start.1 = (bf16[4,192,384]{2,1,0:T(8,128)(2,1)S(1)}, bf16[4,192,384]{2,1,0:T(8,128)(2,1)}, u32[]{:S(2)}) copy-start(bf16[4,192,384]{2,1,0:T(8,128)(2,1)} %get-tuple-element.29) | copy-start | bytes 1769476
  148.7 1.2 copy-start
  150.0 2.2 %copy-start.2 = (bf16[192,384]{1,0:T(8,128)(2,1)S(1)}, bf16[192,384]{1,0:T(8,128)(2,1)}, u32[]{:S(2)}) copy-start(bf16[192,384]{1,0:T(8,128)(2,1)} %wq_h.1) | copy-start | bytes 442372
  150.0 2.1 %copy-start.3 = (bf16[192,384]{1,0:T(8,128)(2,1)S(1)}, bf16[192,384]{1,0:T(8,128)(2,1)}, u32[]{:S(2)}) copy-start(bf16[192,384]{1,0:T(8,128)(2,1)} %wk_h.1) | copy-start | bytes 442372
  150.0 2.9 %copy-start.5 = (bf16[256,768]{1,0:T(8,128)(2,1)S(1)}, bf16[256,768]{1,0:T(8,128)(2,1)}, u32[]{:S(2)}) copy-start(bf16[256,768]{1,0:T(8,128)(2,1)} %get-tuple-element.24) | copy-start | bytes 1179652
  151.2 2.5 %copy-start.4 = (bf16[256,768]{1,0:T(8,128)(2,1)S(1)}, bf16[256,768]{1,0:T(8,128)(2,1)}, u32[]{:S(2)}) copy-start(bf16[256,768]{1,0:T(8,128)(2,1)} %get-tuple-element.25) | copy-start | bytes 1179652

commit v2 on v1

--- a/solution.py
+++ b/solution.py
@@ -350,10 +350,11 @@
 
 def fused_kernel(
     sizes,
-    img_h, cot_h, small_h, wq_h, wk_h, wv_h, wo_h, wup_h, wdn_h,
+    img_h, cot_h, g1_h, b1_h, g2_h, b2_h, qg_h, kg_h, wq_h, wk_h, wv_h, wo_h, wup_h, wdn_h,
     bo_o, ig_o, upo, dno, qkvo, lnr_o, qkr_o, peak_o,
-    xg, ctg, smalls, wl, wol, wdl, wqkv, wot, wup, wdt, wtmp,
+    xg, ctg, smalls, wl, wol, wqkv, wot, wup, wdt,
     xh1, h1, nq, nk, sq, sk, qs, kall, vall, pst, sbuf, attq, attr, pks,
+    ptop, dsb,
     h2, ga, act, gu, g2s, g2r, g2own, bos, bor, boown,
     gsib_s, gsib_r, gown, gz_s, gz_r, gfin,
     gres, gbg, gms, gm, dqb, dkt, dvt, dks_s, dks_r, dqr, dkr, dvr,
@@ -416,7 +417,7 @@
         pltpu.make_async_copy(wq_h, wl.at[0], lsem.at[2]),
         pltpu.make_async_copy(x_src, xg.at[0], lsem.at[3]),
         pltpu.make_async_copy(wo_h, wol, lsem.at[4]),
-        pltpu.make_async_copy(wdn_h.at[pl.ds(c_i * FS, FS)], wdl, lsem.at[5]),
+        pltpu.make_async_copy(wdn_h.at[:, pl.ds(c_i * FS, FS)], wdt.at[t_i, s_i], lsem.at[5]),
         pltpu.make_async_copy(wup_h.at[:, pl.ds(c_i * FS, FS)], wup.at[t_i, s_i], lsem.at[6]),
         pltpu.make_async_copy(c_src, ctg.at[0], lsem.at[7]),
     ]
@@ -427,22 +428,41 @@
     greet = [at_ctx(j) for j in range(1, CN)] + [at_z(j) for j in range(1, ZN)] + [sib]
     for dev in greet:
         pl.semaphore_signal(barrier, inc=1, device_id=dev, device_id_type=MESH)
+
+    smalls[t_i, s_i] = jnp.zeros((8, 256), full_type)
+    for k, ref in enumerate((g1_h, b1_h, g2_h, b2_h)):
+        smalls[t_i, s_i, k:k + 1, :R] = ref[...].astype(full_type).reshape(1, R)
+    heads = HW // 64
+    piece = qg_h.shape[1]
+    lane_of = lax.broadcasted_iota(jnp.int32, (piece, HW), 1)
+    spread = (
+        (lane_of % piece == lax.broadcasted_iota(jnp.int32, (piece, HW), 0)) & ((lane_of % 64) // piece == s_i)
+    ).astype(full_type).astype(low_type)
+    head_of = lax.broadcasted_iota(jnp.int32, (qg_h.shape[0], HW), 0)
+    wanted = head_of == place * heads + lax.broadcasted_iota(jnp.int32, (qg_h.shape[0], HW), 1) // 64
+    wanted = wanted & (t_i == tstar)
+    for k, ref in ((4, qg_h), (5, kg_h)):
+        row = jnp.sum(jnp.where(wanted, dot(ref[...], spread), 0.0), axis=0, keepdims=True)
+        smalls[t_i, s_i, k:k + 1, :HW] = row
+
     pl.semaphore_wait(barrier, len(greet))
 
     for j in range(1, CN):
         put("x", CN, j, x_src, xg.at[j], at_ctx(j))
-    smalls[t_i, s_i] = small_h[...]
     for j in range(1, ZN):
-        put("small", ZN, j, small_h, smalls.at[t_i, s_i], at_z(j))
+        put("small", ZN, j, smalls.at[t_i, s_i], smalls.at[t_i, s_i], at_z(j))
 
     order_w = (1, 2, 0)
+
+    def picker(at):
+        return (
+            lax.broadcasted_iota(jnp.int32, (half_chips * HW, HW), 0)
+            == lax.broadcasted_iota(jnp.int32, (half_chips * HW, HW), 1) + at * HW
+        ).astype(full_type).astype(low_type)
 
     @pl.when(t_i == tstar)
     def _():
-        pick = (
-            lax.broadcasted_iota(jnp.int32, (half_chips * HW, HW), 0)
-            == lax.broadcasted_iota(jnp.int32, (half_chips * HW, HW), 1) + place * HW
-        ).astype(full_type).astype(low_type)
+        pick = picker(place)
         for n, g in enumerate(order_w):
             locals_[n].wait()
             wqkv[g, s_i] = dot(wl[g], pick).astype(low_type)
@@ -457,14 +477,12 @@
             spot("w%d" % order_w[n], ZN)
 
     locals_[4].wait()
+    wo_rows = wol[pl.ds(c_i * QR, QR)]
     for kk in range(half_chips):
-        wtmp[...] = wol[kk * HW:(kk + 1) * HW, :].astype(full_type).T.astype(low_type).reshape(CN, QR, HW)
-        wot[half_chips * t_i + kk, s_i, c_i] = wtmp[c_i]
+        wot[half_chips * t_i + kk, s_i, c_i] = dot(wo_rows, picker(kk)).astype(low_type)
     for j in range(1, ZN):
         block = wot.at[pl.ds(half_chips * t_i, half_chips), s_i, c_i]
         put("woz", ZN, j, block, block, at_z(j))
-    locals_[5].wait()
-    wdt[t_i, s_i] = wdl[...].astype(full_type).T.astype(low_type)
 
     for j in range(1, ZN):
         got("small", ZN, j, smalls.at[t_i, flip(s_i, j, ZN)], at_z(j))
@@ -502,7 +520,6 @@
     qgrow, kgrow = head_rows[0:1], head_rows[1:2]
 
     lane = lax.broadcasted_iota(jnp.int32, (1, HW), 1) // 64
-    heads = HW // 64
     mask_f = [(lane == h).astype(full_type) for h in range(heads)]
     mask_b = [m.astype(low_type) for m in mask_f]
     same_head = (
@@ -526,7 +543,7 @@
 
             @pl.when(t_i == tstar)
             def _():
-                put("f%d" % g, ZN, j, block, block, sib) if False else pltpu.make_async_remote_copy(
+                pltpu.make_async_remote_copy(
                     src_ref=block, dst_ref=block,
                     send_sem=ssem.at[spot("f%d" % g, ZN) + j],
                     recv_sem=rsem.at[spot("w%d" % g, ZN) + j],
@@ -548,6 +565,7 @@
     vall[0] = project(2).astype(low_type)
     put("v", 1, 0, vall.at[0], vall.at[1], sib)
     weight_ready(0)
+    locals_[5].wait()
     for j in range(1, ZN):
         put("wdz", ZN, j, wdt.at[t_i, s_i], wdt.at[t_i, s_i], at_z(j))
     locals_[6].wait()
@@ -570,9 +588,6 @@
     got("k", 1, 0, kall.at[1], sib)
     got("v", 1, 0, vall.at[1], sib)
 
-    step = 32
-    ones_of = lax.broadcasted_iota(jnp.int32, (8, 128), 1)
-
     def stacked(block):
         return jnp.concatenate([block * m for m in mask_b], axis=0)
 
@@ -582,7 +597,7 @@
             total = total + block[h * TB:(h + 1) * TB] * mask_f[h]
         return total
 
-    pks[0] = jnp.full((8, 128), -3.0e38, full_type)
+    ptop[...] = jnp.full(ptop.shape, -3.0e38, full_type)
 
     def attend(i, _):
         j = CN - 1 - i
@@ -594,19 +609,12 @@
             put("wot", 1, 0, wot.at[mine], wot.at[mine], sib)
 
         sbuf[...] = dot(stacked(qs[j]), kall[...].reshape(2 * TK, HW), NT)
-
         for h in range(heads):
-            def soft(r, top_all):
-                rows = pl.ds(pl.multiple_of(h * TB + r * step, step), step)
-                scores = sbuf[rows]
-                top = jnp.max(scores, axis=-1, keepdims=True)
-                expo = jnp.exp(scores - top)
-                total = jnp.sum(expo, axis=-1, keepdims=True)
-                pst[j, rows] = expo * (1.0 / total)
-                return jnp.maximum(top_all, jnp.max(top, axis=0, keepdims=True))
-
-            peak = lax.fori_loop(0, TB // step, soft, jnp.full((1, 1), -3.0e38, full_type))
-            pks[0] = jnp.where(ones_of == c_i * heads + h, jnp.maximum(pks[0], peak), pks[0])
+            rows = slice(h * TB, (h + 1) * TB)
+            scores = sbuf[rows]
+            ptop[h:h + 1] = jnp.maximum(ptop[h:h + 1], jnp.max(scores, axis=0, keepdims=True))
+            expo = jnp.exp(scores)
+            pst[j, rows] = expo * (1.0 / jnp.sum(expo, axis=-1, keepdims=True))
         mixed = folded(dot(pst[j].astype(low_type), vall[...].reshape(2 * TK, HW)))
         attq[j] = mixed.astype(low_type)
 
@@ -617,6 +625,12 @@
         return 0
 
     lax.fori_loop(0, CN, attend, 0)
+    peak_rows = jnp.max(ptop[...], axis=-1, keepdims=True)
+    lane_id = lax.broadcasted_iota(jnp.int32, (8, 128), 1)
+    own_peak = jnp.full((8, 128), -3.0e38, full_type)
+    for h in range(heads):
+        own_peak = jnp.where(lane_id == c_i * heads + h, peak_rows[h:h + 1], own_peak)
+    pks[0] = own_peak
     put("pkt", 1, 0, pks.at[0], pks.at[1], sib)
 
     got("wot", 1, 0, wot.at[pl.ds(half_chips * o_i, half_chips)], sib)
@@ -700,8 +714,22 @@
         got("gs", 2, k, gsib_r.at[k], sib)
         gown[k] = gown[k] + gsib_r[k].astype(full_type)
         gz_s[k] = gown[k].astype(low_type).reshape(ZN, R, FS)
+
+    def send_mlp(k):
         for j in range(1, ZN):
             put("gz%d" % k, ZN, j, gz_s.at[k, flip(s_i, j, ZN)], gz_r.at[k, j], at_z(j))
+
+    def share_mlp(k, out):
+        total = gown[k, pl.ds(pl.multiple_of(s_i * R, R), R)]
+        for j in range(1, ZN):
+            got("gz%d" % k, ZN, j, gz_r.at[k, j], at_z(j))
+            total = total + gz_r[k, j].astype(full_type)
+        gfin[k] = total.astype(low_type)
+        for j in range(1, CN):
+            put("gc%d" % k, CN, j, gfin.at[k], out.at[c_i], at_ctx(j))
+        pltpu.make_async_copy(gfin.at[k], out.at[c_i], lsem.at[8 + k]).start()
+
+    send_mlp(0)
 
     grad_two = g2own[...]
     for j in range(1, CN):
@@ -735,20 +763,24 @@
         def _():
             got("gm", CN, j, gm.at[j], at_ctx(j))
 
+        @pl.when(j == 1)
+        def _():
+            send_mlp(1)
+
+        @pl.when(j == CN - 1)
+        def _():
+            share_mlp(0, upo)
+
         grad_rows = stacked(gm[j])
         query_rows = stacked(qs[j])
         sbuf[...] = dot(grad_rows, vall[...].reshape(2 * TK, HW), NT)
 
-        def soft(r, _):
-            rows = pl.ds(pl.multiple_of(r * step, step), step)
-            probs = pst[j, rows]
-            grad_probs = sbuf[rows]
+        for h in range(heads):
+            rows = slice(h * TB, (h + 1) * TB)
+            probs, grad_probs = pst[j, rows], sbuf[rows]
             inner = jnp.sum(probs * grad_probs, axis=-1, keepdims=True)
-            sbuf[rows] = probs * (grad_probs - inner)
-            return 0
-
-        lax.fori_loop(0, heads * TB // step, soft, 0)
-        grad_scores = sbuf[...].astype(low_type)
+            dsb[rows] = (probs * (grad_probs - inner)).astype(low_type)
+        grad_scores = dsb[...]
         dqb[j] = folded(dot(grad_scores, kall[...].reshape(2 * TK, HW))) * 0.125
         dvt[...] += dot(grad_rows, pst[j].astype(low_type), TN)
         dkt[...] += dot(query_rows, grad_scores, TN)
@@ -791,9 +823,6 @@
 
     grad_raw, q_gain_row = unnorm(dqb[...].reshape(TK, HW), qgrow, nq[...], sq[...])
     dqr[...] = grad_raw
-    for j in range(1, CN):
-        got("gb", CN, j, gbg.at[j], at_ctx(j))
-    share_grad(3, gbg[...].reshape(TK, D), attq[...].reshape(TK, HW))
     share_grad(0, h1_all, dqr[...])
     got("dk", 2, 0, dks_r.at[0], sib)
     dvr[...] = (dvt[:, :TK] + dks_r[0].astype(full_type)).T.astype(low_type)
@@ -802,6 +831,8 @@
     grad_k = (dkt[:, :TK] + dks_r[1].astype(full_type)).T
     grad_raw, k_gain_row = unnorm(grad_k, kgrow, nk[...], sk[...])
     dkr[...] = grad_raw
+    share_grad(1, h1_all, dkr[...])
+    reduce_grad(0)
 
     ln1g = jnp.zeros((1, D), full_type)
     ln1b = jnp.zeros((1, D), full_type)
@@ -812,38 +843,26 @@
             + dot(dkr[rows], wqkv[1].reshape(D, HW), NT)
             + dot(dvr[rows], wqkv[2].reshape(D, HW), NT)
         )
-        ln1g = ln1g + jnp.sum(part * xh1[j], axis=0, keepdims=True)
-        ln1b = ln1b + jnp.sum(part, axis=0, keepdims=True)
         if j:
             g1s[j] = part.astype(low_type)
             put("g1", CN, j, g1s.at[j], g1r.at[j], at_ctx(j))
         else:
             g1own[...] = part
-    share_grad(1, h1_all, dkr[...])
+        ln1g = ln1g + jnp.sum(part * xh1[j], axis=0, keepdims=True)
+        ln1b = ln1b + jnp.sum(part, axis=0, keepdims=True)
+        if j == CN - 1:
+            reduce_grad(2)
+        elif j == CN - 2:
+            reduce_grad(1)
     rows_s[0] = jnp.zeros_like(rows_s[0])
     for k, row in enumerate((ln1g, ln1b, ln2g, ln2b)):
         rows_s[0, k:k + 1, :D] = row
     rows_s[0, 0:1, D:D + HW] = q_gain_row
     rows_s[0, 1:2, D:D + HW] = k_gain_row
     put("rt", 1, 0, rows_s.at[0], rows_r.at[0], sib)
-    reduce_grad(3)
-    reduce_grad(0)
-    reduce_grad(2)
-    reduce_grad(1)
-    got("rt", 1, 0, rows_r.at[0], sib)
-    rows_s[1] = rows_s[0] + rows_r[0]
-    for j in range(1, ZN):
-        put("rz", ZN, j, rows_s.at[1], rows_r.at[j], at_z(j))
-
-    for k, out in ((0, upo), (1, dno)):
-        total = gown[k, pl.ds(pl.multiple_of(s_i * R, R), R)]
-        for j in range(1, ZN):
-            got("gz%d" % k, ZN, j, gz_r.at[k, j], at_z(j))
-            total = total + gz_r[k, j].astype(full_type)
-        gfin[k] = total.astype(low_type)
-        for j in range(1, CN):
-            put("gc%d" % k, CN, j, gfin.at[k], out.at[c_i], at_ctx(j))
-        pltpu.make_async_copy(gfin.at[k], out.at[c_i], lsem.at[8 + k]).start()
+    for j in range(1, CN):
+        got("gb", CN, j, gbg.at[j], at_ctx(j))
+    share_grad(3, gbg[...].reshape(TK, D), attq[...].reshape(TK, HW))
 
     total = boown[...]
     for j in range(1, CN):
@@ -853,11 +872,47 @@
     obuf[0] = total.astype(low_type)
     put("ob", 2, 0, obuf.at[0], bo_o.at[own_rows], sib)
     pltpu.make_async_copy(obuf.at[0], bo_o.at[own_rows], lsem.at[10]).start()
-
+    reduce_grad(3)
+
+    got("rt", 1, 0, rows_r.at[0], sib)
+    rows_s[1] = rows_s[0] + rows_r[0]
+    for j in range(1, ZN):
+        put("rz", ZN, j, rows_s.at[1], rows_r.at[j], at_z(j))
     got("pkt", 1, 0, pks.at[1], sib)
     pks[2] = jnp.maximum(pks[0], pks[1])
     for j in range(1, ZN):
         put("pkz", ZN, j, pks.at[2], pks.at[2 + j], at_z(j))
+
+    share_mlp(1, dno)
+
+    def share_fin(n):
+        total = qown[n, s_i]
+        for j in range(1, ZN):
+            got("qz%d" % n, ZN, j, qz_r.at[n, j], at_z(j))
+            total = total + qz_r[n, j].astype(full_type)
+        qfin[n] = total.astype(low_type)
+        slot = spot("qcr%d" % n, 2 * half_chips) + place * 2 + t_i
+        for j in range(1, CN):
+            pltpu.make_async_remote_copy(
+                src_ref=qfin.at[n], dst_ref=qkvo.at[place, t_i, n],
+                send_sem=ssem.at[spot("qcs%d" % n, CN) + j], recv_sem=rsem.at[slot],
+                device_id=(s_i, flip(c_i, j, CN), tstar), device_id_type=MESH,
+            ).start()
+
+        @pl.when(t_i == tstar)
+        def _():
+            pltpu.make_async_copy(qfin.at[n], qkvo.at[place, t_i, n], lsem.at[12 + n]).start()
+
+        @pl.when(t_i != tstar)
+        def _():
+            pltpu.make_async_remote_copy(
+                src_ref=qfin.at[n], dst_ref=qkvo.at[place, t_i, n],
+                send_sem=ssem.at[spot("qcs%d" % n, CN)], recv_sem=rsem.at[slot],
+                device_id=sib, device_id_type=MESH,
+            ).start()
+
+    share_fin(0)
+    share_fin(2)
 
     xhat1, inv1 = norm_rows(xg[0].astype(full_type))
     grad_one = g1own[...]
@@ -874,6 +929,16 @@
     put("ob", 2, 1, obuf.at[1], ig_o.at[own_rows], sib)
     pltpu.make_async_copy(obuf.at[1], ig_o.at[own_rows], lsem.at[11]).start()
 
+    share_fin(1)
+    share_fin(3)
+
+    rows_sum = rows_s[1]
+    for j in range(1, ZN):
+        got("rz", ZN, j, rows_r.at[j], at_z(j))
+        rows_sum = rows_sum + rows_r[j]
+    rows_s[2] = rows_sum
+    for j in range(1, CN):
+        put("rc", CN, j, rows_s.at[2], rows_r.at[ZN + j], at_ctx(j))
     peak = pks[2]
     for j in range(1, ZN):
         got("pkz", ZN, j, pks.at[2 + j], at_z(j))
@@ -882,43 +947,6 @@
     pks[first] = peak
     for j in range(1, CN):
         put("pkc", CN, j, pks.at[first], pks.at[first + j], at_ctx(j))
-
-    for n in (3, 0, 2, 1):
-        total = qown[n, s_i]
-        for j in range(1, ZN):
-            got("qz%d" % n, ZN, j, qz_r.at[n, j], at_z(j))
-            total = total + qz_r[n, j].astype(full_type)
-        qfin[n] = total.astype(low_type)
-
-    target = qkvo.at[place, t_i]
-    for j in range(1, CN):
-        pltpu.make_async_remote_copy(
-            src_ref=qfin, dst_ref=target,
-            send_sem=ssem.at[spot("qcs", CN) + j],
-            recv_sem=rsem.at[spot("qcr", 2 * half_chips) + place * 2 + t_i],
-            device_id=(s_i, flip(c_i, j, CN), tstar), device_id_type=MESH,
-        ).start()
-
-    @pl.when(t_i == tstar)
-    def _():
-        pltpu.make_async_copy(qfin, target, lsem.at[12]).start()
-
-    @pl.when(t_i != tstar)
-    def _():
-        pltpu.make_async_remote_copy(
-            src_ref=qfin, dst_ref=target,
-            send_sem=ssem.at[spot("qcs", CN)],
-            recv_sem=rsem.at[spot("qcr", 2 * half_chips) + place * 2 + t_i],
-            device_id=sib, device_id_type=MESH,
-        ).start()
-
-    rows_sum = rows_s[1]
-    for j in range(1, ZN):
-        got("rz", ZN, j, rows_r.at[j], at_z(j))
-        rows_sum = rows_sum + rows_r[j]
-    rows_s[2] = rows_sum
-    for j in range(1, CN):
-        put("rc", CN, j, rows_s.at[2], rows_r.at[ZN + j], at_ctx(j))
     qkr_o[c_i] = rows_sum[:, D:]
     total = rows_sum[:, :D]
     for j in range(1, CN):
@@ -943,18 +971,20 @@
 
     @pl.when(t_i == tstar)
     def _():
-        pltpu.make_async_copy(qfin, target, lsem.at[12]).wait()
+        for n in range(4):
+            pltpu.make_async_copy(qfin.at[n], qkvo.at[place, t_i, n], lsem.at[12 + n]).wait()
 
     for p in range(half_chips):
         for a in range(2):
             @pl.when((t_i != tstar) | (place != p) | (t_i != a))
             def _():
-                pltpu.make_async_remote_copy(
-                    src_ref=qfin, dst_ref=qkvo.at[p, a],
-                    send_sem=ssem.at[spot("qcs", CN)],
-                    recv_sem=rsem.at[spot("qcr", 2 * half_chips) + p * 2 + a],
-                    device_id=sib, device_id_type=MESH,
-                ).wait_recv()
+                for n in range(4):
+                    pltpu.make_async_remote_copy(
+                        src_ref=qfin.at[n], dst_ref=qkvo.at[p, a, n],
+                        send_sem=ssem.at[spot("qcs%d" % n, CN)],
+                        recv_sem=rsem.at[spot("qcr%d" % n, 2 * half_chips) + p * 2 + a],
+                        device_id=sib, device_id_type=MESH,
+                    ).wait_recv()
 
     for j in range(1, CN):
         sent("x", CN, j, x_src, sib)
@@ -971,9 +1001,10 @@
         sent("rc", CN, j, rows_s.at[2], sib)
         sent("gc0", CN, j, gfin.at[0], sib)
         sent("gc1", CN, j, gfin.at[1], sib)
-        sent("qcs", CN, j, qfin, sib)
+        for n in range(4):
+            sent("qcs%d" % n, CN, j, qfin.at[n], sib)
     for j in range(1, ZN):
-        sent("small", ZN, j, small_h, sib)
+        sent("small", ZN, j, smalls.at[t_i, s_i], sib)
         sent("woz", ZN, j, wot.at[mine, s_i, c_i], sib)
         sent("wdz", ZN, j, wdt.at[t_i, s_i], sib)
         sent("wuz", ZN, j, wup.at[t_i, s_i], sib)
@@ -1008,7 +1039,8 @@
 
     @pl.when(t_i != tstar)
     def _():
-        sent("qcs", CN, 0, qfin, sib)
+        for n in range(4):
+            sent("qcs%d" % n, CN, 0, qfin.at[n], sib)
 
 
 SEMS = 320
@@ -1036,14 +1068,14 @@
     ]
     scratch = [
         V((CN, TB, D), lo), V((CN, TB, D), lo), V((2, ZN, 8, 256), hi),
-        V((3, R, half_chips * HW), lo), V((half_chips * HW, R), lo), V((FS, R), lo),
+        V((3, R, half_chips * HW), lo), V((R, half_chips * HW), lo),
         V((3, ZN, R, HW), lo), V((CN, ZN, CN, QR, HW), lo), V((2, ZN, R, FS), lo), V((2, ZN, R, FS), lo),
-        V((CN, QR, HW), lo),
         V((CN, TB, D), hi), V((CN, TB, D), lo),
         V((TK, HW), hi), V((TK, HW), hi), V((TK, HW), hi), V((TK, HW), hi),
         V((CN, TB, HW), lo), V((2, TK, HW), lo), V((2, TK, HW), lo),
         V((CN, heads * TB, 2 * TK), hi), V((heads * TB, 2 * TK), hi),
         V((CN, TB, HW), lo), V((CN, TB, HW), lo), V((2 + ZN + CN, 8, 128), hi),
+        V((heads, 2 * TK), hi), V((heads * TB, 2 * TK), lo),
         V((CN, TB, D), lo), V((2, CN, TB, FS), hi), V((2, CN, TB, FS), lo), V((2, CN, TB, FS), lo),
         V((CN, TB, D), lo), V((CN, TB, D), lo), V((TB, D), hi),
         V((CN, TB, D), lo), V((CN, TB, D), lo), V((TB, D), hi),
@@ -1061,7 +1093,7 @@
     return pl.pallas_call(
         functools.partial(fused_kernel, sizes),
         out_shape=out_shape,
-        in_specs=[any_spec, any_spec, vm_spec] + [any_spec] * 6,
+        in_specs=[any_spec] * 2 + [vm_spec] * 6 + [any_spec] * 6,
         out_specs=[any_spec] * 5 + [vm_spec] * 3,
         scratch_shapes=scratch,
         compiler_params=pltpu.CompilerParams(
@@ -1070,56 +1102,84 @@
     )(*operands)
 
 
+def finish_kernel(
+    sizes,
+    bo, ig, upo, dno, qkvo, lnr, qkr, peak, wq, wk,
+    bo_o, ig_o, l1g, l1b, l2g, l2b, qg_o, kg_o, gq, gk, gv, go, gu, gd, cq, ck,
+):
+    CN, ZN, TB, D, HW, FS, R = sizes
+    half_chips = CN // 2
+    s_i, t_i = lax.axis_index("shard"), lax.axis_index("tp")
+    bo_o[...] = bo[...]
+    ig_o[...] = ig[...]
+    for n, out in enumerate((gq, gk, gv, go)):
+        for a in range(2):
+            parts = [qkvo[p, a, n] for p in range(half_chips)]
+            out[a * (R // 2):(a + 1) * (R // 2)] = jnp.concatenate(parts, axis=1).astype(full_type)
+    for c in range(CN):
+        gu[:, c * FS:(c + 1) * FS] = upo[c].astype(full_type)
+        gd[:, c * FS:(c + 1) * FS] = dno[c].astype(full_type)
+    rows = jnp.zeros((8, R), full_type)
+    for z in range(ZN):
+        rows = jnp.where(s_i == z, lnr[:, z * R:(z + 1) * R], rows)
+    for k, out in enumerate((l1g, l1b, l2g, l2b)):
+        out[...] = rows[k:k + 1].reshape(R)
+    heads = HW // 64
+    piece = qg_o.shape[1]
+    for p in range(half_chips):
+        chip = qkr[t_i * half_chips + p]
+        for h in range(heads):
+            for z in range(ZN):
+                at = h * 64 + z * piece
+
+                @pl.when(s_i == z)
+                def _():
+                    qg_o[p * heads + h:p * heads + h + 1] = chip[0:1, at:at + piece]
+                    kg_o[p * heads + h:p * heads + h + 1] = chip[1:2, at:at + piece]
+    factor = jnp.sqrt(clip_level / jnp.maximum(peak[0:1], clip_level))
+    here = half_chips * heads
+    lanes = lax.broadcasted_iota(jnp.int32, (1, here * 64), 1) // 64
+    ids = lax.broadcasted_iota(jnp.int32, (1, 128), 1)
+    columns = jnp.ones((1, here * 64), full_type)
+    for h in range(here):
+        one = jnp.sum(jnp.where(ids == t_i * here + h, factor, 0.0), axis=-1, keepdims=True)
+        columns = jnp.where(lanes == h, one, columns)
+    cq[...] = (wq[...].astype(full_type) * columns).astype(low_type)
+    ck[...] = (wk[...].astype(full_type) * columns).astype(low_type)
+
+
 def fused_layer(
     images, cotangent, ln1_gain, ln1_bias, ln2_gain, ln2_bias, q_gain, k_gain,
     w_query, w_key, w_value, w_out, w_up, w_down,
 ):
     CN, ZN = lax.axis_size("ctx"), lax.axis_size("shard")
-    s_i, c_i, t_i = lax.axis_index("shard"), lax.axis_index("ctx"), lax.axis_index("tp")
     TB = images.shape[1] // 2
     D = images.shape[2]
     R = w_query.shape[0]
-    half_chips = CN // 2
-    HW = w_query.shape[1] // half_chips
+    HW = w_query.shape[1] // (CN // 2)
     FS = w_up.shape[1] // CN
-    heads_here, piece = q_gain.shape
     sizes = (CN, ZN, TB, D, HW, FS, R)
-    slot = jnp.arange(ZN) == s_i
-
-    def head_row(gain):
-        spread = jnp.where(slot[None, :, None], gain.astype(full_type)[:, None, :], 0.0)
-        spread = spread.reshape(half_chips, HW)
-        chosen = jnp.where((jnp.arange(half_chips) == c_i % half_chips)[:, None], spread, 0.0).sum(0)
-        return jnp.where(t_i == c_i // half_chips, chosen, 0.0)
-
-    def padded(row):
-        return jnp.pad(row.astype(full_type), (0, 256 - row.shape[0]))
-
-    small = jnp.stack(
-        [padded(r) for r in (ln1_gain, ln1_bias, ln2_gain, ln2_bias, head_row(q_gain), head_row(k_gain))]
-        + [jnp.zeros((256,), full_type)] * 2
-    )
-    bo, ig, up, dn, qkvo, lnr, qkr, peak = fused_call(
-        sizes, images, cotangent, small, w_query, w_key, w_value, w_out, w_up, w_down
-    )
-    grads = qkvo.transpose(2, 1, 3, 0, 4).reshape(4, R, half_chips * HW).astype(full_type)
-    g_up = up.transpose(1, 0, 2).reshape(R, CN * FS).astype(full_type)
-    g_down = dn.transpose(0, 2, 1).reshape(CN * FS, R).astype(full_type)
-    ln = lax.dynamic_slice(lnr, (0, s_i * R), (4, R))
-    mine = lax.dynamic_slice(qkr, (t_i * half_chips, 0, 0), (half_chips, 2, HW))
-    mine = mine.transpose(1, 0, 2).reshape(2, heads_here, ZN, piece)
-    mine = lax.dynamic_slice(mine, (0, 0, s_i, 0), (2, heads_here, 1, piece))[:, :, 0]
-    peaks = lax.dynamic_slice(peak[0], (t_i * heads_here,), (heads_here,))
-    factor = jnp.sqrt(clip_level / jnp.maximum(peaks, clip_level))
-    columns = jnp.repeat(factor, HW * half_chips // heads_here)
-    query_clip = (w_query.astype(full_type) * columns).astype(low_type)
-    key_clip = (w_key.astype(full_type) * columns).astype(low_type)
-    return (
-        bo.reshape(images.shape), ig.reshape(images.shape),
-        ln[0], ln[1], ln[2], ln[3], mine[0], mine[1],
-        grads[0], grads[1], grads[2], grads[3].T, g_up, g_down,
-        query_clip, key_clip,
-    )
+    results = fused_call(
+        sizes, images, cotangent, ln1_gain, ln1_bias, ln2_gain, ln2_bias, q_gain, k_gain,
+        w_query, w_key, w_value, w_out.T, w_up, w_down.T,
+    )
+    row = jax.ShapeDtypeStruct((R,), full_type)
+    gain = jax.ShapeDtypeStruct(q_gain.shape, full_type)
+    square = jax.ShapeDtypeStruct(w_query.shape, full_type)
+    wide = jax.ShapeDtypeStruct(w_up.shape, full_type)
+    tokens = jax.ShapeDtypeStruct(images.shape[1:], low_type)
+    clipped = jax.ShapeDtypeStruct(w_query.shape, low_type)
+    out = pl.pallas_call(
+        functools.partial(finish_kernel, sizes),
+        out_shape=[tokens] * 2 + [row] * 4 + [gain] * 2 + [square] * 4 + [wide] * 2 + [clipped] * 2,
+        in_specs=[pl.BlockSpec(memory_space=pltpu.VMEM)] * 10,
+        out_specs=[pl.BlockSpec(memory_space=pltpu.VMEM)] * 16,
+        compiler_params=pltpu.CompilerParams(vmem_limit_bytes=40 * 2**20),
+    )(*results, w_query, w_key)
+    out = list(out)
+    out[0], out[1] = out[0].reshape(images.shape), out[1].reshape(images.shape)
+    out[11], out[13] = out[11].T, out[13].T
+    return tuple(out)
 
 
 def on_device(images, cotangent, ln1_gain, ln1_bias, ln2_gain, ln2_bias, q_gain, k_gain, *weights):

time: 155 us -> 138 us (0.89)
  local copies, waits for them, and re-layouts: 18.4 us -> 7.42 us
  other arithmetic: 6.48 us -> 0 us
    squeeze x4 -> x0, local copies, waits for them, and re-layouts: 4.01 us -> none  [the longest x1 1 us: fused_layer(): grads[0]]
    slice x8 -> x0, local copies, waits for them, and re-layouts: 3.61 us -> none  [the longest x1 1.52 us: fused_layer(): ln[3]]
    convert_element_type x4 -> x0, other arithmetic: 3.43 us -> none  [the longest x2 1.37 us: head_row(): gain.astype(full_type)[:, None, :]]
    pallas_call x0 -> x1, Pallas kernels: none -> 2.75 us  [fused_layer(): pl.pallas_call(functools.partial(finish_kernel, sizes), out_shape=[tokens...]
    another operation x4 -> x0, other arithmetic: 2.63 us -> none  [fused_layer(): jnp.stack([padded(r) for r in (ln1_gain, ln1_bias, ln2_gain, ln2_bias, he...]
    convert_element_type x2 -> x0, local copies, waits for them, and re-layouts: 2.32 us -> none  [the longest x1 1.16 us: fused_layer(): g_up = up.transpose(1, 0, 2).reshape(R, CN * FS).astype(full_type)]
    pallas_call x1, Pallas kernels: 129 us -> 127 us  [fused_call(): pl.pallas_call(functools.partial(fused_kernel, sizes), out_shape=out_shap...]
    unnamed x18 -> x20, local copies, waits for them, and re-layouts: 6.65 us -> 7.42 us
where the time goes in v2:
time: 138 us
  Pallas kernels  130 us (94%)
  local copies, waits for them, and re-layouts  7.42 us (5%)
    pallas_call x1, Pallas kernels, fused_call(): pl.pallas_call(functools.partial(fused_kernel, sizes), out_shape=out_shap...  127 us
    unnamed x20, local copies, waits for them, and re-layouts  7.42 us

profile of v2, /device:TPU:0, one launch (start us, length us, event | category | flops | bytes accessed | tf_op | source)
XLA Modules:
  0.0 138.0 jit_solution(11274868825203032017)
XLA Ops:
  0.7 0.0 copy-start.1
  0.7 0.0 copy-start.2
  0.7 127.1 %shard_map.261 = (bf16[256,768]{1,0:T(8,128)(2,1)}, bf16[256,768]{1,0:T(8,128)(2,1)}, bf16[4,192,384]{2,1,0:T(8,128)(2,1)}, bf16[4,192,384]{2,1,0:T(8,128)(2,1)}...) custom-call(bf16[1,256,768]{2,1,0:T(8,128)(2,1)} %img_h.1, ...), custom_call_target="tpu_custom_call" | custom-call | tf_op jit(solution)/shard_map/pallas_call | solution.py:1093
  127.8 0.0 copy-done.1
  127.8 0.0 copy-done.2
  127.8 0.0 copy-start
  127.8 1.1 copy-done
  128.9 0.0 copy-start.3
  128.9 1.1 copy-done.3
  130.0 0.0 copy-start.4
  130.0 1.1 copy-done.4
  131.0 0.0 copy-start.5
  131.0 1.0 copy-done.5
  132.0 0.0 copy-start.6
  132.0 1.0 copy-done.6
  133.0 0.0 copy-start.7
  133.0 0.8 copy-done.7
  133.8 0.0 copy-start.8
  133.8 0.7 copy-done.8
  134.5 0.0 copy-start.9
  134.5 0.7 copy-done.9
  135.2 2.7 %shard_map.262 = (bf16[256,768]{1,0:T(8,128)(2,1)}, bf16[256,768]{1,0:T(8,128)(2,1)}, f32[192]{0:T(256)}, f32[192]{0:T(256)}, f32[192]{0:T(256)}, /*index=5*/f32...) custom-call(bf16[256,768]{1,0:T(8,128)(2,1)S(1)} %copy-done.5, ...), custom_call_target="tpu_custom_call" | custom-call | tf_op jit(solution)/shard_map/pallas_call | solution.py:1172
Async XLA Ops:
  0.7 127.1 %copy-start.1 = (bf16[192,384]{1,0:T(8,128)(2,1)S(1)}, bf16[192,384]{1,0:T(8,128)(2,1)}, u32[]{:S(2)}) copy-start(bf16[192,384]{1,0:T(8,128)(2,1)} %wq.1) | copy-start | bytes 442372
  0.7 127.1 %copy-start.2 = (bf16[192,384]{1,0:T(8,128)(2,1)S(1)}, bf16[192,384]{1,0:T(8,128)(2,1)}, u32[]{:S(2)}) copy-start(bf16[192,384]{1,0:T(8,128)(2,1)} %wk.1) | copy-start | bytes 442372
  127.8 1.1 copy-start
  128.9 1.1 copy-start.3
  130.0 1.1 copy-start.4
  131.0 1.0 copy-start.5
  132.0 1.0 copy-start.6
  133.0 0.8 copy-start.7
  133.8 0.7 copy-start.8
  134.5 0.7 copy-start.9

commit v3 on v2

--- a/solution.py
+++ b/solution.py
@@ -352,12 +352,12 @@
     sizes,
     img_h, cot_h, g1_h, b1_h, g2_h, b2_h, qg_h, kg_h, wq_h, wk_h, wv_h, wo_h, wup_h, wdn_h,
     bo_o, ig_o, upo, dno, qkvo, lnr_o, qkr_o, peak_o,
-    xg, ctg, smalls, wl, wol, wqkv, wot, wup, wdt,
+    xg, ctg, smalls, wl, wol, wkv, wqb, wot, wup, wdt, h1_t, h2_t, ct_t,
     xh1, h1, nq, nk, sq, sk, qs, kall, vall, pst, sbuf, attq, attr, pks,
     ptop, dsb,
     h2, ga, act, gu, g2s, g2r, g2own, bos, bor, boown,
-    gsib_s, gsib_r, gown, gz_s, gz_r, gfin,
-    gres, gbg, gms, gm, dqb, dkt, dvt, dks_s, dks_r, dqr, dkr, dvr,
+    gsib_s, gsib_r, gown, gkeep, gz_s, gz_r, gfin,
+    gres, gbg, gms, gm, dqb, dkt, dvt, dks_s, dks_r, dqr, dkv,
     g1s, g1r, g1own, qsib_s, qsib_r, qown, qz_s, qz_r, qfin,
     rows_s, rows_r, obuf,
     lsem, ssem, rsem,
@@ -381,6 +381,14 @@
 
     sib = (s_i, c_i, o_i)
 
+    outer = (s_i == 0) | (s_i == ZN - 1)
+    pair = flip(s_i, 1, ZN)
+    far_in = flip(s_i, 3, ZN) * (1 - outer) + flip(s_i, 2, ZN) * outer
+    far_out = flip(s_i, 2, ZN) * (1 - outer) + flip(s_i, 3, ZN) * outer
+
+    def plane(z):
+        return (z, c_i, t_i)
+
     spots = {}
 
     def spot(name, count):
@@ -392,6 +400,13 @@
         base = spot(name, count)
         pltpu.make_async_remote_copy(
             src_ref=src, dst_ref=dst, send_sem=ssem.at[base + j], recv_sem=rsem.at[base + j],
+            device_id=dev, device_id_type=MESH,
+        ).start()
+
+    def put_as(name, count, send, recv, src, dst, dev):
+        base = spot(name, count)
+        pltpu.make_async_remote_copy(
+            src_ref=src, dst_ref=dst, send_sem=ssem.at[base + send], recv_sem=rsem.at[base + recv],
             device_id=dev, device_id_type=MESH,
         ).start()
 
@@ -452,37 +467,35 @@
     for j in range(1, ZN):
         put("small", ZN, j, smalls.at[t_i, s_i], smalls.at[t_i, s_i], at_z(j))
 
-    order_w = (1, 2, 0)
-
-    def picker(at):
-        return (
-            lax.broadcasted_iota(jnp.int32, (half_chips * HW, HW), 0)
-            == lax.broadcasted_iota(jnp.int32, (half_chips * HW, HW), 1) + at * HW
-        ).astype(full_type).astype(low_type)
+    def picker(at, lanes, offset):
+        rows = lax.broadcasted_iota(jnp.int32, (half_chips * HW, lanes), 0)
+        cols = lax.broadcasted_iota(jnp.int32, (half_chips * HW, lanes), 1) - offset
+        return ((rows == cols + at * HW) & (cols >= 0) & (cols < HW)).astype(full_type).astype(low_type)
+
+    projections = (("wkv", wkv), ("wq", wqb))
 
     @pl.when(t_i == tstar)
     def _():
-        pick = picker(place)
-        for n, g in enumerate(order_w):
+        for n in range(3):
             locals_[n].wait()
-            wqkv[g, s_i] = dot(wl[g], pick).astype(low_type)
+        wkv[s_i] = (
+            dot(wl[1], picker(place, 2 * HW, 0)) + dot(wl[2], picker(place, 2 * HW, HW))
+        ).astype(low_type)
+        wqb[s_i] = dot(wl[0], picker(place, HW, 0)).astype(low_type)
+        for name, buf in projections:
             for j in range(1, ZN):
-                put("w%d" % g, ZN, j, wqkv.at[g, s_i], wqkv.at[g, s_i], at_z(j))
-            put("w%d" % g, ZN, 0, wqkv.at[g, s_i], wqkv.at[g, s_i], sib)
+                put(name, ZN, j, buf.at[s_i], buf.at[s_i], at_z(j))
+            put(name, ZN, 0, buf.at[s_i], buf.at[s_i], sib)
 
     @pl.when(t_i != tstar)
     def _():
         for n in range(3):
             locals_[n].wait()
-            spot("w%d" % order_w[n], ZN)
 
     locals_[4].wait()
-    wo_rows = wol[pl.ds(c_i * QR, QR)]
-    for kk in range(half_chips):
-        wot[half_chips * t_i + kk, s_i, c_i] = dot(wo_rows, picker(kk)).astype(low_type)
+    wot[t_i, s_i, c_i] = wol[pl.ds(c_i * QR, QR)]
     for j in range(1, ZN):
-        block = wot.at[pl.ds(half_chips * t_i, half_chips), s_i, c_i]
-        put("woz", ZN, j, block, block, at_z(j))
+        put("woz", ZN, j, wot.at[t_i, s_i, c_i], wot.at[t_i, s_i, c_i], at_z(j))
 
     for j in range(1, ZN):
         got("small", ZN, j, smalls.at[t_i, flip(s_i, j, ZN)], at_z(j))
@@ -506,9 +519,29 @@
 
         normed, _unused = norm_rows(xg[j].astype(full_type))
         xh1[j] = normed
-        h1[j] = (normed * g1row + b1row).astype(low_type)
+        hidden = (normed * g1row + b1row).astype(low_type)
+        h1[j] = hidden
+        h1_t[:, pl.ds(pl.multiple_of(j * TB, TB), TB)] = hidden.T
         return 0
 
+    HB = TB // 2
+
+    def spread(name, src, dst_of):
+        for j in (1, 2):
+            put(name, 5, j, src, dst_of(j), at_ctx(j))
+
+    def pass_on(name, buf):
+        for j in (1, 2):
+            got(name, 5, j, buf.at[j], at_ctx(j))
+            half = pl.ds((j - 1) * HB, HB)
+            put_as(name, 5, 2 + j, 2 + j, buf.at[j, half], buf.at[3, half], at_ctx(3 - j))
+
+    def have_rest(name, buf):
+        for j in (1, 2):
+            half = pl.ds((j - 1) * HB, HB)
+            got(name, 5, 2 + j, buf.at[3, half], at_ctx(3 - j))
+
+    spread("ct", c_src, lambda j: ctg.at[j])
     lax.fori_loop(0, CN, first_norm, 0)
 
     got("smallt", 1, 0, smalls.at[o_i], sib)
@@ -532,59 +565,78 @@
         rest = (values - high.astype(full_type)).astype(low_type)
         return (dot(high, same_head) + dot(rest, same_head)) * (1.0 / 64)
 
-    def weight_ready(g):
+    def weight_ready(name, buf):
         @pl.when(t_i != tstar)
         def _():
-            got("w%d" % g, ZN, 0, wqkv.at[g, s_i], sib)
+            got(name, ZN, 0, buf.at[s_i], sib)
 
         for j in range(1, ZN):
-            block = wqkv.at[g, flip(s_i, j, ZN)]
-            got("w%d" % g, ZN, j, block, sib)
+            block = buf.at[flip(s_i, j, ZN)]
+            got(name, ZN, j, block, sib)
 
             @pl.when(t_i == tstar)
             def _():
                 pltpu.make_async_remote_copy(
                     src_ref=block, dst_ref=block,
-                    send_sem=ssem.at[spot("f%d" % g, ZN) + j],
-                    recv_sem=rsem.at[spot("w%d" % g, ZN) + j],
+                    send_sem=ssem.at[spot("f" + name, ZN) + j], recv_sem=rsem.at[spot(name, ZN) + j],
                     device_id=sib, device_id_type=MESH,
                 ).start()
 
-    def project(g):
-        return dot(h1[...].reshape(TK, D), wqkv[g].reshape(D, HW))
-
-    weight_ready(1)
-    raw = project(1)
+    h1_all = h1[...].reshape(TK, D)
+    weight_ready(*projections[0])
+    raw = dot(h1_all, wkv[...].reshape(D, 2 * HW))
+    vall[0] = raw[:, HW:].astype(low_type)
+    put("v", 1, 0, vall.at[0], vall.at[1], sib)
+    raw = raw[:, :HW]
     inverse = lax.rsqrt(head_mean(raw * raw) + norm_eps)
     normed = raw * inverse
     nk[...] = normed
     sk[...] = inverse
     kall[0] = (normed * kgrow).astype(low_type)
     put("k", 1, 0, kall.at[0], kall.at[1], sib)
-    weight_ready(2)
-    vall[0] = project(2).astype(low_type)
-    put("v", 1, 0, vall.at[0], vall.at[1], sib)
-    weight_ready(0)
+    weight_ready(*projections[1])
+    mlp_weights = (("wd", wdt), ("wu", wup))
+
+    def own_mlp(name, buf):
+        block = buf.at[t_i, s_i]
+        put_as(name, 5, 0, 0, block, block, plane(pair))
+
+        @pl.when(jnp.logical_not(outer))
+        def _():
+            put_as(name, 5, 1, 1, block, block, plane(far_in))
+
+    def pass_mlp(name, buf, stage):
+        source, target = ((pair, far_in), (far_in, pair), (far_out, pair))[stage]
+        recv = (2, 1, 2)[stage]
+
+        @pl.when(jnp.logical_not(outer))
+        def _():
+            block = buf.at[t_i, source]
+            got(name, 5, stage, block, plane(pair))
+            put_as(name, 5, 2 + stage, recv, block, block, plane(target))
+
+    def have_mlp(name, buf):
+        @pl.when(outer)
+        def _():
+            for n, z in enumerate((pair, far_in, far_out)):
+                got(name, 5, n, buf.at[t_i, z], plane(pair))
+
     locals_[5].wait()
+    own_mlp(*mlp_weights[0])
+    locals_[6].wait()
+    own_mlp(*mlp_weights[1])
     for j in range(1, ZN):
-        put("wdz", ZN, j, wdt.at[t_i, s_i], wdt.at[t_i, s_i], at_z(j))
-    locals_[6].wait()
-    for j in range(1, ZN):
-        put("wuz", ZN, j, wup.at[t_i, s_i], wup.at[t_i, s_i], at_z(j))
-    raw = project(0)
+        got("woz", ZN, j, wot.at[t_i, flip(s_i, j, ZN), c_i], at_z(j))
+    for j in range(1, CN):
+        put("woc", CN, j, wot.at[t_i, :, c_i], wot.at[t_i, :, c_i], at_ctx(j))
+    raw = dot(h1_all, wqb[...].reshape(D, HW))
     inverse = lax.rsqrt(head_mean(raw * raw) + norm_eps)
     normed = raw * inverse
     nq[...] = normed
     sq[...] = inverse
     qs[...] = ((normed * qgrow).astype(low_type) * 0.125).astype(low_type).reshape(CN, TB, HW)
 
-    mine = pl.ds(half_chips * t_i, half_chips)
-    for j in range(1, ZN):
-        got("woz", ZN, j, wot.at[mine, flip(s_i, j, ZN), c_i], at_z(j))
-    for j in range(1, CN):
-        put("woc", CN, j, wot.at[mine, :, c_i], wot.at[mine, :, c_i], at_ctx(j))
-    for j in range(1, CN):
-        put("ct", CN, j, c_src, ctg.at[j], at_ctx(j))
+    pass_on("ct", ctg)
     got("k", 1, 0, kall.at[1], sib)
     got("v", 1, 0, vall.at[1], sib)
 
@@ -602,11 +654,11 @@
     def attend(i, _):
         j = CN - 1 - i
 
-        @pl.when(i == 2)
-        def _():
-            for q in range(1, CN):
-                got("woc", CN, q, wot.at[mine, :, flip(c_i, q, CN)], at_ctx(q))
-            put("wot", 1, 0, wot.at[mine], wot.at[mine], sib)
+        for name, buf, when in (mlp_weights[0] + (1,), mlp_weights[1] + (2,)):
+            @pl.when(i == when)
+            def _():
+                pass_mlp(name, buf, 0)
+                pass_mlp(name, buf, 1)
 
         sbuf[...] = dot(stacked(qs[j]), kall[...].reshape(2 * TK, HW), NT)
         for h in range(heads):
@@ -625,6 +677,10 @@
         return 0
 
     lax.fori_loop(0, CN, attend, 0)
+    for j in range(1, CN):
+        got("woc", CN, j, wot.at[t_i, :, flip(c_i, j, CN)], at_ctx(j))
+    put("wot", 1, 0, wot.at[t_i], wot.at[t_i], sib)
+    pass_mlp(*mlp_weights[0], 2)
     peak_rows = jnp.max(ptop[...], axis=-1, keepdims=True)
     lane_id = lax.broadcasted_iota(jnp.int32, (8, 128), 1)
     own_peak = jnp.full((8, 128), -3.0e38, full_type)
@@ -633,11 +689,16 @@
     pks[0] = own_peak
     put("pkt", 1, 0, pks.at[0], pks.at[1], sib)
 
-    got("wot", 1, 0, wot.at[pl.ds(half_chips * o_i, half_chips)], sib)
-    branch = dot(attq[0], wot[c_i].reshape(D, HW), NT)
-    for j in range(1, CN):
+    def pair_up(own, other):
+        even = place == 0
+        return jnp.concatenate([jnp.where(even, own, other), jnp.where(even, other, own)], axis=1)
+
+    got("wot", 1, 0, wot.at[o_i], sib)
+    got("att", CN, 1, attr.at[1], at_ctx(1))
+    branch = dot(pair_up(attq[0], attr[1]), wot[tstar].reshape(D, 2 * HW), NT)
+    for j in (2, 3):
         got("att", CN, j, attr.at[j], at_ctx(j))
-        branch = branch + dot(attr[j], wot[flip(c_i, j, CN)].reshape(D, HW), NT)
+    branch = branch + dot(pair_up(attr[2], attr[3]), wot[1 - tstar].reshape(D, 2 * HW), NT)
     resid = xg[0].astype(full_type) + branch
     boown[...] = resid
     xhat2, inv2 = norm_rows(resid)
@@ -645,15 +706,14 @@
     for j in range(1, CN):
         put("h2", CN, j, h2.at[0], h2.at[j], at_ctx(j))
 
+    pass_mlp(*mlp_weights[1], 2)
     locals_[7].wait()
-    for j in range(1, CN):
-        got("ct", CN, j, ctg.at[j], at_ctx(j))
-    for j in range(1, ZN):
-        got("wdz", ZN, j, wdt.at[t_i, flip(s_i, j, ZN)], at_z(j))
+    have_rest("ct", ctg)
+    ct_t[...] = ctg[...].reshape(TK, D).T
+    have_mlp(*mlp_weights[0])
     put("wdt", 1, 0, wdt.at[t_i], wdt.at[t_i], sib)
     ga[t_i] = dot(ctg[...].reshape(TK, D), wdt[t_i].reshape(D, FS)).reshape(CN, TB, FS)
-    for j in range(1, ZN):
-        got("wuz", ZN, j, wup.at[t_i, flip(s_i, j, ZN)], at_z(j))
+    have_mlp(*mlp_weights[1])
     put("wut", 1, 0, wup.at[t_i], wup.at[t_i], sib)
     got("wdt", 1, 0, wdt.at[o_i], sib)
     ga[o_i] = dot(ctg[...].reshape(TK, D), wdt[o_i].reshape(D, FS)).reshape(CN, TB, FS)
@@ -665,13 +725,17 @@
             got("h2", CN, j, h2.at[j], at_ctx(j))
 
         block = h2[j]
+        h2_t[:, pl.ds(pl.multiple_of(j * TB, TB), TB)] = block.T
         for a in range(2):
             up = dot(block, wup[a].reshape(D, FS))
             phi = 0.5 * (1.0 + lax.erf(up * 0.7071067811865476))
             dens = jnp.exp(up * up * -0.5) * 0.3989422804014327
-            act[a, j] = (up * phi).astype(low_type)
-            gu[a, j] = (ga[a, j] * (phi + up * dens)).astype(low_type)
-        grad_two = dot(gu[0, j], wup[0].reshape(D, FS), NT) + dot(gu[1, j], wup[1].reshape(D, FS), NT)
+            part = slice(a * FS, (a + 1) * FS)
+            act[j, :, part] = (up * phi).astype(low_type)
+            gu[j, :, part] = (ga[a, j] * (phi + up * dens)).astype(low_type)
+        grad_two = (
+            dot(gu[j, :, :FS], wup[0].reshape(D, FS), NT) + dot(gu[j, :, FS:], wup[1].reshape(D, FS), NT)
+        )
 
         @pl.when(j == 0)
         def _():
@@ -686,17 +750,17 @@
 
     lax.fori_loop(0, CN, mlp, 0)
 
-    h2_all = h2[...].reshape(TK, D)
-    ct_all = ctg[...].reshape(TK, D)
-    gsib_s[0] = dot(h2_all, gu[o_i].reshape(TK, FS), TN).astype(low_type)
-    put("gs", 2, 0, gsib_s.at[0], gsib_r.at[0], sib)
-    gsib_s[1] = dot(ct_all, act[o_i].reshape(TK, FS), TN).astype(low_type)
-    put("gs", 2, 1, gsib_s.at[1], gsib_r.at[1], sib)
-    gown[0] = dot(h2_all, gu[t_i].reshape(TK, FS), TN)
-    gown[1] = dot(ct_all, act[t_i].reshape(TK, FS), TN)
+    own_part = pl.ds(pl.multiple_of(t_i * FS, FS), FS)
+    other_part = pl.ds(pl.multiple_of(o_i * FS, FS), FS)
+    for k, (left, right) in enumerate(((h2_t, gu), (ct_t, act))):
+        gown[k] = dot(left[...], right[...].reshape(TK, 2 * FS))
+        gsib_s[k] = gown[k, :, other_part].astype(low_type)
+        put("gs", 2, k, gsib_s.at[k], gsib_r.at[k], sib)
 
     def down(j, _):
-        part = dot(act[0, j], wdt[0].reshape(D, FS), NT) + dot(act[1, j], wdt[1].reshape(D, FS), NT)
+        part = (
+            dot(act[j, :, :FS], wdt[0].reshape(D, FS), NT) + dot(act[j, :, FS:], wdt[1].reshape(D, FS), NT)
+        )
 
         @pl.when(j == 0)
         def _():
@@ -712,24 +776,41 @@
 
     for k in range(2):
         got("gs", 2, k, gsib_r.at[k], sib)
-        gown[k] = gown[k] + gsib_r[k].astype(full_type)
-        gz_s[k] = gown[k].astype(low_type).reshape(ZN, R, FS)
-
-    def send_mlp(k):
-        for j in range(1, ZN):
-            put("gz%d" % k, ZN, j, gz_s.at[k, flip(s_i, j, ZN)], gz_r.at[k, j], at_z(j))
+        total = gown[k, :, own_part] + gsib_r[k].astype(full_type)
+        gkeep[k] = total
+        gz_s[k] = total.astype(low_type).reshape(ZN, R, FS)
+
+    @pl.when(outer)
+    def _():
+        for k in range(2):
+            put("gz%d" % k, 4, 2, gz_s.at[k, far_out], gz_r.at[k, 2], plane(pair))
+            put("gz%d" % k, 4, 3, gz_s.at[k, far_in], gz_r.at[k, 3], plane(pair))
+
+    for k in range(2):
+        put("gz%d" % k, 4, 0, gz_s.at[k, pair], gz_r.at[k, 0], plane(pair))
+
+    def relay_mlp(k):
+        @pl.when(jnp.logical_not(outer))
+        def _():
+            for n, z in ((2, far_out), (3, far_in)):
+                got("gz%d" % k, 4, n, gz_r.at[k, n], plane(pair))
+                mine_part = gkeep[k, pl.ds(pl.multiple_of(z * R, R), R)]
+                gz_s[k, z] = (mine_part + gz_r[k, n].astype(full_type)).astype(low_type)
+                base = spot("gz%d" % k, 4)
+                pltpu.make_async_remote_copy(
+                    src_ref=gz_s.at[k, z], dst_ref=gz_r.at[k, 1],
+                    send_sem=ssem.at[base + n], recv_sem=rsem.at[base + 1],
+                    device_id=plane(z), device_id_type=MESH,
+                ).start()
 
     def share_mlp(k, out):
-        total = gown[k, pl.ds(pl.multiple_of(s_i * R, R), R)]
-        for j in range(1, ZN):
-            got("gz%d" % k, ZN, j, gz_r.at[k, j], at_z(j))
-            total = total + gz_r[k, j].astype(full_type)
+        total = gkeep[k, pl.ds(pl.multiple_of(s_i * R, R), R)]
+        for n in range(2):
+            got("gz%d" % k, 4, n, gz_r.at[k, n], plane(pair))
+            total = total + gz_r[k, n].astype(full_type)
         gfin[k] = total.astype(low_type)
-        for j in range(1, CN):
-            put("gc%d" % k, CN, j, gfin.at[k], out.at[c_i], at_ctx(j))
+        spread("gc%d" % k, gfin.at[k], lambda j: out.at[c_i])
         pltpu.make_async_copy(gfin.at[k], out.at[c_i], lsem.at[8 + k]).start()
-
-    send_mlp(0)
 
     grad_two = g2own[...]
     for j in range(1, CN):
@@ -746,14 +827,21 @@
     gres[...] = grad_resid
     gb = grad_resid.astype(low_type)
     gbg[0] = gb
-    for j in range(CN - 1, 0, -1):
-        gms[j] = dot(gb, wot[flip(c_i, j, CN)].reshape(D, HW)).astype(low_type)
-        put("gm", CN, j, gms.at[j], gm.at[j], at_ctx(j))
-    gm[0] = dot(gb, wot[c_i].reshape(D, HW)).astype(low_type)
-    for j in range(1, CN):
-        put("gb", CN, j, gbg.at[0], gbg.at[j], at_ctx(j))
-    for j in range(1, CN):
-        put("bo", CN, j, bos.at[j], bor.at[j], at_ctx(j))
+    for near in (0, 1):
+        mixed = dot(gb, wot[(1 - tstar) * (1 - near) + tstar * near].reshape(D, 2 * HW)).astype(low_type)
+        even, odd = mixed[:, :HW], mixed[:, HW:]
+        first, second = (1, 0) if near else (3, 2)
+        flag = place == 0
+        gms[first] = jnp.where(flag, odd, even)
+        gms[second] = jnp.where(flag, even, odd)
+        for j in (first, second):
+            if j:
+                put("gm", CN, j, gms.at[j], gm.at[j], at_ctx(j))
+    gm[0] = gms[0]
+    spread("gb", gbg.at[0], lambda j: gbg.at[j])
+    for j in (1, 2):
+        half = pl.ds((j - 1) * HB, HB)
+        put_as("bo", 5, 2 + j, 2 + j, bos.at[3, half], bor.at[3, half], at_ctx(j))
 
     dkt[...] = jnp.zeros_like(dkt)
     dvt[...] = jnp.zeros_like(dvt)
@@ -765,11 +853,11 @@
 
         @pl.when(j == 1)
         def _():
-            send_mlp(1)
-
-        @pl.when(j == CN - 1)
-        def _():
-            share_mlp(0, upo)
+            relay_mlp(0)
+
+        @pl.when(j == 2)
+        def _():
+            relay_mlp(1)
 
         grad_rows = stacked(gm[j])
         query_rows = stacked(qs[j])
@@ -792,15 +880,21 @@
     for k in range(2):
         put("dk", 2, k, dks_s.at[k], dks_r.at[k], sib)
 
+    pass_on("gb", gbg)
+    for j in (1, 2):
+        half = pl.ds((j - 1) * HB, HB)
+        got("bo", 5, 2 + j, bor.at[3, half], at_ctx(j))
+        bos[3 - j, half] = (bos[3 - j, half].astype(full_type) + bor[3, half].astype(full_type)).astype(low_type)
+    for j in (1, 2):
+        put_as("bo", 5, j, j, bos.at[j], bor.at[j], at_ctx(j))
+
     def unnorm(grad_n, gain_row, normed, inverse):
         gain_grad = jnp.sum(grad_n * normed, axis=0, keepdims=True)
         e = grad_n * gain_row
         return (inverse * (e - normed * head_mean(e * normed))).astype(low_type), gain_grad
 
-    h1_all = h1[...].reshape(TK, D)
-
-    def share_grad(n, left, right):
-        full = dot(left, right, TN).reshape(ZN, 2, HR, HW)
+    def share_grad(n, full):
+        full = full.reshape(ZN, 2, HR, 2 * HW)
         low_full = full.astype(low_type)
         for k in range(2):
             @pl.when(o_i == k)
@@ -811,10 +905,10 @@
             def _():
                 qown[n] = full[:, k]
 
-        put("qg", 4, n, qsib_s.at[n], qsib_r.at[n], sib)
+        put("qg", 2, n, qsib_s.at[n], qsib_r.at[n], sib)
 
     def reduce_grad(n):
-        got("qg", 4, n, qsib_r.at[n], sib)
+        got("qg", 2, n, qsib_r.at[n], sib)
         total = qown[n] + qsib_r[n].astype(full_type)
         qown[n] = total
         qz_s[n] = total.astype(low_type)
@@ -823,26 +917,27 @@
 
     grad_raw, q_gain_row = unnorm(dqb[...].reshape(TK, HW), qgrow, nq[...], sq[...])
     dqr[...] = grad_raw
-    share_grad(0, h1_all, dqr[...])
     got("dk", 2, 0, dks_r.at[0], sib)
-    dvr[...] = (dvt[:, :TK] + dks_r[0].astype(full_type)).T.astype(low_type)
-    share_grad(2, h1_all, dvr[...])
+    grad_v = (dvt[:, :TK] + dks_r[0].astype(full_type)).T.astype(low_type)
     got("dk", 2, 1, dks_r.at[1], sib)
     grad_k = (dkt[:, :TK] + dks_r[1].astype(full_type)).T
     grad_raw, k_gain_row = unnorm(grad_k, kgrow, nk[...], sk[...])
-    dkr[...] = grad_raw
-    share_grad(1, h1_all, dkr[...])
+    dkv[...] = jnp.concatenate([grad_raw, grad_v], axis=1)
+    share_grad(0, dot(h1_t[...], dkv[...]))
+    have_rest("gb", gbg)
+    empty = jnp.zeros((TK, HW), low_type)
+    share_grad(1, (
+        dot(h1_t[...], jnp.concatenate([dqr[...], empty], axis=1))
+        + dot(gbg[...].reshape(TK, D), jnp.concatenate([empty, attq[...].reshape(TK, HW)], axis=1), TN)
+    ))
     reduce_grad(0)
+    reduce_grad(1)
 
     ln1g = jnp.zeros((1, D), full_type)
     ln1b = jnp.zeros((1, D), full_type)
     for j in range(CN - 1, -1, -1):
         rows = slice(j * TB, (j + 1) * TB)
-        part = (
-            dot(dqr[rows], wqkv[0].reshape(D, HW), NT)
-            + dot(dkr[rows], wqkv[1].reshape(D, HW), NT)
-            + dot(dvr[rows], wqkv[2].reshape(D, HW), NT)
-        )
+        part = dot(dqr[rows], wqb[...].reshape(D, HW), NT) + dot(dkv[rows], wkv[...].reshape(D, 2 * HW), NT)
         if j:
             g1s[j] = part.astype(low_type)
             put("g1", CN, j, g1s.at[j], g1r.at[j], at_ctx(j))
@@ -850,29 +945,14 @@
             g1own[...] = part
         ln1g = ln1g + jnp.sum(part * xh1[j], axis=0, keepdims=True)
         ln1b = ln1b + jnp.sum(part, axis=0, keepdims=True)
-        if j == CN - 1:
-            reduce_grad(2)
-        elif j == CN - 2:
-            reduce_grad(1)
     rows_s[0] = jnp.zeros_like(rows_s[0])
     for k, row in enumerate((ln1g, ln1b, ln2g, ln2b)):
         rows_s[0, k:k + 1, :D] = row
     rows_s[0, 0:1, D:D + HW] = q_gain_row
     rows_s[0, 1:2, D:D + HW] = k_gain_row
     put("rt", 1, 0, rows_s.at[0], rows_r.at[0], sib)
-    for j in range(1, CN):
-        got("gb", CN, j, gbg.at[j], at_ctx(j))
-    share_grad(3, gbg[...].reshape(TK, D), attq[...].reshape(TK, HW))
-
-    total = boown[...]
-    for j in range(1, CN):
-        got("bo", CN, j, bor.at[j], at_ctx(j))
-        total = total + bor[j].astype(full_type)
-    own_rows = pl.ds(t_i * TB, TB)
-    obuf[0] = total.astype(low_type)
-    put("ob", 2, 0, obuf.at[0], bo_o.at[own_rows], sib)
-    pltpu.make_async_copy(obuf.at[0], bo_o.at[own_rows], lsem.at[10]).start()
-    reduce_grad(3)
+    share_mlp(0, upo)
+    share_mlp(1, dno)
 
     got("rt", 1, 0, rows_r.at[0], sib)
     rows_s[1] = rows_s[0] + rows_r[0]
@@ -883,7 +963,14 @@
     for j in range(1, ZN):
         put("pkz", ZN, j, pks.at[2], pks.at[2 + j], at_z(j))
 
-    share_mlp(1, dno)
+    total = boown[...]
+    for j in (1, 2):
+        got("bo", 5, j, bor.at[j], at_ctx(j))
+        total = total + bor[j].astype(full_type)
+    own_rows = pl.ds(t_i * TB, TB)
+    obuf[0] = total.astype(low_type)
+    put("ob", 2, 0, obuf.at[0], bo_o.at[own_rows], sib)
+    pltpu.make_async_copy(obuf.at[0], bo_o.at[own_rows], lsem.at[10]).start()
 
     def share_fin(n):
         total = qown[n, s_i]
@@ -912,8 +999,15 @@
             ).start()
 
     share_fin(0)
-    share_fin(2)
-
+
+    for k, out in ((0, upo), (1, dno)):
+        for j in (1, 2):
+            block = out.at[flip(c_i, j, CN)]
+            got("gc%d" % k, 5, j, block, at_ctx(j))
+            half = block.at[pl.ds((j - 1) * HR, HR)]
+            put_as("gc%d" % k, 5, 2 + j, 2 + j, half, half, at_ctx(3 - j))
+
+    share_fin(1)
     xhat1, inv1 = norm_rows(xg[0].astype(full_type))
     grad_one = g1own[...]
     for j in range(1, CN):
@@ -928,9 +1022,6 @@
     obuf[1] = grad_in.astype(low_type)
     put("ob", 2, 1, obuf.at[1], ig_o.at[own_rows], sib)
     pltpu.make_async_copy(obuf.at[1], ig_o.at[own_rows], lsem.at[11]).start()
-
-    share_fin(1)
-    share_fin(3)
 
     rows_sum = rows_s[1]
     for j in range(1, ZN):
@@ -961,8 +1052,9 @@
     peak_o[...] = peak
 
     for k, out in ((0, upo), (1, dno)):
-        for j in range(1, CN):
-            got("gc%d" % k, CN, j, out.at[flip(c_i, j, CN)], at_ctx(j))
+        for j in (1, 2):
+            half = out.at[flip(c_i, 3, CN), pl.ds((j - 1) * HR, HR)]
+            got("gc%d" % k, 5, 2 + j, half, at_ctx(3 - j))
         pltpu.make_async_copy(gfin.at[k], out.at[c_i], lsem.at[8 + k]).wait()
     other_rows = pl.ds(o_i * TB, TB)
     for k, out in ((0, bo_o), (1, ig_o)):
@@ -971,14 +1063,14 @@
 
     @pl.when(t_i == tstar)
     def _():
-        for n in range(4):
+        for n in range(2):
             pltpu.make_async_copy(qfin.at[n], qkvo.at[place, t_i, n], lsem.at[12 + n]).wait()
 
     for p in range(half_chips):
         for a in range(2):
             @pl.when((t_i != tstar) | (place != p) | (t_i != a))
             def _():
-                for n in range(4):
+                for n in range(2):
                     pltpu.make_async_remote_copy(
                         src_ref=qfin.at[n], dst_ref=qkvo.at[p, a, n],
                         send_sem=ssem.at[spot("qcs%d" % n, CN)],
@@ -988,37 +1080,44 @@
 
     for j in range(1, CN):
         sent("x", CN, j, x_src, sib)
-        sent("ct", CN, j, c_src, sib)
-        sent("woc", CN, j, wot.at[mine, :, c_i], sib)
+        sent("woc", CN, j, wot.at[t_i, :, c_i], sib)
         sent("att", CN, j, attq.at[j], sib)
         sent("h2", CN, j, h2.at[0], sib)
         sent("g2", CN, j, g2s.at[j], sib)
         sent("gm", CN, j, gms.at[j], sib)
-        sent("gb", CN, j, gbg.at[0], sib)
-        sent("bo", CN, j, bos.at[j], sib)
         sent("g1", CN, j, g1s.at[j], sib)
         sent("pkc", CN, j, pks.at[first], sib)
         sent("rc", CN, j, rows_s.at[2], sib)
-        sent("gc0", CN, j, gfin.at[0], sib)
-        sent("gc1", CN, j, gfin.at[1], sib)
-        for n in range(4):
+        for n in range(2):
             sent("qcs%d" % n, CN, j, qfin.at[n], sib)
     for j in range(1, ZN):
         sent("small", ZN, j, smalls.at[t_i, s_i], sib)
-        sent("woz", ZN, j, wot.at[mine, s_i, c_i], sib)
-        sent("wdz", ZN, j, wdt.at[t_i, s_i], sib)
-        sent("wuz", ZN, j, wup.at[t_i, s_i], sib)
-        sent("gz0", ZN, j, gz_s.at[0, 0], sib)
-        sent("gz1", ZN, j, gz_s.at[1, 0], sib)
+        sent("woz", ZN, j, wot.at[t_i, s_i, c_i], sib)
         sent("pkz", ZN, j, pks.at[2], sib)
         sent("rz", ZN, j, rows_s.at[1], sib)
-        for n in range(4):
+        for n in range(2):
             sent("qz%d" % n, ZN, j, qz_s.at[n, 0], sib)
+    for n in range(1, 5):
+        for name, buf, half in (("ct", ctg, ctg), ("gb", gbg, gbg), ("bo", bos, bos)):
+            sent(name, 5, n, buf.at[1] if n < 3 else half.at[1, pl.ds(0, HB)], sib)
+        for k, out in ((0, upo), (1, dno)):
+            sent("gc%d" % k, 5, n, gfin.at[k] if n < 3 else gfin.at[k, pl.ds(0, HR)], sib)
+    for name, buf in mlp_weights:
+        sent(name, 5, 0, buf.at[t_i, s_i], sib)
+
+        @pl.when(jnp.logical_not(outer))
+        def _():
+            for n in range(1, 5):
+                sent(name, 5, n, buf.at[t_i, s_i], sib)
+
+    for k in range(2):
+        for n in (0, 2, 3):
+            sent("gz%d" % k, 4, n, gz_s.at[k, 0], sib)
     sent("smallt", 1, 0, smalls.at[t_i], sib)
     sent("k", 1, 0, kall.at[0], sib)
     sent("v", 1, 0, vall.at[0], sib)
     sent("pkt", 1, 0, pks.at[0], sib)
-    sent("wot", 1, 0, wot.at[mine], sib)
+    sent("wot", 1, 0, wot.at[t_i], sib)
     sent("wdt", 1, 0, wdt.at[t_i], sib)
     sent("wut", 1, 0, wup.at[t_i], sib)
     sent("rt", 1, 0, rows_s.at[0], sib)
@@ -1026,20 +1125,20 @@
         sent("gs", 2, k, gsib_s.at[k], sib)
         sent("dk", 2, k, dks_s.at[k], sib)
         sent("ob", 2, k, obuf.at[k], sib)
-    for n in range(4):
-        sent("qg", 4, n, qsib_s.at[n], sib)
+    for n in range(2):
+        sent("qg", 2, n, qsib_s.at[n], sib)
 
     @pl.when(t_i == tstar)
     def _():
-        for g in range(3):
+        for name, buf in projections:
             for j in range(ZN):
-                sent("w%d" % g, ZN, j, wqkv.at[g, s_i], sib)
+                sent(name, ZN, j, buf.at[s_i], sib)
                 if j:
-                    sent("f%d" % g, ZN, j, wqkv.at[g, s_i], sib)
+                    sent("f" + name, ZN, j, buf.at[s_i], sib)
 
     @pl.when(t_i != tstar)
     def _():
-        for n in range(4):
+        for n in range(2):
             sent("qcs%d" % n, CN, 0, qfin.at[n], sib)
 
 
@@ -1061,7 +1160,7 @@
         jax.ShapeDtypeStruct((2 * TB, D), lo),
         jax.ShapeDtypeStruct((CN, R, FS), lo),
         jax.ShapeDtypeStruct((CN, R, FS), lo),
-        jax.ShapeDtypeStruct((half_chips, 2, 4, HR, HW), lo),
+        jax.ShapeDtypeStruct((half_chips, 2, 2, HR, 2 * HW), lo),
         jax.ShapeDtypeStruct((8, D), hi),
         jax.ShapeDtypeStruct((CN, 8, 256), hi),
         jax.ShapeDtypeStruct((8, 128), hi),
@@ -1069,24 +1168,25 @@
     scratch = [
         V((CN, TB, D), lo), V((CN, TB, D), lo), V((2, ZN, 8, 256), hi),
         V((3, R, half_chips * HW), lo), V((R, half_chips * HW), lo),
-        V((3, ZN, R, HW), lo), V((CN, ZN, CN, QR, HW), lo), V((2, ZN, R, FS), lo), V((2, ZN, R, FS), lo),
+        V((ZN, R, 2 * HW), lo), V((ZN, R, HW), lo), V((2, ZN, CN, QR, 2 * HW), lo), V((2, ZN, R, FS), lo), V((2, ZN, R, FS), lo),
+        V((D, TK), lo), V((D, TK), lo), V((D, TK), lo),
         V((CN, TB, D), hi), V((CN, TB, D), lo),
         V((TK, HW), hi), V((TK, HW), hi), V((TK, HW), hi), V((TK, HW), hi),
         V((CN, TB, HW), lo), V((2, TK, HW), lo), V((2, TK, HW), lo),
         V((CN, heads * TB, 2 * TK), hi), V((heads * TB, 2 * TK), hi),
         V((CN, TB, HW), lo), V((CN, TB, HW), lo), V((2 + ZN + CN, 8, 128), hi),
         V((heads, 2 * TK), hi), V((heads * TB, 2 * TK), lo),
-        V((CN, TB, D), lo), V((2, CN, TB, FS), hi), V((2, CN, TB, FS), lo), V((2, CN, TB, FS), lo),
+        V((CN, TB, D), lo), V((2, CN, TB, FS), hi), V((CN, TB, 2 * FS), lo), V((CN, TB, 2 * FS), lo),
         V((CN, TB, D), lo), V((CN, TB, D), lo), V((TB, D), hi),
         V((CN, TB, D), lo), V((CN, TB, D), lo), V((TB, D), hi),
-        V((2, D, FS), lo), V((2, D, FS), lo), V((2, D, FS), hi),
+        V((2, D, FS), lo), V((2, D, FS), lo), V((2, D, 2 * FS), hi), V((2, D, FS), hi),
         V((2, ZN, R, FS), lo), V((2, ZN, R, FS), lo), V((2, R, FS), lo),
         V((TB, D), hi), V((CN, TB, D), lo), V((CN, TB, HW), lo), V((CN, TB, HW), lo),
         V((CN, TB, HW), hi), V((HW, 2 * TK), hi), V((HW, 2 * TK), hi),
-        V((2, HW, TK), lo), V((2, HW, TK), lo), V((TK, HW), lo), V((TK, HW), lo), V((TK, HW), lo),
+        V((2, HW, TK), lo), V((2, HW, TK), lo), V((TK, HW), lo), V((TK, 2 * HW), lo),
         V((CN, TB, D), lo), V((CN, TB, D), lo), V((TB, D), hi),
-        V((4, ZN, HR, HW), lo), V((4, ZN, HR, HW), lo), V((4, ZN, HR, HW), hi),
-        V((4, ZN, HR, HW), lo), V((4, ZN, HR, HW), lo), V((4, HR, HW), lo),
+        V((2, ZN, HR, 2 * HW), lo), V((2, ZN, HR, 2 * HW), lo), V((2, ZN, HR, 2 * HW), hi),
+        V((2, ZN, HR, 2 * HW), lo), V((2, ZN, HR, 2 * HW), lo), V((2, HR, 2 * HW), lo),
         V((3, 8, D + 256), hi), V((ZN + CN, 8, D + 256), hi), V((2, TB, D), lo),
         pltpu.SemaphoreType.DMA((16,)), pltpu.SemaphoreType.DMA((SEMS,)), pltpu.SemaphoreType.DMA((SEMS,)),
     ]
@@ -1104,38 +1204,46 @@
 
 def finish_kernel(
     sizes,
-    bo, ig, upo, dno, qkvo, lnr, qkr, peak, wq, wk,
-    bo_o, ig_o, l1g, l1b, l2g, l2b, qg_o, kg_o, gq, gk, gv, go, gu, gd, cq, ck,
+    bo, ig, up_h, dn_h, qkvo_h, lnr_h, qkr_h, peak_h, wq_h, wk_h,
+    bo_o, ig_o, l1g, l1b, l2g, l2b, qg_o, kg_o, gq_o, gk_o, gv_o, go_o, gu_o, gd_o, cq_o, ck_o,
+    upo, dno, qkvo, lnr, qkr, peak, wq, wk, bov, igv, gq, gk, gv, go, gu, gd, cq, ck, isem, osem,
 ):
     CN, ZN, TB, D, HW, FS, R = sizes
     half_chips = CN // 2
     s_i, t_i = lax.axis_index("shard"), lax.axis_index("tp")
-    bo_o[...] = bo[...]
-    ig_o[...] = ig[...]
-    for n, out in enumerate((gq, gk, gv, go)):
+    ins = [
+        pltpu.make_async_copy(src, dst, isem.at[n])
+        for n, (src, dst) in enumerate((
+            (qkvo_h, qkvo), (up_h, upo), (dn_h, dno), (peak_h, peak), (wq_h, wq), (wk_h, wk),
+            (lnr_h, lnr), (qkr_h, qkr), (bo, bov), (ig, igv),
+        ))
+    ]
+    for n in (8, 9, 0, 1, 2, 3, 4, 5, 6, 7):
+        ins[n].start()
+    outs = []
+
+    def leave(src, dst):
+        copy = pltpu.make_async_copy(src, dst, osem.at[len(outs)])
+        copy.start()
+        outs.append(copy)
+
+    for n, stage, out in ((8, bov, bo_o), (9, igv, ig_o)):
+        ins[n].wait()
+        leave(stage, out)
+    ins[0].wait()
+    for n, first, stage, out in ((1, 0, gq, gq_o), (0, 0, gk, gk_o), (0, HW, gv, gv_o), (1, HW, go, go_o)):
         for a in range(2):
-            parts = [qkvo[p, a, n] for p in range(half_chips)]
-            out[a * (R // 2):(a + 1) * (R // 2)] = jnp.concatenate(parts, axis=1).astype(full_type)
-    for c in range(CN):
-        gu[:, c * FS:(c + 1) * FS] = upo[c].astype(full_type)
-        gd[:, c * FS:(c + 1) * FS] = dno[c].astype(full_type)
-    rows = jnp.zeros((8, R), full_type)
-    for z in range(ZN):
-        rows = jnp.where(s_i == z, lnr[:, z * R:(z + 1) * R], rows)
-    for k, out in enumerate((l1g, l1b, l2g, l2b)):
-        out[...] = rows[k:k + 1].reshape(R)
+            parts = [qkvo[p, a, n][:, first:first + HW] for p in range(half_chips)]
+            stage[a * (R // 2):(a + 1) * (R // 2)] = jnp.concatenate(parts, axis=1).astype(full_type)
+        leave(stage, out)
+    for n, grads, stage, out in ((1, upo, gu, gu_o), (2, dno, gd, gd_o)):
+        ins[n].wait()
+        for c in range(CN):
+            stage[:, c * FS:(c + 1) * FS] = grads[c].astype(full_type)
+        leave(stage, out)
     heads = HW // 64
-    piece = qg_o.shape[1]
-    for p in range(half_chips):
-        chip = qkr[t_i * half_chips + p]
-        for h in range(heads):
-            for z in range(ZN):
-                at = h * 64 + z * piece
-
-                @pl.when(s_i == z)
-                def _():
-                    qg_o[p * heads + h:p * heads + h + 1] = chip[0:1, at:at + piece]
-                    kg_o[p * heads + h:p * heads + h + 1] = chip[1:2, at:at + piece]
+    for n in (3, 4, 5):
+        ins[n].wait()
     factor = jnp.sqrt(clip_level / jnp.maximum(peak[0:1], clip_level))
     here = half_chips * heads
     lanes = lax.broadcasted_iota(jnp.int32, (1, here * 64), 1) // 64
@@ -1144,8 +1252,29 @@
     for h in range(here):
         one = jnp.sum(jnp.where(ids == t_i * here + h, factor, 0.0), axis=-1, keepdims=True)
         columns = jnp.where(lanes == h, one, columns)
-    cq[...] = (wq[...].astype(full_type) * columns).astype(low_type)
-    ck[...] = (wk[...].astype(full_type) * columns).astype(low_type)
+    for weights, stage, out in ((wq, cq, cq_o), (wk, ck, ck_o)):
+        stage[...] = (weights[...].astype(full_type) * columns).astype(low_type)
+        leave(stage, out)
+    ins[6].wait()
+    ins[7].wait()
+    rows = jnp.zeros((8, R), full_type)
+    for z in range(ZN):
+        rows = jnp.where(s_i == z, lnr[:, z * R:(z + 1) * R], rows)
+    for k, out in enumerate((l1g, l1b, l2g, l2b)):
+        out[...] = rows[k:k + 1].reshape(R)
+    piece = qg_o.shape[1]
+    for p in range(half_chips):
+        chip = qkr[t_i * half_chips + p]
+        for h in range(heads):
+            for z in range(ZN):
+                at = h * 64 + z * piece
+
+                @pl.when(s_i == z)
+                def _():
+                    qg_o[p * heads + h:p * heads + h + 1] = chip[0:1, at:at + piece]
+                    kg_o[p * heads + h:p * heads + h + 1] = chip[1:2, at:at + piece]
+    for copy in outs:
+        copy.wait()
 
 
 def fused_layer(
@@ -1169,12 +1298,23 @@
     wide = jax.ShapeDtypeStruct(w_up.shape, full_type)
     tokens = jax.ShapeDtypeStruct(images.shape[1:], low_type)
     clipped = jax.ShapeDtypeStruct(w_query.shape, low_type)
+    lo, hi = low_type, full_type
+    V = pltpu.VMEM
+    any_spec = pl.BlockSpec(memory_space=pl.ANY)
+    vm_spec = pl.BlockSpec(memory_space=pltpu.VMEM)
     out = pl.pallas_call(
         functools.partial(finish_kernel, sizes),
         out_shape=[tokens] * 2 + [row] * 4 + [gain] * 2 + [square] * 4 + [wide] * 2 + [clipped] * 2,
-        in_specs=[pl.BlockSpec(memory_space=pltpu.VMEM)] * 10,
-        out_specs=[pl.BlockSpec(memory_space=pltpu.VMEM)] * 16,
-        compiler_params=pltpu.CompilerParams(vmem_limit_bytes=40 * 2**20),
+        in_specs=[any_spec] * 10,
+        out_specs=[any_spec] * 2 + [vm_spec] * 6 + [any_spec] * 8,
+        scratch_shapes=[
+            V((CN, R, FS), lo), V((CN, R, FS), lo), V((CN // 2, 2, 2, R // 2, 2 * HW), lo), V((8, D), hi),
+            V((CN, 8, 256), hi), V((8, 128), hi), V(w_query.shape, lo), V(w_query.shape, lo),
+            V(images.shape[1:], lo), V(images.shape[1:], lo),
+        ]
+        + [V(w_query.shape, hi)] * 4 + [V(w_up.shape, hi)] * 2 + [V(w_query.shape, lo)] * 2
+        + [pltpu.SemaphoreType.DMA((10,)), pltpu.SemaphoreType.DMA((10,))],
+        compiler_params=pltpu.CompilerParams(vmem_limit_bytes=60 * 2**20),
     )(*results, w_query, w_key)
     out = list(out)
     out[0], out[1] = out[0].reshape(images.shape), out[1].reshape(images.shape)

time: 138 us -> 115 us (0.83); the launches traced: 138 us -> 113 us
  Pallas kernels: 130 us -> 113 us
  local copies, waits for them, and re-layouts: 7.42 us -> 0 us
    pallas_call x1, Pallas kernels: 127 us -> 109 us  [fused_call(): pl.pallas_call(functools.partial(fused_kernel, sizes), out_shape=out_shap...]
    unnamed x20 -> x0, local copies, waits for them, and re-layouts: 7.42 us -> none
where the time goes in v3:
time: 115 us; the launch traced here: 113 us
  Pallas kernels  113 us (98%)
    pallas_call x1, Pallas kernels, fused_call(): pl.pallas_call(functools.partial(fused_kernel, sizes), out_shape=out_shap...  109 us
    pallas_call x1, Pallas kernels, fused_layer(): pl.pallas_call(functools.partial(finish_kernel, sizes), out_shape=[tokens...  4.07 us

profile of v3, /device:TPU:0, one launch (start us, length us, event | category | flops | bytes accessed | tf_op | source)
XLA Modules:
  0.0 113.5 jit_solution(11544003440883175043)
XLA Ops:
  0.7 108.6 %shard_map.261 = (bf16[256,768]{1,0:T(8,128)(2,1)}, bf16[256,768]{1,0:T(8,128)(2,1)}, bf16[4,192,384]{2,1,0:T(8,128)(2,1)}, bf16[4,192,384]{2,1,0:T(8,128)(2,1)}...) custom-call(bf16[1,256,768]{2,1,0:T(8,128)(2,1)} %img_h.1, ...), custom_call_target="tpu_custom_call" | custom-call | tf_op jit(solution)/shard_map/pallas_call | solution.py:1193
  109.2 4.1 %shard_map.262 = (bf16[256,768]{1,0:T(8,128)(2,1)}, bf16[256,768]{1,0:T(8,128)(2,1)}, f32[192]{0:T(256)}, f32[192]{0:T(256)}, f32[192]{0:T(256)}, /*index=5*/f32...) custom-call(bf16[256,768]{1,0:T(8,128)(2,1)} %get-tuple-element.40.b, ...), custom_call_target="tpu_custom_call" | custom-call | tf_op jit(solution)/shard_map/pallas_call | solution.py:1305

commit v4 on v3

--- a/solution.py
+++ b/solution.py
@@ -352,18 +352,17 @@
     sizes,
     img_h, cot_h, g1_h, b1_h, g2_h, b2_h, qg_h, kg_h, wq_h, wk_h, wv_h, wo_h, wup_h, wdn_h,
     bo_o, ig_o, upo, dno, qkvo, lnr_o, qkr_o, peak_o,
-    xg, ctg, smalls, wl, wol, wkv, wqb, wot, wup, wdt, h1_t, h2_t, ct_t,
-    xh1, h1, nq, nk, sq, sk, qs, kall, vall, pst, sbuf, attq, attr, pks,
+    xg, ctg, smalls, wl, wol, wkv, wqb, wob, wup, wdt, h1_t, h2_t, ct_t,
+    xh1, h1, nq, nk, sq, sk, qs, kall, vall, pst, sbuf, attq, brs, brr, pks,
     ptop, dsb,
     h2, ga, act, gu, g2s, g2r, g2own, bos, bor, boown,
     gsib_s, gsib_r, gown, gkeep, gz_s, gz_r, gfin,
-    gres, gbg, gms, gm, dqb, dkt, dvt, dks_s, dks_r, dqr, dkv,
+    gres, gbg, dqb, dkt, dvt, dks_s, dks_r, dqr, dkv,
     g1s, g1r, g1own, qsib_s, qsib_r, qown, qz_s, qz_r, qfin,
     rows_s, rows_r, obuf,
     lsem, ssem, rsem,
 ):
     CN, ZN, TB, D, HW, FS, R = sizes
-    QR = R // CN
     HR = R // 2
     s_i, c_i, t_i = lax.axis_index("shard"), lax.axis_index("ctx"), lax.axis_index("tp")
     o_i = 1 - t_i
@@ -390,10 +389,14 @@
         return (z, c_i, t_i)
 
     spots = {}
+    from_one = ("x", "small", "fwkv", "fwq", "fwo", "br", "h2", "g2", "qz0", "qz1", "rz", "pkz", "rc", "pkc",
+                "ct", "gb", "bo", "g1", "gc0", "gc1")
 
     def spot(name, count):
         if name not in spots:
-            spots[name] = (sum(n for _, n in spots.values()), count)
+            first = sum(n for _, n in spots.values())
+            skip = 1 if name in from_one else 0
+            spots[name] = (first - skip, count - skip)
         return spots[name][0]
 
     def put(name, count, j, src, dst, dev):
@@ -472,7 +475,9 @@
         cols = lax.broadcasted_iota(jnp.int32, (half_chips * HW, lanes), 1) - offset
         return ((rows == cols + at * HW) & (cols >= 0) & (cols < HW)).astype(full_type).astype(low_type)
 
-    projections = (("wkv", wkv), ("wq", wqb))
+    projections = (("wkv", wkv), ("wq", wqb), ("wo", wob))
+
+    locals_[4].wait()
 
     @pl.when(t_i == tstar)
     def _():
@@ -482,6 +487,7 @@
             dot(wl[1], picker(place, 2 * HW, 0)) + dot(wl[2], picker(place, 2 * HW, HW))
         ).astype(low_type)
         wqb[s_i] = dot(wl[0], picker(place, HW, 0)).astype(low_type)
+        wob[s_i] = dot(wol[...], picker(place, HW, 0)).astype(low_type)
         for name, buf in projections:
             for j in range(1, ZN):
                 put(name, ZN, j, buf.at[s_i], buf.at[s_i], at_z(j))
@@ -491,11 +497,6 @@
     def _():
         for n in range(3):
             locals_[n].wait()
-
-    locals_[4].wait()
-    wot[t_i, s_i, c_i] = wol[pl.ds(c_i * QR, QR)]
-    for j in range(1, ZN):
-        put("woz", ZN, j, wot.at[t_i, s_i, c_i], wot.at[t_i, s_i, c_i], at_z(j))
 
     for j in range(1, ZN):
         got("small", ZN, j, smalls.at[t_i, flip(s_i, j, ZN)], at_z(j))
@@ -535,6 +536,19 @@
             got(name, 5, j, buf.at[j], at_ctx(j))
             half = pl.ds((j - 1) * HB, HB)
             put_as(name, 5, 2 + j, 2 + j, buf.at[j, half], buf.at[3, half], at_ctx(3 - j))
+
+    def send_halves(name, src, land):
+        for j in (1, 2):
+            half = pl.ds((j - 1) * HB, HB)
+            put_as(name, 5, 2 + j, 2 + j, src.at[3, half], land.at[3, half], at_ctx(j))
+
+    def add_halves(name, src, land):
+        for j in (1, 2):
+            half = pl.ds((j - 1) * HB, HB)
+            got(name, 5, 2 + j, land.at[3, half], at_ctx(j))
+            src[3 - j, half] = (src[3 - j, half].astype(full_type) + land[3, half].astype(full_type)).astype(low_type)
+        for j in (1, 2):
+            put_as(name, 5, j, j, src.at[j], land.at[j], at_ctx(j))
 
     def have_rest(name, buf):
         for j in (1, 2):
@@ -625,10 +639,6 @@
     own_mlp(*mlp_weights[0])
     locals_[6].wait()
     own_mlp(*mlp_weights[1])
-    for j in range(1, ZN):
-        got("woz", ZN, j, wot.at[t_i, flip(s_i, j, ZN), c_i], at_z(j))
-    for j in range(1, CN):
-        put("woc", CN, j, wot.at[t_i, :, c_i], wot.at[t_i, :, c_i], at_ctx(j))
     raw = dot(h1_all, wqb[...].reshape(D, HW))
     inverse = lax.rsqrt(head_mean(raw * raw) + norm_eps)
     normed = raw * inverse
@@ -636,7 +646,6 @@
     sq[...] = inverse
     qs[...] = ((normed * qgrow).astype(low_type) * 0.125).astype(low_type).reshape(CN, TB, HW)
 
-    pass_on("ct", ctg)
     got("k", 1, 0, kall.at[1], sib)
     got("v", 1, 0, vall.at[1], sib)
 
@@ -654,11 +663,10 @@
     def attend(i, _):
         j = CN - 1 - i
 
-        for name, buf, when in (mlp_weights[0] + (1,), mlp_weights[1] + (2,)):
-            @pl.when(i == when)
-            def _():
-                pass_mlp(name, buf, 0)
-                pass_mlp(name, buf, 1)
+        @pl.when(i == CN - 1)
+        def _():
+            pass_mlp(*mlp_weights[0], 0)
+            pass_mlp(*mlp_weights[0], 1)
 
         sbuf[...] = dot(stacked(qs[j]), kall[...].reshape(2 * TK, HW), NT)
         for h in range(heads):
@@ -670,16 +678,27 @@
         mixed = folded(dot(pst[j].astype(low_type), vall[...].reshape(2 * TK, HW)))
         attq[j] = mixed.astype(low_type)
 
+        @pl.when(i == 0)
+        def _():
+            weight_ready(*projections[2])
+
+        branch = dot(attq[j], wob[...].reshape(D, HW), NT)
+
         @pl.when(j > 0)
         def _():
-            put("att", CN, j, attq.at[j], attr.at[j], at_ctx(j))
+            brs[j] = branch.astype(low_type)
+            put("br", CN, j, brs.at[j], brr.at[j], at_ctx(j))
+
+        @pl.when(j == 0)
+        def _():
+            boown[...] = branch
 
         return 0
 
     lax.fori_loop(0, CN, attend, 0)
-    for j in range(1, CN):
-        got("woc", CN, j, wot.at[t_i, :, flip(c_i, j, CN)], at_ctx(j))
-    put("wot", 1, 0, wot.at[t_i], wot.at[t_i], sib)
+    pass_mlp(*mlp_weights[1], 0)
+    pass_mlp(*mlp_weights[1], 1)
+    pass_on("ct", ctg)
     pass_mlp(*mlp_weights[0], 2)
     peak_rows = jnp.max(ptop[...], axis=-1, keepdims=True)
     lane_id = lax.broadcasted_iota(jnp.int32, (8, 128), 1)
@@ -689,16 +708,10 @@
     pks[0] = own_peak
     put("pkt", 1, 0, pks.at[0], pks.at[1], sib)
 
-    def pair_up(own, other):
-        even = place == 0
-        return jnp.concatenate([jnp.where(even, own, other), jnp.where(even, other, own)], axis=1)
-
-    got("wot", 1, 0, wot.at[o_i], sib)
-    got("att", CN, 1, attr.at[1], at_ctx(1))
-    branch = dot(pair_up(attq[0], attr[1]), wot[tstar].reshape(D, 2 * HW), NT)
-    for j in (2, 3):
-        got("att", CN, j, attr.at[j], at_ctx(j))
-    branch = branch + dot(pair_up(attr[2], attr[3]), wot[1 - tstar].reshape(D, 2 * HW), NT)
+    branch = boown[...]
+    for j in (3, 2, 1):
+        got("br", CN, j, brr.at[j], at_ctx(j))
+        branch = branch + brr[j].astype(full_type)
     resid = xg[0].astype(full_type) + branch
     boown[...] = resid
     xhat2, inv2 = norm_rows(resid)
@@ -750,6 +763,10 @@
 
     lax.fori_loop(0, CN, mlp, 0)
 
+    got("pkt", 1, 0, pks.at[1], sib)
+    pks[2] = jnp.maximum(pks[0], pks[1])
+    for j in range(1, ZN):
+        put("pkz", ZN, j, pks.at[2], pks.at[2 + j], at_z(j))
     own_part = pl.ds(pl.multiple_of(t_i * FS, FS), FS)
     other_part = pl.ds(pl.multiple_of(o_i * FS, FS), FS)
     for k, (left, right) in enumerate(((h2_t, gu), (ct_t, act))):
@@ -827,39 +844,34 @@
     gres[...] = grad_resid
     gb = grad_resid.astype(low_type)
     gbg[0] = gb
-    for near in (0, 1):
-        mixed = dot(gb, wot[(1 - tstar) * (1 - near) + tstar * near].reshape(D, 2 * HW)).astype(low_type)
-        even, odd = mixed[:, :HW], mixed[:, HW:]
-        first, second = (1, 0) if near else (3, 2)
-        flag = place == 0
-        gms[first] = jnp.where(flag, odd, even)
-        gms[second] = jnp.where(flag, even, odd)
-        for j in (first, second):
-            if j:
-                put("gm", CN, j, gms.at[j], gm.at[j], at_ctx(j))
-    gm[0] = gms[0]
     spread("gb", gbg.at[0], lambda j: gbg.at[j])
-    for j in (1, 2):
-        half = pl.ds((j - 1) * HB, HB)
-        put_as("bo", 5, 2 + j, 2 + j, bos.at[3, half], bor.at[3, half], at_ctx(j))
+    send_halves("bo", bos, bor)
+
+    peak = pks[2]
+    for j in range(1, ZN):
+        got("pkz", ZN, j, pks.at[2 + j], at_z(j))
+        peak = jnp.maximum(peak, pks[2 + j])
+    first = 2 + ZN
+    pks[first] = peak
+    for j in range(1, CN):
+        put("pkc", CN, j, pks.at[first], pks.at[first + j], at_ctx(j))
 
     dkt[...] = jnp.zeros_like(dkt)
     dvt[...] = jnp.zeros_like(dvt)
 
     def attend_back(j, _):
-        @pl.when(j > 0)
-        def _():
-            got("gm", CN, j, gm.at[j], at_ctx(j))
-
         @pl.when(j == 1)
         def _():
+            pass_on("gb", gbg)
             relay_mlp(0)
 
-        @pl.when(j == 2)
-        def _():
+        @pl.when(j == CN - 1)
+        def _():
+            add_halves("bo", bos, bor)
+            have_rest("gb", gbg)
             relay_mlp(1)
 
-        grad_rows = stacked(gm[j])
+        grad_rows = stacked(dot(gbg[j], wob[...].reshape(D, HW)).astype(low_type))
         query_rows = stacked(qs[j])
         sbuf[...] = dot(grad_rows, vall[...].reshape(2 * TK, HW), NT)
 
@@ -880,13 +892,10 @@
     for k in range(2):
         put("dk", 2, k, dks_s.at[k], dks_r.at[k], sib)
 
-    pass_on("gb", gbg)
-    for j in (1, 2):
-        half = pl.ds((j - 1) * HB, HB)
-        got("bo", 5, 2 + j, bor.at[3, half], at_ctx(j))
-        bos[3 - j, half] = (bos[3 - j, half].astype(full_type) + bor[3, half].astype(full_type)).astype(low_type)
-    for j in (1, 2):
-        put_as("bo", 5, j, j, bos.at[j], bor.at[j], at_ctx(j))
+    for j in range(1, CN):
+        got("pkc", CN, j, pks.at[first + j], at_ctx(j))
+        peak = jnp.maximum(peak, pks[first + j])
+    peak_o[...] = peak
 
     def unnorm(grad_n, gain_row, normed, inverse):
         gain_grad = jnp.sum(grad_n * normed, axis=0, keepdims=True)
@@ -917,6 +926,11 @@
 
     grad_raw, q_gain_row = unnorm(dqb[...].reshape(TK, HW), qgrow, nq[...], sq[...])
     dqr[...] = grad_raw
+    empty = jnp.zeros((TK, HW), low_type)
+    share_grad(1, (
+        dot(h1_t[...], jnp.concatenate([dqr[...], empty], axis=1))
+        + dot(gbg[...].reshape(TK, D), jnp.concatenate([empty, attq[...].reshape(TK, HW)], axis=1), TN)
+    ))
     got("dk", 2, 0, dks_r.at[0], sib)
     grad_v = (dvt[:, :TK] + dks_r[0].astype(full_type)).T.astype(low_type)
     got("dk", 2, 1, dks_r.at[1], sib)
@@ -924,14 +938,8 @@
     grad_raw, k_gain_row = unnorm(grad_k, kgrow, nk[...], sk[...])
     dkv[...] = jnp.concatenate([grad_raw, grad_v], axis=1)
     share_grad(0, dot(h1_t[...], dkv[...]))
-    have_rest("gb", gbg)
-    empty = jnp.zeros((TK, HW), low_type)
-    share_grad(1, (
-        dot(h1_t[...], jnp.concatenate([dqr[...], empty], axis=1))
-        + dot(gbg[...].reshape(TK, D), jnp.concatenate([empty, attq[...].reshape(TK, HW)], axis=1), TN)
-    ))
+    reduce_grad(1)
     reduce_grad(0)
-    reduce_grad(1)
 
     ln1g = jnp.zeros((1, D), full_type)
     ln1b = jnp.zeros((1, D), full_type)
@@ -940,9 +948,10 @@
         part = dot(dqr[rows], wqb[...].reshape(D, HW), NT) + dot(dkv[rows], wkv[...].reshape(D, 2 * HW), NT)
         if j:
             g1s[j] = part.astype(low_type)
-            put("g1", CN, j, g1s.at[j], g1r.at[j], at_ctx(j))
         else:
             g1own[...] = part
+        if j == 3:
+            send_halves("g1", g1s, g1r)
         ln1g = ln1g + jnp.sum(part * xh1[j], axis=0, keepdims=True)
         ln1b = ln1b + jnp.sum(part, axis=0, keepdims=True)
     rows_s[0] = jnp.zeros_like(rows_s[0])
@@ -952,16 +961,12 @@
     rows_s[0, 1:2, D:D + HW] = k_gain_row
     put("rt", 1, 0, rows_s.at[0], rows_r.at[0], sib)
     share_mlp(0, upo)
+    add_halves("g1", g1s, g1r)
     share_mlp(1, dno)
-
     got("rt", 1, 0, rows_r.at[0], sib)
     rows_s[1] = rows_s[0] + rows_r[0]
     for j in range(1, ZN):
         put("rz", ZN, j, rows_s.at[1], rows_r.at[j], at_z(j))
-    got("pkt", 1, 0, pks.at[1], sib)
-    pks[2] = jnp.maximum(pks[0], pks[1])
-    for j in range(1, ZN):
-        put("pkz", ZN, j, pks.at[2], pks.at[2 + j], at_z(j))
 
     total = boown[...]
     for j in (1, 2):
@@ -998,9 +1003,7 @@
                 device_id=sib, device_id_type=MESH,
             ).start()
 
-    share_fin(0)
-
-    for k, out in ((0, upo), (1, dno)):
+    def pass_grad(k, out):
         for j in (1, 2):
             block = out.at[flip(c_i, j, CN)]
             got("gc%d" % k, 5, j, block, at_ctx(j))
@@ -1008,10 +1011,12 @@
             put_as("gc%d" % k, 5, 2 + j, 2 + j, half, half, at_ctx(3 - j))
 
     share_fin(1)
+    pass_grad(0, upo)
+
     xhat1, inv1 = norm_rows(xg[0].astype(full_type))
     grad_one = g1own[...]
-    for j in range(1, CN):
-        got("g1", CN, j, g1r.at[j], at_ctx(j))
+    for j in (1, 2):
+        got("g1", 5, j, g1r.at[j], at_ctx(j))
         grad_one = grad_one + g1r[j].astype(full_type)
     hat = grad_one * g1row
     grad_in = gres[...] + inv1 * (
@@ -1023,6 +1028,7 @@
     put("ob", 2, 1, obuf.at[1], ig_o.at[own_rows], sib)
     pltpu.make_async_copy(obuf.at[1], ig_o.at[own_rows], lsem.at[11]).start()
 
+    pass_grad(1, dno)
     rows_sum = rows_s[1]
     for j in range(1, ZN):
         got("rz", ZN, j, rows_r.at[j], at_z(j))
@@ -1030,15 +1036,10 @@
     rows_s[2] = rows_sum
     for j in range(1, CN):
         put("rc", CN, j, rows_s.at[2], rows_r.at[ZN + j], at_ctx(j))
-    peak = pks[2]
-    for j in range(1, ZN):
-        got("pkz", ZN, j, pks.at[2 + j], at_z(j))
-        peak = jnp.maximum(peak, pks[2 + j])
-    first = 2 + ZN
-    pks[first] = peak
-    for j in range(1, CN):
-        put("pkc", CN, j, pks.at[first], pks.at[first + j], at_ctx(j))
     qkr_o[c_i] = rows_sum[:, D:]
+
+    share_fin(0)
+
     total = rows_sum[:, :D]
     for j in range(1, CN):
         got("rc", CN, j, rows_r.at[ZN + j], at_ctx(j))
@@ -1046,10 +1047,6 @@
         total = total + block[:, :D]
         qkr_o[flip(c_i, j, CN)] = block[:, D:]
     lnr_o[...] = total
-    for j in range(1, CN):
-        got("pkc", CN, j, pks.at[first + j], at_ctx(j))
-        peak = jnp.maximum(peak, pks[first + j])
-    peak_o[...] = peak
 
     for k, out in ((0, upo), (1, dno)):
         for j in (1, 2):
@@ -1080,25 +1077,21 @@
 
     for j in range(1, CN):
         sent("x", CN, j, x_src, sib)
-        sent("woc", CN, j, wot.at[t_i, :, c_i], sib)
-        sent("att", CN, j, attq.at[j], sib)
+        sent("br", CN, j, brs.at[j], sib)
         sent("h2", CN, j, h2.at[0], sib)
         sent("g2", CN, j, g2s.at[j], sib)
-        sent("gm", CN, j, gms.at[j], sib)
-        sent("g1", CN, j, g1s.at[j], sib)
         sent("pkc", CN, j, pks.at[first], sib)
         sent("rc", CN, j, rows_s.at[2], sib)
         for n in range(2):
             sent("qcs%d" % n, CN, j, qfin.at[n], sib)
     for j in range(1, ZN):
         sent("small", ZN, j, smalls.at[t_i, s_i], sib)
-        sent("woz", ZN, j, wot.at[t_i, s_i, c_i], sib)
         sent("pkz", ZN, j, pks.at[2], sib)
         sent("rz", ZN, j, rows_s.at[1], sib)
         for n in range(2):
             sent("qz%d" % n, ZN, j, qz_s.at[n, 0], sib)
     for n in range(1, 5):
-        for name, buf, half in (("ct", ctg, ctg), ("gb", gbg, gbg), ("bo", bos, bos)):
+        for name, buf, half in (("ct", ctg, ctg), ("gb", gbg, gbg), ("bo", bos, bos), ("g1", g1s, g1s)):
             sent(name, 5, n, buf.at[1] if n < 3 else half.at[1, pl.ds(0, HB)], sib)
         for k, out in ((0, upo), (1, dno)):
             sent("gc%d" % k, 5, n, gfin.at[k] if n < 3 else gfin.at[k, pl.ds(0, HR)], sib)
@@ -1117,7 +1110,6 @@
     sent("k", 1, 0, kall.at[0], sib)
     sent("v", 1, 0, vall.at[0], sib)
     sent("pkt", 1, 0, pks.at[0], sib)
-    sent("wot", 1, 0, wot.at[t_i], sib)
     sent("wdt", 1, 0, wdt.at[t_i], sib)
     sent("wut", 1, 0, wup.at[t_i], sib)
     sent("rt", 1, 0, rows_s.at[0], sib)
@@ -1142,13 +1134,13 @@
             sent("qcs%d" % n, CN, 0, qfin.at[n], sib)
 
 
-SEMS = 320
+SEMS = 127
 
 
 def fused_call(sizes, *operands):
     CN, ZN, TB, D, HW, FS, R = sizes
     TK = CN * TB
-    QR, HR = R // CN, R // 2
+    HR = R // 2
     half_chips = CN // 2
     heads = HW // 64
     lo, hi = low_type, full_type
@@ -1168,20 +1160,20 @@
     scratch = [
         V((CN, TB, D), lo), V((CN, TB, D), lo), V((2, ZN, 8, 256), hi),
         V((3, R, half_chips * HW), lo), V((R, half_chips * HW), lo),
-        V((ZN, R, 2 * HW), lo), V((ZN, R, HW), lo), V((2, ZN, CN, QR, 2 * HW), lo), V((2, ZN, R, FS), lo), V((2, ZN, R, FS), lo),
+        V((ZN, R, 2 * HW), lo), V((ZN, R, HW), lo), V((ZN, R, HW), lo), V((2, ZN, R, FS), lo), V((2, ZN, R, FS), lo),
         V((D, TK), lo), V((D, TK), lo), V((D, TK), lo),
         V((CN, TB, D), hi), V((CN, TB, D), lo),
         V((TK, HW), hi), V((TK, HW), hi), V((TK, HW), hi), V((TK, HW), hi),
         V((CN, TB, HW), lo), V((2, TK, HW), lo), V((2, TK, HW), lo),
         V((CN, heads * TB, 2 * TK), hi), V((heads * TB, 2 * TK), hi),
-        V((CN, TB, HW), lo), V((CN, TB, HW), lo), V((2 + ZN + CN, 8, 128), hi),
+        V((CN, TB, HW), lo), V((CN, TB, D), lo), V((CN, TB, D), lo), V((2 + ZN + CN, 8, 128), hi),
         V((heads, 2 * TK), hi), V((heads * TB, 2 * TK), lo),
         V((CN, TB, D), lo), V((2, CN, TB, FS), hi), V((CN, TB, 2 * FS), lo), V((CN, TB, 2 * FS), lo),
         V((CN, TB, D), lo), V((CN, TB, D), lo), V((TB, D), hi),
         V((CN, TB, D), lo), V((CN, TB, D), lo), V((TB, D), hi),
         V((2, D, FS), lo), V((2, D, FS), lo), V((2, D, 2 * FS), hi), V((2, D, FS), hi),
         V((2, ZN, R, FS), lo), V((2, ZN, R, FS), lo), V((2, R, FS), lo),
-        V((TB, D), hi), V((CN, TB, D), lo), V((CN, TB, HW), lo), V((CN, TB, HW), lo),
+        V((TB, D), hi), V((CN, TB, D), lo),
         V((CN, TB, HW), hi), V((HW, 2 * TK), hi), V((HW, 2 * TK), hi),
         V((2, HW, TK), lo), V((2, HW, TK), lo), V((TK, HW), lo), V((TK, 2 * HW), lo),
         V((CN, TB, D), lo), V((CN, TB, D), lo), V((TB, D), hi),
@@ -1218,7 +1210,7 @@
             (lnr_h, lnr), (qkr_h, qkr), (bo, bov), (ig, igv),
         ))
     ]
-    for n in (8, 9, 0, 1, 2, 3, 4, 5, 6, 7):
+    for n in (1, 2, 0, 8, 9, 3, 4, 5, 6, 7):
         ins[n].start()
     outs = []
 
@@ -1227,6 +1219,11 @@
         copy.start()
         outs.append(copy)
 
+    for n, grads, stage, out in ((1, upo, gu, gu_o), (2, dno, gd, gd_o)):
+        ins[n].wait()
+        for c in range(CN):
+            stage[:, c * FS:(c + 1) * FS] = grads[c].astype(full_type)
+        leave(stage, out)
     for n, stage, out in ((8, bov, bo_o), (9, igv, ig_o)):
         ins[n].wait()
         leave(stage, out)
@@ -1235,11 +1232,6 @@
         for a in range(2):
             parts = [qkvo[p, a, n][:, first:first + HW] for p in range(half_chips)]
             stage[a * (R // 2):(a + 1) * (R // 2)] = jnp.concatenate(parts, axis=1).astype(full_type)
-        leave(stage, out)
-    for n, grads, stage, out in ((1, upo, gu, gu_o), (2, dno, gd, gd_o)):
-        ins[n].wait()
-        for c in range(CN):
-            stage[:, c * FS:(c + 1) * FS] = grads[c].astype(full_type)
         leave(stage, out)
     heads = HW // 64
     for n in (3, 4, 5):

time: 115 us -> 108 us (0.939)
  Pallas kernels: 113 us -> 106 us
    pallas_call x1, Pallas kernels: 109 us -> 102 us  [fused_call(): pl.pallas_call(functools.partial(fused_kernel, sizes), out_shape=out_shap...]
where the time goes in v4:
time: 108 us; the launch traced here: 107 us
  Pallas kernels  106 us (98%)
    pallas_call x1, Pallas kernels, fused_call(): pl.pallas_call(functools.partial(fused_kernel, sizes), out_shape=out_shap...  102 us
    pallas_call x1, Pallas kernels, fused_layer(): pl.pallas_call(functools.partial(finish_kernel, sizes), out_shape=[tokens...  4.08 us

profile of v4, /device:TPU:0, one launch (start us, length us, event | category | flops | bytes accessed | tf_op | source)
XLA Modules:
  0.0 107.2 jit_solution(14583924754440418643)
XLA Ops:
  0.7 102.3 %shard_map.261 = (bf16[256,768]{1,0:T(8,128)(2,1)}, bf16[256,768]{1,0:T(8,128)(2,1)}, bf16[4,192,384]{2,1,0:T(8,128)(2,1)}, bf16[4,192,384]{2,1,0:T(8,128)(2,1)}...) custom-call(bf16[1,256,768]{2,1,0:T(8,128)(2,1)} %img_h.1, ...), custom_call_target="tpu_custom_call" | custom-call | tf_op jit(solution)/shard_map/pallas_call | solution.py:1185
  103.0 4.1 %shard_map.262 = (bf16[256,768]{1,0:T(8,128)(2,1)}, bf16[256,768]{1,0:T(8,128)(2,1)}, f32[192]{0:T(256)}, f32[192]{0:T(256)}, f32[192]{0:T(256)}, /*index=5*/f32...) custom-call(bf16[256,768]{1,0:T(8,128)(2,1)} %get-tuple-element.40.b, ...), custom_call_target="tpu_custom_call" | custom-call | tf_op jit(solution)/shard_map/pallas_call | solution.py:1297

commit v5 on v4

--- a/solution.py
+++ b/solution.py
@@ -350,16 +350,16 @@
 
 def fused_kernel(
     sizes,
-    img_h, cot_h, g1_h, b1_h, g2_h, b2_h, qg_h, kg_h, wq_h, wk_h, wv_h, wo_h, wup_h, wdn_h,
+    img_h, cot_h, g1_a, b1_a, g2_a, b2_a, qg_a, kg_a, wq_h, wk_h, wv_h, wo_h, wup_h, wdn_h,
     bo_o, ig_o, upo, dno, qkvo, lnr_o, qkr_o, peak_o,
-    xg, ctg, smalls, wl, wol, wkv, wqb, wob, wup, wdt, h1_t, h2_t, ct_t,
+    xg, ctg, smalls, wl, wol, wkv, wqp, wop, wqb, wob, wup, wdt, h1_t, h2_t, ct_t,
     xh1, h1, nq, nk, sq, sk, qs, kall, vall, pst, sbuf, attq, brs, brr, pks,
     ptop, dsb,
     h2, ga, act, gu, g2s, g2r, g2own, bos, bor, boown,
     gsib_s, gsib_r, gown, gkeep, gz_s, gz_r, gfin,
     gres, gbg, dqb, dkt, dvt, dks_s, dks_r, dqr, dkv,
     g1s, g1r, g1own, qsib_s, qsib_r, qown, qz_s, qz_r, qfin,
-    rows_s, rows_r, obuf,
+    rows_s, rows_r, obuf, g1_h, b1_h, g2_h, b2_h, qg_h, kg_h, lnr_v, qkr_v, peak_v,
     lsem, ssem, rsem,
 ):
     CN, ZN, TB, D, HW, FS, R = sizes
@@ -439,7 +439,13 @@
         pltpu.make_async_copy(wup_h.at[:, pl.ds(c_i * FS, FS)], wup.at[t_i, s_i], lsem.at[6]),
         pltpu.make_async_copy(c_src, ctg.at[0], lsem.at[7]),
     ]
-    for copy in locals_:
+    gains = [
+        pltpu.make_async_copy(src, dst, lsem.at[16 + n])
+        for n, (src, dst) in enumerate((
+            (g1_a, g1_h), (b1_a, b1_h), (g2_a, g2_h), (b2_a, b2_h), (qg_a, qg_h), (kg_a, kg_h),
+        ))
+    ]
+    for copy in gains + locals_:
         copy.start()
 
     barrier = pltpu.get_barrier_semaphore()
@@ -447,6 +453,8 @@
     for dev in greet:
         pl.semaphore_signal(barrier, inc=1, device_id=dev, device_id_type=MESH)
 
+    for copy in gains:
+        copy.wait()
     smalls[t_i, s_i] = jnp.zeros((8, 256), full_type)
     for k, ref in enumerate((g1_h, b1_h, g2_h, b2_h)):
         smalls[t_i, s_i, k:k + 1, :R] = ref[...].astype(full_type).reshape(1, R)
@@ -475,7 +483,12 @@
         cols = lax.broadcasted_iota(jnp.int32, (half_chips * HW, lanes), 1) - offset
         return ((rows == cols + at * HW) & (cols >= 0) & (cols < HW)).astype(full_type).astype(low_type)
 
-    projections = (("wkv", wkv), ("wq", wqb), ("wo", wob))
+    projections = (("wkv", wkv), ("wq", wqp), ("wo", wop))
+
+    def send_projection(name, buf):
+        for j in range(1, ZN):
+            put(name, ZN, j, buf.at[s_i], buf.at[s_i], at_z(j))
+        put(name, ZN, 0, buf.at[s_i], buf.at[s_i], sib)
 
     locals_[4].wait()
 
@@ -486,12 +499,11 @@
         wkv[s_i] = (
             dot(wl[1], picker(place, 2 * HW, 0)) + dot(wl[2], picker(place, 2 * HW, HW))
         ).astype(low_type)
-        wqb[s_i] = dot(wl[0], picker(place, HW, 0)).astype(low_type)
-        wob[s_i] = dot(wol[...], picker(place, HW, 0)).astype(low_type)
-        for name, buf in projections:
-            for j in range(1, ZN):
-                put(name, ZN, j, buf.at[s_i], buf.at[s_i], at_z(j))
-            put(name, ZN, 0, buf.at[s_i], buf.at[s_i], sib)
+        for source, packed in ((wl.at[0], wqp), (wol, wop)):
+            packed[s_i] = (
+                dot(source[:HR], picker(place, 2 * HW, 0)) + dot(source[HR:], picker(place, 2 * HW, HW))
+            ).astype(low_type)
+        send_projection(*projections[0])
 
     @pl.when(t_i != tstar)
     def _():
@@ -517,6 +529,11 @@
         @pl.when(j > 0)
         def _():
             got("x", CN, j, xg.at[j], at_ctx(j))
+
+        for n in (1, 2):
+            @pl.when((j == n) & (t_i == tstar))
+            def _():
+                send_projection(*projections[n])
 
         normed, _unused = norm_rows(xg[j].astype(full_type))
         xh1[j] = normed
@@ -595,6 +612,12 @@
                     send_sem=ssem.at[spot("f" + name, ZN) + j], recv_sem=rsem.at[spot(name, ZN) + j],
                     device_id=sib, device_id_type=MESH,
                 ).start()
+
+    def unpack(packed, buf):
+        for z in range(ZN):
+            block = packed[z]
+            buf[z, :HR] = block[:, :HW]
+            buf[z, HR:] = block[:, HW:]
 
     h1_all = h1[...].reshape(TK, D)
     weight_ready(*projections[0])
@@ -609,6 +632,7 @@
     kall[0] = (normed * kgrow).astype(low_type)
     put("k", 1, 0, kall.at[0], kall.at[1], sib)
     weight_ready(*projections[1])
+    unpack(wqp, wqb)
     mlp_weights = (("wd", wdt), ("wu", wup))
 
     def own_mlp(name, buf):
@@ -681,6 +705,7 @@
         @pl.when(i == 0)
         def _():
             weight_ready(*projections[2])
+            unpack(wop, wob)
 
         branch = dot(attq[j], wob[...].reshape(D, HW), NT)
 
@@ -710,6 +735,8 @@
 
     branch = boown[...]
     for j in (3, 2, 1):
+        if j == 1:
+            pass_mlp(*mlp_weights[1], 2)
         got("br", CN, j, brr.at[j], at_ctx(j))
         branch = branch + brr[j].astype(full_type)
     resid = xg[0].astype(full_type) + branch
@@ -719,7 +746,6 @@
     for j in range(1, CN):
         put("h2", CN, j, h2.at[0], h2.at[j], at_ctx(j))
 
-    pass_mlp(*mlp_weights[1], 2)
     locals_[7].wait()
     have_rest("ct", ctg)
     ct_t[...] = ctg[...].reshape(TK, D).T
@@ -774,37 +800,40 @@
         gsib_s[k] = gown[k, :, other_part].astype(low_type)
         put("gs", 2, k, gsib_s.at[k], gsib_r.at[k], sib)
 
-    def down(j, _):
-        part = (
-            dot(act[j, :, :FS], wdt[0].reshape(D, FS), NT) + dot(act[j, :, FS:], wdt[1].reshape(D, FS), NT)
-        )
-
-        @pl.when(j == 0)
-        def _():
-            boown[...] += part
-
-        @pl.when(j > 0)
-        def _():
-            bos[j] = part.astype(low_type)
-
-        return 0
-
-    lax.fori_loop(0, CN, down, 0)
+    def send_far(k):
+        @pl.when(outer)
+        def _():
+            put("gz%d" % k, 4, 2, gz_s.at[k, far_out], gz_r.at[k, 2], plane(pair))
+            put("gz%d" % k, 4, 3, gz_s.at[k, far_in], gz_r.at[k, 3], plane(pair))
+
+    def send_near(k):
+        put("gz%d" % k, 4, 0, gz_s.at[k, pair], gz_r.at[k, 0], plane(pair))
 
     for k in range(2):
         got("gs", 2, k, gsib_r.at[k], sib)
         total = gown[k, :, own_part] + gsib_r[k].astype(full_type)
         gkeep[k] = total
         gz_s[k] = total.astype(low_type).reshape(ZN, R, FS)
-
-    @pl.when(outer)
-    def _():
-        for k in range(2):
-            put("gz%d" % k, 4, 2, gz_s.at[k, far_out], gz_r.at[k, 2], plane(pair))
-            put("gz%d" % k, 4, 3, gz_s.at[k, far_in], gz_r.at[k, 3], plane(pair))
-
-    for k in range(2):
-        put("gz%d" % k, 4, 0, gz_s.at[k, pair], gz_r.at[k, 0], plane(pair))
+        if k == 0:
+            send_far(0)
+            send_near(0)
+
+    def down(j, _):
+        part = (
+            dot(act[j, :, :FS], wdt[0].reshape(D, FS), NT) + dot(act[j, :, FS:], wdt[1].reshape(D, FS), NT)
+        )
+
+        @pl.when(j == 0)
+        def _():
+            boown[...] += part
+
+        @pl.when(j > 0)
+        def _():
+            bos[j] = part.astype(low_type)
+
+        return 0
+
+    lax.fori_loop(0, CN, down, 0)
 
     def relay_mlp(k):
         @pl.when(jnp.logical_not(outer))
@@ -846,6 +875,8 @@
     gbg[0] = gb
     spread("gb", gbg.at[0], lambda j: gbg.at[j])
     send_halves("bo", bos, bor)
+    send_far(1)
+    send_near(1)
 
     peak = pks[2]
     for j in range(1, ZN):
@@ -862,14 +893,13 @@
     def attend_back(j, _):
         @pl.when(j == 1)
         def _():
+            relay_mlp(0)
             pass_on("gb", gbg)
-            relay_mlp(0)
 
         @pl.when(j == CN - 1)
         def _():
             add_halves("bo", bos, bor)
             have_rest("gb", gbg)
-            relay_mlp(1)
 
         grad_rows = stacked(dot(gbg[j], wob[...].reshape(D, HW)).astype(low_type))
         query_rows = stacked(qs[j])
@@ -895,8 +925,11 @@
     for j in range(1, CN):
         got("pkc", CN, j, pks.at[first + j], at_ctx(j))
         peak = jnp.maximum(peak, pks[first + j])
-    peak_o[...] = peak
-
+    peak_v[...] = peak
+    pltpu.make_async_copy(peak_v, peak_o, lsem.at[22]).start()
+
+    relay_mlp(1)
+    share_mlp(0, upo)
     def unnorm(grad_n, gain_row, normed, inverse):
         gain_grad = jnp.sum(grad_n * normed, axis=0, keepdims=True)
         e = grad_n * gain_row
@@ -937,10 +970,6 @@
     grad_k = (dkt[:, :TK] + dks_r[1].astype(full_type)).T
     grad_raw, k_gain_row = unnorm(grad_k, kgrow, nk[...], sk[...])
     dkv[...] = jnp.concatenate([grad_raw, grad_v], axis=1)
-    share_grad(0, dot(h1_t[...], dkv[...]))
-    reduce_grad(1)
-    reduce_grad(0)
-
     ln1g = jnp.zeros((1, D), full_type)
     ln1b = jnp.zeros((1, D), full_type)
     for j in range(CN - 1, -1, -1):
@@ -952,15 +981,20 @@
             g1own[...] = part
         if j == 3:
             send_halves("g1", g1s, g1r)
+            share_grad(0, dot(h1_t[...], dkv[...]))
+            reduce_grad(1)
         ln1g = ln1g + jnp.sum(part * xh1[j], axis=0, keepdims=True)
         ln1b = ln1b + jnp.sum(part, axis=0, keepdims=True)
+        if j == 1:
+            reduce_grad(0)
     rows_s[0] = jnp.zeros_like(rows_s[0])
+    HD2 = D // 2
     for k, row in enumerate((ln1g, ln1b, ln2g, ln2b)):
-        rows_s[0, k:k + 1, :D] = row
-    rows_s[0, 0:1, D:D + HW] = q_gain_row
-    rows_s[0, 1:2, D:D + HW] = k_gain_row
+        rows_s[0, 2 * k:2 * k + 1, :HD2] = row[:, :HD2]
+        rows_s[0, 2 * k + 1:2 * k + 2, :HD2] = row[:, HD2:]
+    rows_s[0, 0:1, HD2:HD2 + HW] = q_gain_row
+    rows_s[0, 1:2, HD2:HD2 + HW] = k_gain_row
     put("rt", 1, 0, rows_s.at[0], rows_r.at[0], sib)
-    share_mlp(0, upo)
     add_halves("g1", g1s, g1r)
     share_mlp(1, dno)
     got("rt", 1, 0, rows_r.at[0], sib)
@@ -1036,18 +1070,22 @@
     rows_s[2] = rows_sum
     for j in range(1, CN):
         put("rc", CN, j, rows_s.at[2], rows_r.at[ZN + j], at_ctx(j))
-    qkr_o[c_i] = rows_sum[:, D:]
+    qkr_v[c_i] = rows_sum[:, HD2:]
 
     share_fin(0)
 
-    total = rows_sum[:, :D]
+    total = rows_sum[:, :HD2]
     for j in range(1, CN):
         got("rc", CN, j, rows_r.at[ZN + j], at_ctx(j))
         block = rows_r[ZN + j]
-        total = total + block[:, :D]
-        qkr_o[flip(c_i, j, CN)] = block[:, D:]
-    lnr_o[...] = total
-
+        total = total + block[:, :HD2]
+        qkr_v[flip(c_i, j, CN)] = block[:, HD2:]
+    lnr_v[...] = total
+    pltpu.make_async_copy(lnr_v, lnr_o, lsem.at[23]).start()
+    pltpu.make_async_copy(qkr_v, qkr_o, lsem.at[24]).start()
+
+    for n, (src, dst) in enumerate(((peak_v, peak_o), (lnr_v, lnr_o), (qkr_v, qkr_o))):
+        pltpu.make_async_copy(src, dst, lsem.at[22 + n]).wait()
     for k, out in ((0, upo), (1, dno)):
         for j in (1, 2):
             half = out.at[flip(c_i, 3, CN), pl.ds((j - 1) * HR, HR)]
@@ -1146,21 +1184,22 @@
     lo, hi = low_type, full_type
     V = pltpu.VMEM
     any_spec = pl.BlockSpec(memory_space=pl.ANY)
-    vm_spec = pl.BlockSpec(memory_space=pltpu.VMEM)
+    gain_shape = operands[6].shape
     out_shape = [
         jax.ShapeDtypeStruct((2 * TB, D), lo),
         jax.ShapeDtypeStruct((2 * TB, D), lo),
         jax.ShapeDtypeStruct((CN, R, FS), lo),
         jax.ShapeDtypeStruct((CN, R, FS), lo),
         jax.ShapeDtypeStruct((half_chips, 2, 2, HR, 2 * HW), lo),
-        jax.ShapeDtypeStruct((8, D), hi),
+        jax.ShapeDtypeStruct((8, D // 2), hi),
         jax.ShapeDtypeStruct((CN, 8, 256), hi),
         jax.ShapeDtypeStruct((8, 128), hi),
     ]
     scratch = [
         V((CN, TB, D), lo), V((CN, TB, D), lo), V((2, ZN, 8, 256), hi),
         V((3, R, half_chips * HW), lo), V((R, half_chips * HW), lo),
-        V((ZN, R, 2 * HW), lo), V((ZN, R, HW), lo), V((ZN, R, HW), lo), V((2, ZN, R, FS), lo), V((2, ZN, R, FS), lo),
+        V((ZN, R, 2 * HW), lo), V((ZN, HR, 2 * HW), lo), V((ZN, HR, 2 * HW), lo),
+        V((ZN, R, HW), lo), V((ZN, R, HW), lo), V((2, ZN, R, FS), lo), V((2, ZN, R, FS), lo),
         V((D, TK), lo), V((D, TK), lo), V((D, TK), lo),
         V((CN, TB, D), hi), V((CN, TB, D), lo),
         V((TK, HW), hi), V((TK, HW), hi), V((TK, HW), hi), V((TK, HW), hi),
@@ -1179,14 +1218,16 @@
         V((CN, TB, D), lo), V((CN, TB, D), lo), V((TB, D), hi),
         V((2, ZN, HR, 2 * HW), lo), V((2, ZN, HR, 2 * HW), lo), V((2, ZN, HR, 2 * HW), hi),
         V((2, ZN, HR, 2 * HW), lo), V((2, ZN, HR, 2 * HW), lo), V((2, HR, 2 * HW), lo),
-        V((3, 8, D + 256), hi), V((ZN + CN, 8, D + 256), hi), V((2, TB, D), lo),
-        pltpu.SemaphoreType.DMA((16,)), pltpu.SemaphoreType.DMA((SEMS,)), pltpu.SemaphoreType.DMA((SEMS,)),
+        V((3, 8, D // 2 + 256), hi), V((ZN + CN, 8, D // 2 + 256), hi), V((2, TB, D), lo),
+        V((R,), lo), V((R,), lo), V((R,), lo), V((R,), lo), V(gain_shape, lo), V(gain_shape, lo),
+        V((8, D // 2), hi), V((CN, 8, 256), hi), V((8, 128), hi),
+        pltpu.SemaphoreType.DMA((25,)), pltpu.SemaphoreType.DMA((SEMS,)), pltpu.SemaphoreType.DMA((SEMS,)),
     ]
     return pl.pallas_call(
         functools.partial(fused_kernel, sizes),
         out_shape=out_shape,
-        in_specs=[any_spec] * 2 + [vm_spec] * 6 + [any_spec] * 6,
-        out_specs=[any_spec] * 5 + [vm_spec] * 3,
+        in_specs=[any_spec] * 14,
+        out_specs=[any_spec] * 8,
         scratch_shapes=scratch,
         compiler_params=pltpu.CompilerParams(
             collective_id=0, has_side_effects=True, vmem_limit_bytes=56 * 2**20
@@ -1249,11 +1290,13 @@
         leave(stage, out)
     ins[6].wait()
     ins[7].wait()
-    rows = jnp.zeros((8, R), full_type)
-    for z in range(ZN):
-        rows = jnp.where(s_i == z, lnr[:, z * R:(z + 1) * R], rows)
     for k, out in enumerate((l1g, l1b, l2g, l2b)):
-        out[...] = rows[k:k + 1].reshape(R)
+        row = jnp.zeros((1, R), full_type)
+        for z in range(ZN):
+            at = z * R % (D // 2)
+            source = 2 * k + z * R // (D // 2)
+            row = jnp.where(s_i == z, lnr[source:source + 1, at:at + R], row)
+        out[...] = row.reshape(R)
     piece = qg_o.shape[1]
     for p in range(half_chips):
         chip = qkr[t_i * half_chips + p]
@@ -1300,7 +1343,7 @@
         in_specs=[any_spec] * 10,
         out_specs=[any_spec] * 2 + [vm_spec] * 6 + [any_spec] * 8,
         scratch_shapes=[
-            V((CN, R, FS), lo), V((CN, R, FS), lo), V((CN // 2, 2, 2, R // 2, 2 * HW), lo), V((8, D), hi),
+            V((CN, R, FS), lo), V((CN, R, FS), lo), V((CN // 2, 2, 2, R // 2, 2 * HW), lo), V((8, D // 2), hi),
             V((CN, 8, 256), hi), V((8, 128), hi), V(w_query.shape, lo), V(w_query.shape, lo),
             V(images.shape[1:], lo), V(images.shape[1:], lo),
         ]

time: 108 us -> 102 us (0.944)
  Pallas kernels: 106 us -> 101 us
    pallas_call x1, Pallas kernels: 102 us -> 97 us  [fused_call(): pl.pallas_call(functools.partial(fused_kernel, sizes), out_shape=out_shap...]
where the time goes in v5:
time: 102 us
  Pallas kernels  101 us (99%)
    pallas_call x1, Pallas kernels, fused_call(): pl.pallas_call(functools.partial(fused_kernel, sizes), out_shape=out_shap...  97 us
    pallas_call x1, Pallas kernels, fused_layer(): pl.pallas_call(functools.partial(finish_kernel, sizes), out_shape=[tokens...  4.08 us

profile of v5, /device:TPU:0, one launch (start us, length us, event | category | flops | bytes accessed | tf_op | source)
XLA Modules:
  0.0 101.9 jit_solution(10578520877572114873)
XLA Ops:
  0.7 97.0 %shard_map.261 = (bf16[256,768]{1,0:T(8,128)(2,1)}, bf16[256,768]{1,0:T(8,128)(2,1)}, bf16[4,192,384]{2,1,0:T(8,128)(2,1)}, bf16[4,192,384]{2,1,0:T(8,128)(2,1)}...) custom-call(bf16[1,256,768]{2,1,0:T(8,128)(2,1)} %img_h.1, ...), custom_call_target="tpu_custom_call" | custom-call | tf_op jit(solution)/shard_map/pallas_call | solution.py:1226
  97.7 4.1 %shard_map.262 = (bf16[256,768]{1,0:T(8,128)(2,1)}, bf16[256,768]{1,0:T(8,128)(2,1)}, f32[192]{0:T(256)}, f32[192]{0:T(256)}, f32[192]{0:T(256)}, /*index=5*/f32...) custom-call(bf16[256,768]{1,0:T(8,128)(2,1)} %get-tuple-element.40.b, ...), custom_call_target="tpu_custom_call" | custom-call | tf_op jit(solution)/shard_map/pallas_call | solution.py:1340

commit v6 on v5

--- a/solution.py
+++ b/solution.py
@@ -356,7 +356,7 @@
     xh1, h1, nq, nk, sq, sk, qs, kall, vall, pst, sbuf, attq, brs, brr, pks,
     ptop, dsb,
     h2, ga, act, gu, g2s, g2r, g2own, bos, bor, boown,
-    gsib_s, gsib_r, gown, gkeep, gz_s, gz_r, gfin,
+    gsib_s, gsib_r, gkeep, gz_s, gz_r, gfin,
     gres, gbg, dqb, dkt, dvt, dks_s, dks_r, dqr, dkv,
     g1s, g1r, g1own, qsib_s, qsib_r, qown, qz_s, qz_r, qfin,
     rows_s, rows_r, obuf, g1_h, b1_h, g2_h, b2_h, qg_h, kg_h, lnr_v, qkr_v, peak_v,
@@ -388,43 +388,45 @@
     def plane(z):
         return (z, c_i, t_i)
 
-    spots = {}
-    from_one = ("x", "small", "fwkv", "fwq", "fwo", "br", "h2", "g2", "qz0", "qz1", "rz", "pkz", "rc", "pkc",
+    arrivals, leavings = {}, {}
+    from_one = ("x", "small", "br", "h2", "g2", "qz0", "qz1", "qz2", "rz", "pkz", "rc", "pkc",
                 "ct", "gb", "bo", "g1", "gc0", "gc1")
+    apart = ("wd", "wu", "gs", "dk", "qg", "ob")
 
     def spot(name, count):
-        if name not in spots:
-            first = sum(n for _, n in spots.values())
+        if name not in arrivals:
+            first = sum(n for _, n in arrivals.values())
             skip = 1 if name in from_one else 0
-            spots[name] = (first - skip, count - skip)
-        return spots[name][0]
-
-    def put(name, count, j, src, dst, dev):
-        base = spot(name, count)
+            arrivals[name] = (first - skip, count - skip)
+        return arrivals[name][0]
+
+    def arrival(name, count, j):
+        return rsem.at[spot(name, count) + j]
+
+    def leaving(name, count, j):
+        if name not in leavings:
+            leavings[name] = (sum(n for _, n in leavings.values()), count if name in apart else 1)
+        return ssem.at[leavings[name][0] + (j if name in apart else 0)]
+
+    def put_as(name, count, send, recv, src, dst, dev):
         pltpu.make_async_remote_copy(
-            src_ref=src, dst_ref=dst, send_sem=ssem.at[base + j], recv_sem=rsem.at[base + j],
+            src_ref=src, dst_ref=dst, send_sem=leaving(name, count, send), recv_sem=arrival(name, count, recv),
             device_id=dev, device_id_type=MESH,
         ).start()
 
-    def put_as(name, count, send, recv, src, dst, dev):
-        base = spot(name, count)
+    def put(name, count, j, src, dst, dev):
+        put_as(name, count, j, j, src, dst, dev)
+
+    def got(name, count, j, dst, dev):
         pltpu.make_async_remote_copy(
-            src_ref=src, dst_ref=dst, send_sem=ssem.at[base + send], recv_sem=rsem.at[base + recv],
-            device_id=dev, device_id_type=MESH,
-        ).start()
-
-    def got(name, count, j, dst, dev):
-        base = spot(name, count)
-        pltpu.make_async_remote_copy(
-            src_ref=dst, dst_ref=dst, send_sem=ssem.at[base + j], recv_sem=rsem.at[base + j],
+            src_ref=dst, dst_ref=dst, send_sem=ssem.at[0], recv_sem=arrival(name, count, j),
             device_id=dev, device_id_type=MESH,
         ).wait_recv()
 
-    def sent(name, count, j, src, dev):
-        base = spot(name, count)
+    def sent(name, count, j, src):
         pltpu.make_async_remote_copy(
-            src_ref=src, dst_ref=src, send_sem=ssem.at[base + j], recv_sem=rsem.at[base + j],
-            device_id=dev, device_id_type=MESH,
+            src_ref=src, dst_ref=src, send_sem=leaving(name, count, j), recv_sem=rsem.at[0],
+            device_id=sib, device_id_type=MESH,
         ).wait_send()
 
     x_src = img_h.at[0, pl.ds(t_i * TB, TB)]
@@ -499,11 +501,11 @@
         wkv[s_i] = (
             dot(wl[1], picker(place, 2 * HW, 0)) + dot(wl[2], picker(place, 2 * HW, HW))
         ).astype(low_type)
+        send_projection(*projections[0])
         for source, packed in ((wl.at[0], wqp), (wol, wop)):
             packed[s_i] = (
                 dot(source[:HR], picker(place, 2 * HW, 0)) + dot(source[HR:], picker(place, 2 * HW, HW))
             ).astype(low_type)
-        send_projection(*projections[0])
 
     @pl.when(t_i != tstar)
     def _():
@@ -609,7 +611,7 @@
             def _():
                 pltpu.make_async_remote_copy(
                     src_ref=block, dst_ref=block,
-                    send_sem=ssem.at[spot("f" + name, ZN) + j], recv_sem=rsem.at[spot(name, ZN) + j],
+                    send_sem=leaving("f" + name, ZN, j), recv_sem=arrival(name, ZN, j),
                     device_id=sib, device_id_type=MESH,
                 ).start()
 
@@ -795,9 +797,9 @@
         put("pkz", ZN, j, pks.at[2], pks.at[2 + j], at_z(j))
     own_part = pl.ds(pl.multiple_of(t_i * FS, FS), FS)
     other_part = pl.ds(pl.multiple_of(o_i * FS, FS), FS)
-    for k, (left, right) in enumerate(((h2_t, gu), (ct_t, act))):
-        gown[k] = dot(left[...], right[...].reshape(TK, 2 * FS))
-        gsib_s[k] = gown[k, :, other_part].astype(low_type)
+    pairs = ((h2_t, gu), (ct_t, act))
+    for k, (left, right) in enumerate(pairs):
+        gsib_s[k] = dot(left[...], right[:, :, other_part].reshape(TK, FS)).astype(low_type)
         put("gs", 2, k, gsib_s.at[k], gsib_r.at[k], sib)
 
     def send_far(k):
@@ -809,14 +811,15 @@
     def send_near(k):
         put("gz%d" % k, 4, 0, gz_s.at[k, pair], gz_r.at[k, 0], plane(pair))
 
+    own_grads = [dot(left[...], right[:, :, own_part].reshape(TK, FS)) for left, right in pairs]
     for k in range(2):
         got("gs", 2, k, gsib_r.at[k], sib)
-        total = gown[k, :, own_part] + gsib_r[k].astype(full_type)
+        total = own_grads[k] + gsib_r[k].astype(full_type)
         gkeep[k] = total
         gz_s[k] = total.astype(low_type).reshape(ZN, R, FS)
-        if k == 0:
-            send_far(0)
-            send_near(0)
+        send_far(k)
+    send_near(0)
+    send_near(1)
 
     def down(j, _):
         part = (
@@ -842,12 +845,7 @@
                 got("gz%d" % k, 4, n, gz_r.at[k, n], plane(pair))
                 mine_part = gkeep[k, pl.ds(pl.multiple_of(z * R, R), R)]
                 gz_s[k, z] = (mine_part + gz_r[k, n].astype(full_type)).astype(low_type)
-                base = spot("gz%d" % k, 4)
-                pltpu.make_async_remote_copy(
-                    src_ref=gz_s.at[k, z], dst_ref=gz_r.at[k, 1],
-                    send_sem=ssem.at[base + n], recv_sem=rsem.at[base + 1],
-                    device_id=plane(z), device_id_type=MESH,
-                ).start()
+                put_as("gz%d" % k, 4, n, 1, gz_s.at[k, z], gz_r.at[k, 1], plane(z))
 
     def share_mlp(k, out):
         total = gkeep[k, pl.ds(pl.multiple_of(s_i * R, R), R)]
@@ -875,8 +873,6 @@
     gbg[0] = gb
     spread("gb", gbg.at[0], lambda j: gbg.at[j])
     send_halves("bo", bos, bor)
-    send_far(1)
-    send_near(1)
 
     peak = pks[2]
     for j in range(1, ZN):
@@ -949,13 +945,17 @@
 
         put("qg", 2, n, qsib_s.at[n], qsib_r.at[n], sib)
 
+    pieces = {1: (("qz1", 0, HR),), 0: (("qz0", 0, HR // 2), ("qz2", HR // 2, HR // 2))}
+
     def reduce_grad(n):
         got("qg", 2, n, qsib_r.at[n], sib)
         total = qown[n] + qsib_r[n].astype(full_type)
         qown[n] = total
         qz_s[n] = total.astype(low_type)
-        for j in range(1, ZN):
-            put("qz%d" % n, ZN, j, qz_s.at[n, flip(s_i, j, ZN)], qz_r.at[n, j], at_z(j))
+        for name, first, count in pieces[n]:
+            rows = pl.ds(first, count)
+            for j in range(1, ZN):
+                put(name, ZN, j, qz_s.at[n, flip(s_i, j, ZN), rows], qz_r.at[n, j, rows], at_z(j))
 
     grad_raw, q_gain_row = unnorm(dqb[...].reshape(TK, HW), qgrow, nq[...], sq[...])
     dqr[...] = grad_raw
@@ -1011,31 +1011,38 @@
     put("ob", 2, 0, obuf.at[0], bo_o.at[own_rows], sib)
     pltpu.make_async_copy(obuf.at[0], bo_o.at[own_rows], lsem.at[10]).start()
 
-    def share_fin(n):
-        total = qown[n, s_i]
-        for j in range(1, ZN):
-            got("qz%d" % n, ZN, j, qz_r.at[n, j], at_z(j))
-            total = total + qz_r[n, j].astype(full_type)
-        qfin[n] = total.astype(low_type)
-        slot = spot("qcr%d" % n, 2 * half_chips) + place * 2 + t_i
-        for j in range(1, CN):
-            pltpu.make_async_remote_copy(
-                src_ref=qfin.at[n], dst_ref=qkvo.at[place, t_i, n],
-                send_sem=ssem.at[spot("qcs%d" % n, CN) + j], recv_sem=rsem.at[slot],
-                device_id=(s_i, flip(c_i, j, CN), tstar), device_id_type=MESH,
-            ).start()
-
-        @pl.when(t_i == tstar)
-        def _():
-            pltpu.make_async_copy(qfin.at[n], qkvo.at[place, t_i, n], lsem.at[12 + n]).start()
-
-        @pl.when(t_i != tstar)
-        def _():
-            pltpu.make_async_remote_copy(
-                src_ref=qfin.at[n], dst_ref=qkvo.at[place, t_i, n],
-                send_sem=ssem.at[spot("qcs%d" % n, CN)], recv_sem=rsem.at[slot],
-                device_id=sib, device_id_type=MESH,
-            ).start()
+    def to_owner(name, first, count, n):
+        rows = pl.ds(first, count)
+        return qfin.at[n, rows], qkvo.at[place, t_i, n, rows]
+
+    def share_fin(n, which=slice(None)):
+        for name, first, count in pieces[n][which]:
+            rows = slice(first, first + count)
+            total = qown[n, s_i, rows]
+            for j in range(1, ZN):
+                got(name, ZN, j, qz_r.at[n, j, pl.ds(first, count)], at_z(j))
+                total = total + qz_r[n, j, rows].astype(full_type)
+            qfin[n, rows] = total.astype(low_type)
+            src, dst = to_owner(name, first, count, n)
+            slot = spot("r" + name, 2 * half_chips) + place * 2 + t_i
+            for j in range(1, CN):
+                pltpu.make_async_remote_copy(
+                    src_ref=src, dst_ref=dst,
+                    send_sem=leaving("s" + name, CN, j), recv_sem=rsem.at[slot],
+                    device_id=(s_i, flip(c_i, j, CN), tstar), device_id_type=MESH,
+                ).start()
+
+            @pl.when(t_i == tstar)
+            def _():
+                pltpu.make_async_copy(src, dst, lsem.at[12 + (name == "qz2") * 2 + n]).start()
+
+            @pl.when(t_i != tstar)
+            def _():
+                pltpu.make_async_remote_copy(
+                    src_ref=src, dst_ref=dst,
+                    send_sem=leaving("o" + name, 1, 0), recv_sem=rsem.at[slot],
+                    device_id=sib, device_id_type=MESH,
+                ).start()
 
     def pass_grad(k, out):
         for j in (1, 2):
@@ -1063,6 +1070,8 @@
     pltpu.make_async_copy(obuf.at[1], ig_o.at[own_rows], lsem.at[11]).start()
 
     pass_grad(1, dno)
+    share_fin(0, slice(0, 1))
+
     rows_sum = rows_s[1]
     for j in range(1, ZN):
         got("rz", ZN, j, rows_r.at[j], at_z(j))
@@ -1072,8 +1081,7 @@
         put("rc", CN, j, rows_s.at[2], rows_r.at[ZN + j], at_ctx(j))
     qkr_v[c_i] = rows_sum[:, HD2:]
 
-    share_fin(0)
-
+    share_fin(0, slice(1, 2))
     total = rows_sum[:, :HD2]
     for j in range(1, CN):
         got("rc", CN, j, rows_r.at[ZN + j], at_ctx(j))
@@ -1096,83 +1104,69 @@
         got("ob", 2, k, out.at[other_rows], sib)
         pltpu.make_async_copy(obuf.at[k], out.at[own_rows], lsem.at[10 + k]).wait()
 
+    all_pieces = [(name, first, count, n) for n in pieces for name, first, count in pieces[n]]
+
     @pl.when(t_i == tstar)
     def _():
-        for n in range(2):
-            pltpu.make_async_copy(qfin.at[n], qkvo.at[place, t_i, n], lsem.at[12 + n]).wait()
+        for name, first, count, n in all_pieces:
+            src, dst = to_owner(name, first, count, n)
+            pltpu.make_async_copy(src, dst, lsem.at[12 + (name == "qz2") * 2 + n]).wait()
 
     for p in range(half_chips):
         for a in range(2):
             @pl.when((t_i != tstar) | (place != p) | (t_i != a))
             def _():
-                for n in range(2):
+                for name, first, count, n in all_pieces:
+                    rows = pl.ds(first, count)
                     pltpu.make_async_remote_copy(
-                        src_ref=qfin.at[n], dst_ref=qkvo.at[p, a, n],
-                        send_sem=ssem.at[spot("qcs%d" % n, CN)],
-                        recv_sem=rsem.at[spot("qcr%d" % n, 2 * half_chips) + p * 2 + a],
+                        src_ref=qfin.at[n, rows], dst_ref=qkvo.at[p, a, n, rows],
+                        send_sem=ssem.at[0],
+                        recv_sem=rsem.at[spot("r" + name, 2 * half_chips) + p * 2 + a],
                         device_id=sib, device_id_type=MESH,
                     ).wait_recv()
 
-    for j in range(1, CN):
-        sent("x", CN, j, x_src, sib)
-        sent("br", CN, j, brs.at[j], sib)
-        sent("h2", CN, j, h2.at[0], sib)
-        sent("g2", CN, j, g2s.at[j], sib)
-        sent("pkc", CN, j, pks.at[first], sib)
-        sent("rc", CN, j, rows_s.at[2], sib)
-        for n in range(2):
-            sent("qcs%d" % n, CN, j, qfin.at[n], sib)
-    for j in range(1, ZN):
-        sent("small", ZN, j, smalls.at[t_i, s_i], sib)
-        sent("pkz", ZN, j, pks.at[2], sib)
-        sent("rz", ZN, j, rows_s.at[1], sib)
-        for n in range(2):
-            sent("qz%d" % n, ZN, j, qz_s.at[n, 0], sib)
-    for n in range(1, 5):
-        for name, buf, half in (("ct", ctg, ctg), ("gb", gbg, gbg), ("bo", bos, bos), ("g1", g1s, g1s)):
-            sent(name, 5, n, buf.at[1] if n < 3 else half.at[1, pl.ds(0, HB)], sib)
-        for k, out in ((0, upo), (1, dno)):
-            sent("gc%d" % k, 5, n, gfin.at[k] if n < 3 else gfin.at[k, pl.ds(0, HR)], sib)
+    three = pl.ds(1, 3)
+    for name, ref in (
+        ("x", xg), ("br", brs), ("h2", h2), ("g2", g2s), ("pkc", pks), ("rc", rows_r), ("small", smalls.at[t_i]),
+        ("pkz", pks), ("rz", rows_r), ("ct", ctg), ("gb", gbg), ("bo", bos), ("g1", g1s),
+        ("gc0", gz_s.at[0]), ("gc1", gz_s.at[1]), ("gz0", gz_s.at[0]), ("gz1", gz_s.at[1]),
+    ):
+        sent(name, 5, 0, ref.at[three])
+    for name, first, count, n in all_pieces:
+        for way in ("", "s"):
+            sent(way + name, 4, 0, qz_s.at[n, three, pl.ds(first, count)])
     for name, buf in mlp_weights:
-        sent(name, 5, 0, buf.at[t_i, s_i], sib)
+        sent(name, 5, 0, buf.at[t_i, s_i])
 
         @pl.when(jnp.logical_not(outer))
         def _():
             for n in range(1, 5):
-                sent(name, 5, n, buf.at[t_i, s_i], sib)
-
+                sent(name, 5, n, buf.at[t_i, s_i])
+
+    for name, ref in (
+        ("smallt", smalls.at[t_i]), ("k", kall.at[0]), ("v", vall.at[0]), ("pkt", pks.at[0]),
+        ("wdt", wdt.at[t_i]), ("wut", wup.at[t_i]), ("rt", rows_s.at[0]),
+    ):
+        sent(name, 1, 0, ref)
     for k in range(2):
-        for n in (0, 2, 3):
-            sent("gz%d" % k, 4, n, gz_s.at[k, 0], sib)
-    sent("smallt", 1, 0, smalls.at[t_i], sib)
-    sent("k", 1, 0, kall.at[0], sib)
-    sent("v", 1, 0, vall.at[0], sib)
-    sent("pkt", 1, 0, pks.at[0], sib)
-    sent("wdt", 1, 0, wdt.at[t_i], sib)
-    sent("wut", 1, 0, wup.at[t_i], sib)
-    sent("rt", 1, 0, rows_s.at[0], sib)
-    for k in range(2):
-        sent("gs", 2, k, gsib_s.at[k], sib)
-        sent("dk", 2, k, dks_s.at[k], sib)
-        sent("ob", 2, k, obuf.at[k], sib)
-    for n in range(2):
-        sent("qg", 2, n, qsib_s.at[n], sib)
+        sent("gs", 2, k, gsib_s.at[k])
+        sent("dk", 2, k, dks_s.at[k])
+        sent("ob", 2, k, obuf.at[k])
+        sent("qg", 2, k, qsib_s.at[k])
 
     @pl.when(t_i == tstar)
     def _():
         for name, buf in projections:
-            for j in range(ZN):
-                sent(name, ZN, j, buf.at[s_i], sib)
-                if j:
-                    sent("f" + name, ZN, j, buf.at[s_i], sib)
+            sent(name, ZN, 0, buf)
+            sent("f" + name, ZN, 0, buf.at[three])
 
     @pl.when(t_i != tstar)
     def _():
-        for n in range(2):
-            sent("qcs%d" % n, CN, 0, qfin.at[n], sib)
-
-
-SEMS = 127
+        for name, first, count, n in all_pieces:
+            sent("o" + name, 1, 0, qfin.at[n, pl.ds(first, count)])
+
+
+ARRIVALS, LEAVINGS = 117, 57
 
 
 def fused_call(sizes, *operands):
@@ -1210,7 +1204,7 @@
         V((CN, TB, D), lo), V((2, CN, TB, FS), hi), V((CN, TB, 2 * FS), lo), V((CN, TB, 2 * FS), lo),
         V((CN, TB, D), lo), V((CN, TB, D), lo), V((TB, D), hi),
         V((CN, TB, D), lo), V((CN, TB, D), lo), V((TB, D), hi),
-        V((2, D, FS), lo), V((2, D, FS), lo), V((2, D, 2 * FS), hi), V((2, D, FS), hi),
+        V((2, D, FS), lo), V((2, D, FS), lo), V((2, D, FS), hi),
         V((2, ZN, R, FS), lo), V((2, ZN, R, FS), lo), V((2, R, FS), lo),
         V((TB, D), hi), V((CN, TB, D), lo),
         V((CN, TB, HW), hi), V((HW, 2 * TK), hi), V((HW, 2 * TK), hi),
@@ -1221,7 +1215,7 @@
         V((3, 8, D // 2 + 256), hi), V((ZN + CN, 8, D // 2 + 256), hi), V((2, TB, D), lo),
         V((R,), lo), V((R,), lo), V((R,), lo), V((R,), lo), V(gain_shape, lo), V(gain_shape, lo),
         V((8, D // 2), hi), V((CN, 8, 256), hi), V((8, 128), hi),
-        pltpu.SemaphoreType.DMA((25,)), pltpu.SemaphoreType.DMA((SEMS,)), pltpu.SemaphoreType.DMA((SEMS,)),
+        pltpu.SemaphoreType.DMA((25,)), pltpu.SemaphoreType.DMA((LEAVINGS,)), pltpu.SemaphoreType.DMA((ARRIVALS,)),
     ]
     return pl.pallas_call(
         functools.partial(fused_kernel, sizes),
@@ -1238,8 +1232,8 @@
 def finish_kernel(
     sizes,
     bo, ig, up_h, dn_h, qkvo_h, lnr_h, qkr_h, peak_h, wq_h, wk_h,
-    bo_o, ig_o, l1g, l1b, l2g, l2b, qg_o, kg_o, gq_o, gk_o, gv_o, go_o, gu_o, gd_o, cq_o, ck_o,
-    upo, dno, qkvo, lnr, qkr, peak, wq, wk, bov, igv, gq, gk, gv, go, gu, gd, cq, ck, isem, osem,
+    bo_o, ig_o, l1g_o, l1b_o, l2g_o, l2b_o, qg_o, kg_o, gq_o, gk_o, gv_o, go_o, gu_o, gd_o, cq_o, ck_o,
+    upo, dno, qkvo, lnr, qkr, peak, wq, wk, bov, igv, gq, gk, gv, go, gu, gd, cq, ck, l1g, l1b, l2g, l2b, qg, kg, isem, osem,
 ):
     CN, ZN, TB, D, HW, FS, R = sizes
     half_chips = CN // 2
@@ -1265,14 +1259,14 @@
         for c in range(CN):
             stage[:, c * FS:(c + 1) * FS] = grads[c].astype(full_type)
         leave(stage, out)
-    for n, stage, out in ((8, bov, bo_o), (9, igv, ig_o)):
-        ins[n].wait()
-        leave(stage, out)
     ins[0].wait()
     for n, first, stage, out in ((1, 0, gq, gq_o), (0, 0, gk, gk_o), (0, HW, gv, gv_o), (1, HW, go, go_o)):
         for a in range(2):
             parts = [qkvo[p, a, n][:, first:first + HW] for p in range(half_chips)]
             stage[a * (R // 2):(a + 1) * (R // 2)] = jnp.concatenate(parts, axis=1).astype(full_type)
+        leave(stage, out)
+    for n, stage, out in ((8, bov, bo_o), (9, igv, ig_o)):
+        ins[n].wait()
         leave(stage, out)
     heads = HW // 64
     for n in (3, 4, 5):
@@ -1290,24 +1284,22 @@
         leave(stage, out)
     ins[6].wait()
     ins[7].wait()
-    for k, out in enumerate((l1g, l1b, l2g, l2b)):
+    for k, (stage, out) in enumerate(((l1g, l1g_o), (l1b, l1b_o), (l2g, l2g_o), (l2b, l2b_o))):
         row = jnp.zeros((1, R), full_type)
         for z in range(ZN):
             at = z * R % (D // 2)
             source = 2 * k + z * R // (D // 2)
             row = jnp.where(s_i == z, lnr[source:source + 1, at:at + R], row)
-        out[...] = row.reshape(R)
-    piece = qg_o.shape[1]
+        stage[...] = row.reshape(R)
+        leave(stage, out)
+    piece = qg.shape[1]
     for p in range(half_chips):
-        chip = qkr[t_i * half_chips + p]
+        chip = pltpu.roll(qkr[t_i * half_chips + p], (256 - s_i * piece) % 256, 1)
         for h in range(heads):
-            for z in range(ZN):
-                at = h * 64 + z * piece
-
-                @pl.when(s_i == z)
-                def _():
-                    qg_o[p * heads + h:p * heads + h + 1] = chip[0:1, at:at + piece]
-                    kg_o[p * heads + h:p * heads + h + 1] = chip[1:2, at:at + piece]
+            for k, stage in ((0, qg), (1, kg)):
+                stage[p * heads + h:p * heads + h + 1] = chip[k:k + 1, h * 64:h * 64 + piece]
+    leave(qg, qg_o)
+    leave(kg, kg_o)
     for copy in outs:
         copy.wait()
 
@@ -1336,19 +1328,19 @@
     lo, hi = low_type, full_type
     V = pltpu.VMEM
     any_spec = pl.BlockSpec(memory_space=pl.ANY)
-    vm_spec = pl.BlockSpec(memory_space=pltpu.VMEM)
     out = pl.pallas_call(
         functools.partial(finish_kernel, sizes),
         out_shape=[tokens] * 2 + [row] * 4 + [gain] * 2 + [square] * 4 + [wide] * 2 + [clipped] * 2,
         in_specs=[any_spec] * 10,
-        out_specs=[any_spec] * 2 + [vm_spec] * 6 + [any_spec] * 8,
+        out_specs=[any_spec] * 16,
         scratch_shapes=[
             V((CN, R, FS), lo), V((CN, R, FS), lo), V((CN // 2, 2, 2, R // 2, 2 * HW), lo), V((8, D // 2), hi),
             V((CN, 8, 256), hi), V((8, 128), hi), V(w_query.shape, lo), V(w_query.shape, lo),
             V(images.shape[1:], lo), V(images.shape[1:], lo),
         ]
         + [V(w_query.shape, hi)] * 4 + [V(w_up.shape, hi)] * 2 + [V(w_query.shape, lo)] * 2
-        + [pltpu.SemaphoreType.DMA((10,)), pltpu.SemaphoreType.DMA((10,))],
+        + [V((R,), hi)] * 4 + [V(q_gain.shape, hi)] * 2
+        + [pltpu.SemaphoreType.DMA((10,)), pltpu.SemaphoreType.DMA((16,))],
         compiler_params=pltpu.CompilerParams(vmem_limit_bytes=60 * 2**20),
     )(*results, w_query, w_key)
     out = list(out)

time: 102 us -> 101 us (level)
  no operation moved by 1% of the time
where the time goes in v6:
time: 101 us
  Pallas kernels  100 us (99%)
    pallas_call x1, Pallas kernels, fused_call(): pl.pallas_call(functools.partial(fused_kernel, sizes), out_shape=out_shap...  96.6 us
    pallas_call x1, Pallas kernels, fused_layer(): pl.pallas_call(functools.partial(finish_kernel, sizes), out_shape=[tokens...  3.52 us

profile of v6, /device:TPU:0, one launch (start us, length us, event | category | flops | bytes accessed | tf_op | source)
XLA Modules:
  0.0 101.0 jit_solution(11923466807859914526)
XLA Ops:
  0.7 96.6 %shard_map.261 = (bf16[256,768]{1,0:T(8,128)(2,1)}, bf16[256,768]{1,0:T(8,128)(2,1)}, bf16[4,192,384]{2,1,0:T(8,128)(2,1)}, bf16[4,192,384]{2,1,0:T(8,128)(2,1)}...) custom-call(bf16[1,256,768]{2,1,0:T(8,128)(2,1)} %img_h.1, ...), custom_call_target="tpu_custom_call" | custom-call | tf_op jit(solution)/shard_map/pallas_call | solution.py:1220
  97.3 3.5 %shard_map.262 = (bf16[256,768]{1,0:T(8,128)(2,1)}, bf16[256,768]{1,0:T(8,128)(2,1)}, f32[192]{0:T(256)}, f32[192]{0:T(256)}, f32[192]{0:T(256)}, /*index=5*/f32...) custom-call(bf16[256,768]{1,0:T(8,128)(2,1)} %get-tuple-element.40.b, ...), custom_call_target="tpu_custom_call" | custom-call | tf_op jit(solution)/shard_map/pallas_call | solution.py:1331

commit v7 on v6

--- a/solution.py
+++ b/solution.py
@@ -389,7 +389,7 @@
         return (z, c_i, t_i)
 
     arrivals, leavings = {}, {}
-    from_one = ("x", "small", "br", "h2", "g2", "qz0", "qz1", "qz2", "rz", "pkz", "rc", "pkc",
+    from_one = ("x", "small", "br", "h2", "g2", "qz0", "qz2", "rz", "pkz", "rc", "pkc",
                 "ct", "gb", "bo", "g1", "gc0", "gc1")
     apart = ("wd", "wu", "gs", "dk", "qg", "ob")
 
@@ -871,7 +871,12 @@
     gres[...] = grad_resid
     gb = grad_resid.astype(low_type)
     gbg[0] = gb
-    spread("gb", gbg.at[0], lambda j: gbg.at[j])
+    for j in (1, 2):
+        half = pl.ds((j - 1) * HB, HB)
+        put("gb", 7, j, gbg.at[0, half], gbg.at[j, half], at_ctx(j))
+    for j in (1, 2):
+        half = pl.ds((2 - j) * HB, HB)
+        put("gb", 7, 4 + j, gbg.at[0, half], gbg.at[j, half], at_ctx(j))
     send_halves("bo", bos, bor)
 
     peak = pks[2]
@@ -889,13 +894,22 @@
     def attend_back(j, _):
         @pl.when(j == 1)
         def _():
+            for n in (1, 2):
+                half = pl.ds((n - 1) * HB, HB)
+                got("gb", 7, n, gbg.at[n, half], at_ctx(n))
+                put_as("gb", 7, 2 + n, 2 + n, gbg.at[n, half], gbg.at[3, half], at_ctx(3 - n))
             relay_mlp(0)
-            pass_on("gb", gbg)
+            got("gb", 7, 5, gbg.at[1, pl.ds(HB, HB)], at_ctx(1))
+
+        @pl.when(j == 2)
+        def _():
+            got("gb", 7, 6, gbg.at[2, pl.ds(0, HB)], at_ctx(2))
 
         @pl.when(j == CN - 1)
         def _():
             add_halves("bo", bos, bor)
-            have_rest("gb", gbg)
+            for n in (1, 2):
+                got("gb", 7, 2 + n, gbg.at[3, pl.ds((n - 1) * HB, HB)], at_ctx(3 - n))
 
         grad_rows = stacked(dot(gbg[j], wob[...].reshape(D, HW)).astype(low_type))
         query_rows = stacked(qs[j])
@@ -925,7 +939,6 @@
     pltpu.make_async_copy(peak_v, peak_o, lsem.at[22]).start()
 
     relay_mlp(1)
-    share_mlp(0, upo)
     def unnorm(grad_n, gain_row, normed, inverse):
         gain_grad = jnp.sum(grad_n * normed, axis=0, keepdims=True)
         e = grad_n * gain_row
@@ -952,10 +965,26 @@
         total = qown[n] + qsib_r[n].astype(full_type)
         qown[n] = total
         qz_s[n] = total.astype(low_type)
+        if n == 1:
+            @pl.when(outer)
+            def _():
+                put("qz1", 4, 2, qz_s.at[1, far_out], qz_r.at[1, 2], plane(pair))
+                put("qz1", 4, 3, qz_s.at[1, far_in], qz_r.at[1, 3], plane(pair))
+
+            put("qz1", 4, 0, qz_s.at[1, pair], qz_r.at[1, 0], plane(pair))
+            return
         for name, first, count in pieces[n]:
             rows = pl.ds(first, count)
             for j in range(1, ZN):
                 put(name, ZN, j, qz_s.at[n, flip(s_i, j, ZN), rows], qz_r.at[n, j, rows], at_z(j))
+
+    def relay_grad():
+        @pl.when(jnp.logical_not(outer))
+        def _():
+            for n, z in ((2, far_out), (3, far_in)):
+                got("qz1", 4, n, qz_r.at[1, n], plane(pair))
+                qz_s[1, z] = (qown[1, z] + qz_r[1, n].astype(full_type)).astype(low_type)
+                put_as("qz1", 4, n, 1, qz_s.at[1, z], qz_r.at[1, 1], plane(z))
 
     grad_raw, q_gain_row = unnorm(dqb[...].reshape(TK, HW), qgrow, nq[...], sq[...])
     dqr[...] = grad_raw
@@ -964,6 +993,7 @@
         dot(h1_t[...], jnp.concatenate([dqr[...], empty], axis=1))
         + dot(gbg[...].reshape(TK, D), jnp.concatenate([empty, attq[...].reshape(TK, HW)], axis=1), TN)
     ))
+    share_mlp(0, upo)
     got("dk", 2, 0, dks_r.at[0], sib)
     grad_v = (dvt[:, :TK] + dks_r[0].astype(full_type)).T.astype(low_type)
     got("dk", 2, 1, dks_r.at[1], sib)
@@ -996,6 +1026,7 @@
     rows_s[0, 1:2, HD2:HD2 + HW] = k_gain_row
     put("rt", 1, 0, rows_s.at[0], rows_r.at[0], sib)
     add_halves("g1", g1s, g1r)
+    relay_grad()
     share_mlp(1, dno)
     got("rt", 1, 0, rows_r.at[0], sib)
     rows_s[1] = rows_s[0] + rows_r[0]
@@ -1019,8 +1050,8 @@
         for name, first, count in pieces[n][which]:
             rows = slice(first, first + count)
             total = qown[n, s_i, rows]
-            for j in range(1, ZN):
-                got(name, ZN, j, qz_r.at[n, j, pl.ds(first, count)], at_z(j))
+            for j in (0, 1) if n == 1 else range(1, ZN):
+                got(name, 4, j, qz_r.at[n, j, pl.ds(first, count)], at_z(1))
                 total = total + qz_r[n, j, rows].astype(full_type)
             qfin[n, rows] = total.astype(low_type)
             src, dst = to_owner(name, first, count, n)
@@ -1051,8 +1082,8 @@
             half = block.at[pl.ds((j - 1) * HR, HR)]
             put_as("gc%d" % k, 5, 2 + j, 2 + j, half, half, at_ctx(3 - j))
 
-    share_fin(1)
     pass_grad(0, upo)
+    share_fin(0, slice(0, 1))
 
     xhat1, inv1 = norm_rows(xg[0].astype(full_type))
     grad_one = g1own[...]
@@ -1070,7 +1101,7 @@
     pltpu.make_async_copy(obuf.at[1], ig_o.at[own_rows], lsem.at[11]).start()
 
     pass_grad(1, dno)
-    share_fin(0, slice(0, 1))
+    share_fin(0, slice(1, 2))
 
     rows_sum = rows_s[1]
     for j in range(1, ZN):
@@ -1081,7 +1112,7 @@
         put("rc", CN, j, rows_s.at[2], rows_r.at[ZN + j], at_ctx(j))
     qkr_v[c_i] = rows_sum[:, HD2:]
 
-    share_fin(0, slice(1, 2))
+    share_fin(1)
     total = rows_sum[:, :HD2]
     for j in range(1, CN):
         got("rc", CN, j, rows_r.at[ZN + j], at_ctx(j))
@@ -1166,7 +1197,7 @@
             sent("o" + name, 1, 0, qfin.at[n, pl.ds(first, count)])
 
 
-ARRIVALS, LEAVINGS = 117, 57
+ARRIVALS, LEAVINGS = 120, 57
 
 
 def fused_call(sizes, *operands):

time: 101 us -> 101 us (level); the launches traced: 101 us -> 99.9 us
    pallas_call x1, Pallas kernels: 96.6 us -> 95.5 us  [fused_call(): pl.pallas_call(functools.partial(fused_kernel, sizes), out_shape=out_shap...]
where the time goes in v7:
time: 101 us; the launch traced here: 99.9 us
  Pallas kernels  99 us (98%)
    pallas_call x1, Pallas kernels, fused_call(): pl.pallas_call(functools.partial(fused_kernel, sizes), out_shape=out_shap...  95.5 us
    pallas_call x1, Pallas kernels, fused_layer(): pl.pallas_call(functools.partial(finish_kernel, sizes), out_shape=[tokens...  3.52 us

profile of v7, /device:TPU:0, one launch (start us, length us, event | category | flops | bytes accessed | tf_op | source)
XLA Modules:
  0.0 99.9 jit_solution(6526563056924026943)
XLA Ops:
  0.7 95.5 %shard_map.261 = (bf16[256,768]{1,0:T(8,128)(2,1)}, bf16[256,768]{1,0:T(8,128)(2,1)}, bf16[4,192,384]{2,1,0:T(8,128)(2,1)}, bf16[4,192,384]{2,1,0:T(8,128)(2,1)}...) custom-call(bf16[1,256,768]{2,1,0:T(8,128)(2,1)} %img_h.1, ...), custom_call_target="tpu_custom_call" | custom-call | tf_op jit(solution)/shard_map/pallas_call | solution.py:1251
  96.2 3.5 %shard_map.262 = (bf16[256,768]{1,0:T(8,128)(2,1)}, bf16[256,768]{1,0:T(8,128)(2,1)}, f32[192]{0:T(256)}, f32[192]{0:T(256)}, f32[192]{0:T(256)}, /*index=5*/f32...) custom-call(bf16[256,768]{1,0:T(8,128)(2,1)} %get-tuple-element.40.b, ...), custom_call_target="tpu_custom_call" | custom-call | tf_op jit(solution)/shard_map/pallas_call | solution.py:1362

commit v8 on v7

--- a/solution.py
+++ b/solution.py
@@ -556,6 +556,27 @@
             half = pl.ds((j - 1) * HB, HB)
             put_as(name, 5, 2 + j, 2 + j, buf.at[j, half], buf.at[3, half], at_ctx(3 - j))
 
+    def spread_halves(name, buf):
+        for j in (1, 2):
+            half = pl.ds((j - 1) * HB, HB)
+            put(name, 7, j, buf.at[0, half], buf.at[j, half], at_ctx(j))
+        for j in (1, 2):
+            half = pl.ds((2 - j) * HB, HB)
+            put(name, 7, 4 + j, buf.at[0, half], buf.at[j, half], at_ctx(j))
+
+    def pass_halves(name, buf):
+        for j in (1, 2):
+            half = pl.ds((j - 1) * HB, HB)
+            got(name, 7, j, buf.at[j, half], at_ctx(j))
+            put_as(name, 7, 2 + j, 2 + j, buf.at[j, half], buf.at[3, half], at_ctx(3 - j))
+
+    def second_half(name, buf, j):
+        got(name, 7, 4 + j, buf.at[j, pl.ds((2 - j) * HB, HB)], at_ctx(j))
+
+    def diagonal_halves(name, buf):
+        for j in (1, 2):
+            got(name, 7, 2 + j, buf.at[3, pl.ds((j - 1) * HB, HB)], at_ctx(3 - j))
+
     def send_halves(name, src, land):
         for j in (1, 2):
             half = pl.ds((j - 1) * HB, HB)
@@ -745,8 +766,7 @@
     boown[...] = resid
     xhat2, inv2 = norm_rows(resid)
     h2[0] = (xhat2 * g2row + b2row).astype(low_type)
-    for j in range(1, CN):
-        put("h2", CN, j, h2.at[0], h2.at[j], at_ctx(j))
+    spread_halves("h2", h2)
 
     locals_[7].wait()
     have_rest("ct", ctg)
@@ -754,16 +774,24 @@
     have_mlp(*mlp_weights[0])
     put("wdt", 1, 0, wdt.at[t_i], wdt.at[t_i], sib)
     ga[t_i] = dot(ctg[...].reshape(TK, D), wdt[t_i].reshape(D, FS)).reshape(CN, TB, FS)
+    pass_halves("h2", h2)
     have_mlp(*mlp_weights[1])
     put("wut", 1, 0, wup.at[t_i], wup.at[t_i], sib)
     got("wdt", 1, 0, wdt.at[o_i], sib)
     ga[o_i] = dot(ctg[...].reshape(TK, D), wdt[o_i].reshape(D, FS)).reshape(CN, TB, FS)
     got("wut", 1, 0, wup.at[o_i], sib)
 
-    def mlp(j, _):
-        @pl.when(j > 0)
-        def _():
-            got("h2", CN, j, h2.at[j], at_ctx(j))
+    def mlp(i, _):
+        j = ((i + 1) % 3) * (1 - i // 3) + 3 * (i // 3)
+
+        for n in (1, 2):
+            @pl.when(j == n)
+            def _():
+                second_half("h2", h2, n)
+
+        @pl.when(j == 3)
+        def _():
+            diagonal_halves("h2", h2)
 
         block = h2[j]
         h2_t[:, pl.ds(pl.multiple_of(j * TB, TB), TB)] = block.T
@@ -871,12 +899,7 @@
     gres[...] = grad_resid
     gb = grad_resid.astype(low_type)
     gbg[0] = gb
-    for j in (1, 2):
-        half = pl.ds((j - 1) * HB, HB)
-        put("gb", 7, j, gbg.at[0, half], gbg.at[j, half], at_ctx(j))
-    for j in (1, 2):
-        half = pl.ds((2 - j) * HB, HB)
-        put("gb", 7, 4 + j, gbg.at[0, half], gbg.at[j, half], at_ctx(j))
+    spread_halves("gb", gbg)
     send_halves("bo", bos, bor)
 
     peak = pks[2]
@@ -894,22 +917,18 @@
     def attend_back(j, _):
         @pl.when(j == 1)
         def _():
-            for n in (1, 2):
-                half = pl.ds((n - 1) * HB, HB)
-                got("gb", 7, n, gbg.at[n, half], at_ctx(n))
-                put_as("gb", 7, 2 + n, 2 + n, gbg.at[n, half], gbg.at[3, half], at_ctx(3 - n))
+            pass_halves("gb", gbg)
             relay_mlp(0)
-            got("gb", 7, 5, gbg.at[1, pl.ds(HB, HB)], at_ctx(1))
+            second_half("gb", gbg, 1)
 
         @pl.when(j == 2)
         def _():
-            got("gb", 7, 6, gbg.at[2, pl.ds(0, HB)], at_ctx(2))
+            second_half("gb", gbg, 2)
 
         @pl.when(j == CN - 1)
         def _():
             add_halves("bo", bos, bor)
-            for n in (1, 2):
-                got("gb", 7, 2 + n, gbg.at[3, pl.ds((n - 1) * HB, HB)], at_ctx(3 - n))
+            diagonal_halves("gb", gbg)
 
         grad_rows = stacked(dot(gbg[j], wob[...].reshape(D, HW)).astype(low_type))
         query_rows = stacked(qs[j])
@@ -1197,7 +1216,7 @@
             sent("o" + name, 1, 0, qfin.at[n, pl.ds(first, count)])
 
 
-ARRIVALS, LEAVINGS = 120, 57
+ARRIVALS, LEAVINGS = 123, 57
 
 
 def fused_call(sizes, *operands):

time: 101 us -> 99.2 us (0.982)
    pallas_call x1, Pallas kernels: 95.5 us -> 94.5 us  [fused_call(): pl.pallas_call(functools.partial(fused_kernel, sizes), out_shape=out_shap...]
where the time goes in v8:
time: 99.2 us; the launch traced here: 98.9 us
  Pallas kernels  98 us (99%)
    pallas_call x1, Pallas kernels, fused_call(): pl.pallas_call(functools.partial(fused_kernel, sizes), out_shape=out_shap...  94.5 us
    pallas_call x1, Pallas kernels, fused_layer(): pl.pallas_call(functools.partial(finish_kernel, sizes), out_shape=[tokens...  3.52 us

profile of v8, /device:TPU:0, one launch (start us, length us, event | category | flops | bytes accessed | tf_op | source)
XLA Modules:
  0.0 98.9 jit_solution(5399233378539240249)
XLA Ops:
  0.7 94.5 %shard_map.261 = (bf16[256,768]{1,0:T(8,128)(2,1)}, bf16[256,768]{1,0:T(8,128)(2,1)}, bf16[4,192,384]{2,1,0:T(8,128)(2,1)}, bf16[4,192,384]{2,1,0:T(8,128)(2,1)}...) custom-call(bf16[1,256,768]{2,1,0:T(8,128)(2,1)} %img_h.1, ...), custom_call_target="tpu_custom_call" | custom-call | tf_op jit(solution)/shard_map/pallas_call | solution.py:1270
  95.2 3.5 %shard_map.262 = (bf16[256,768]{1,0:T(8,128)(2,1)}, bf16[256,768]{1,0:T(8,128)(2,1)}, f32[192]{0:T(256)}, f32[192]{0:T(256)}, f32[192]{0:T(256)}, /*index=5*/f32...) custom-call(bf16[256,768]{1,0:T(8,128)(2,1)} %get-tuple-element.40.b, ...), custom_call_target="tpu_custom_call" | custom-call | tf_op jit(solution)/shard_map/pallas_call | solution.py:1381

commit v9 on v8

--- a/solution.py
+++ b/solution.py
@@ -577,10 +577,29 @@
         for j in (1, 2):
             got(name, 7, 2 + j, buf.at[3, pl.ds((j - 1) * HB, HB)], at_ctx(3 - j))
 
-    def send_halves(name, src, land):
+    def send_halves(name, src, land, count=5):
         for j in (1, 2):
             half = pl.ds((j - 1) * HB, HB)
-            put_as(name, 5, 2 + j, 2 + j, src.at[3, half], land.at[3, half], at_ctx(j))
+            put_as(name, count, 2 + j, 2 + j, src.at[3, half], land.at[3, half], at_ctx(j))
+
+    def send_plain(name, src, land):
+        for j in (1, 2):
+            half = pl.ds((j - 1) * HB, HB)
+            put_as(name, 7, 4 + j, 4 + j, src.at[j, half], land.at[j, half], at_ctx(j))
+
+    def add_rest(name, src, land):
+        for j in (1, 2):
+            half = pl.ds((j - 1) * HB, HB)
+            got(name, 7, 2 + j, land.at[3, half], at_ctx(j))
+            src[3 - j, half] = (src[3 - j, half].astype(full_type) + land[3, half].astype(full_type)).astype(low_type)
+        for j in (1, 2):
+            half = pl.ds((2 - j) * HB, HB)
+            put_as(name, 7, j, j, src.at[j, half], land.at[j, half], at_ctx(j))
+
+    def have_sums(name, land):
+        for j in (1, 2):
+            got(name, 7, 4 + j, land.at[j, pl.ds((j - 1) * HB, HB)], at_ctx(j))
+            got(name, 7, j, land.at[j, pl.ds((2 - j) * HB, HB)], at_ctx(j))
 
     def add_halves(name, src, land):
         for j in (1, 2):
@@ -1029,12 +1048,13 @@
         else:
             g1own[...] = part
         if j == 3:
-            send_halves("g1", g1s, g1r)
+            send_halves("g1", g1s, g1r, 7)
             share_grad(0, dot(h1_t[...], dkv[...]))
             reduce_grad(1)
         ln1g = ln1g + jnp.sum(part * xh1[j], axis=0, keepdims=True)
         ln1b = ln1b + jnp.sum(part, axis=0, keepdims=True)
         if j == 1:
+            send_plain("g1", g1s, g1r)
             reduce_grad(0)
     rows_s[0] = jnp.zeros_like(rows_s[0])
     HD2 = D // 2
@@ -1044,7 +1064,7 @@
     rows_s[0, 0:1, HD2:HD2 + HW] = q_gain_row
     rows_s[0, 1:2, HD2:HD2 + HW] = k_gain_row
     put("rt", 1, 0, rows_s.at[0], rows_r.at[0], sib)
-    add_halves("g1", g1s, g1r)
+    add_rest("g1", g1s, g1r)
     relay_grad()
     share_mlp(1, dno)
     got("rt", 1, 0, rows_r.at[0], sib)
@@ -1106,8 +1126,8 @@
 
     xhat1, inv1 = norm_rows(xg[0].astype(full_type))
     grad_one = g1own[...]
+    have_sums("g1", g1r)
     for j in (1, 2):
-        got("g1", 5, j, g1r.at[j], at_ctx(j))
         grad_one = grad_one + g1r[j].astype(full_type)
     hat = grad_one * g1row
     grad_in = gres[...] + inv1 * (
@@ -1216,7 +1236,7 @@
             sent("o" + name, 1, 0, qfin.at[n, pl.ds(first, count)])
 
 
-ARRIVALS, LEAVINGS = 123, 57
+ARRIVALS, LEAVINGS = 125, 57
 
 
 def fused_call(sizes, *operands):

time: 99.2 us -> 98.7 us (level)
  no operation moved by 1% of the time
where the time goes in v9:
time: 98.7 us; the launch traced here: 98.2 us
  Pallas kernels  97.4 us (99%)
    pallas_call x1, Pallas kernels, fused_call(): pl.pallas_call(functools.partial(fused_kernel, sizes), out_shape=out_shap...  93.9 us
    pallas_call x1, Pallas kernels, fused_layer(): pl.pallas_call(functools.partial(finish_kernel, sizes), out_shape=[tokens...  3.52 us

profile of v9, /device:TPU:0, one launch (start us, length us, event | category | flops | bytes accessed | tf_op | source)
XLA Modules:
  0.0 98.2 jit_solution(3063157837288794581)
XLA Ops:
  0.7 93.9 %shard_map.261 = (bf16[256,768]{1,0:T(8,128)(2,1)}, bf16[256,768]{1,0:T(8,128)(2,1)}, bf16[4,192,384]{2,1,0:T(8,128)(2,1)}, bf16[4,192,384]{2,1,0:T(8,128)(2,1)}...) custom-call(bf16[1,256,768]{2,1,0:T(8,128)(2,1)} %img_h.1, ...), custom_call_target="tpu_custom_call" | custom-call | tf_op jit(solution)/shard_map/pallas_call | solution.py:1290
  94.5 3.5 %shard_map.262 = (bf16[256,768]{1,0:T(8,128)(2,1)}, bf16[256,768]{1,0:T(8,128)(2,1)}, f32[192]{0:T(256)}, f32[192]{0:T(256)}, f32[192]{0:T(256)}, /*index=5*/f32...) custom-call(bf16[256,768]{1,0:T(8,128)(2,1)} %get-tuple-element.40.b, ...), custom_call_target="tpu_custom_call" | custom-call | tf_op jit(solution)/shard_map/pallas_call | solution.py:1401
